TPU v7x, 512 devices: a whole 4x4x16 slice. The times are simulated.
512 devices in a mesh: gx: 8 (over y, core), gy: 4 (over x), gz: 16 (over z).
Axes of the slice: x: 4, y: 4, z: 16, core: 2. Of those that a mesh axis runs over, the one named last changes fastest.
Arguments:
- right_side: float32 [64, 256, 2048], P('gx', 'gy', 'gz'), may hold values from -4 to 4
- start: float32 [64, 256, 2048], P('gx', 'gy', 'gz'), may hold values from -6 to 6
Outputs:
- solution: float32 [64, 256, 2048], P('gx', 'gy', 'gz')
All inputs are finite; a program needn't handle non-finite values.
Results may differ from a plain program's by a relative error of at most 0.0003.
Values sent between devices are 32-bit elements; how exact they have to be, the bound alone decides.
No kernel may reach another device: no remote copies, remote signals or barrier semaphores. Data moves between devices by JAX's collectives and lax.ppermute only.
A program may use at most 128 MiB of HBM per device.

v0:
```python
import jax
import jax.numpy as jnp
from jax import lax
from jax.sharding import PartitionSpec as P

LEVELS = 4
SWEEPS = 2
CSWEEPS = 8


def extended(value, sides, width):
    edges = {}
    for axis, dim in sides:
        size, length = (lax.axis_size(axis), value.shape[dim])
        up = [(i, (i + 1) % size) for i in range(size - 1)]
        last = lax.slice_in_dim(value, length - width, length, axis=dim)
        initial = lax.slice_in_dim(value, 0, width, axis=dim)
        edges[dim] = (
            lax.ppermute(last, axis, up),
            lax.ppermute(initial, axis, [(b, a) for a, b in up]),
        )
    done = []
    for _, dim in sides:
        low, high = edges[dim]
        around = [(width, width) if d in done else (0, 0) for d in range(value.ndim)]
        value = jnp.concatenate([jnp.pad(low, around), value, jnp.pad(high, around)], axis=dim)
        done.append(dim)
    return value


def sent_to_all(value, axis):
    copies = jnp.broadcast_to(value, (lax.axis_size(axis), *value.shape))
    return lax.all_to_all(copies, axis, split_axis=0, concat_axis=0, tiled=True)


def in_order(blocks, dim):
    blocks = jnp.moveaxis(blocks, 0, dim)
    shape = blocks.shape
    return blocks.reshape(*shape[:dim], shape[dim] * shape[dim + 1], *shape[dim + 2 :])


def gathered_copies(value, axis, dim):
    blocks = sent_to_all(value, axis)
    return in_order(blocks, dim)


def neighbours(padded):
    total = padded[2:, 1:-1, 1:-1] + padded[:-2, 1:-1, 1:-1]
    total = total + padded[1:-1, 2:, 1:-1] + padded[1:-1, :-2, 1:-1]
    return total + padded[1:-1, 1:-1, 2:] + padded[1:-1, 1:-1, :-2]


def anchor(dims):
    return (
        lax.axis_index("gx") * dims[0],
        lax.axis_index("gy") * dims[1],
        lax.axis_index("gz") * dims[2],
    )


def parity(dims, corner):
    first = lax.broadcasted_iota(jnp.int32, dims, 0) + corner[0]
    second = lax.broadcasted_iota(jnp.int32, dims, 1) + corner[1]
    third = lax.broadcasted_iota(jnp.int32, dims, 2) + corner[2]
    return (first + second + third) % 2


def smooth(correction, source, factor, colours):
    for pass_index in range(SWEEPS):
        for colour in (0, 1):
            padded = extended(correction, (("gx", 0), ("gy", 1), ("gz", 2)), 1)
            correction = jnp.where(
                colours == colour, (factor * source + neighbours(padded)) / 6.0, correction
            )
    return correction


def restrict(residual):
    sx, sy, sz = residual.shape
    return residual.reshape(sx // 2, 2, sy // 2, 2, sz // 2, 2).mean(axis=(1, 3, 5))


def prolong(coarse):
    return jnp.repeat(jnp.repeat(jnp.repeat(coarse, 2, axis=0), 2, axis=1), 2, axis=2)


def local(right_side, start):
    stored = []
    correction = start
    source = right_side
    for depth in range(LEVELS - 1):
        factor = 4.0**depth
        if depth > 0:
            correction = jnp.zeros_like(source)
        colours = parity(source.shape, anchor(source.shape))
        correction = smooth(correction, source, factor, colours)
        padded = extended(correction, (("gx", 0), ("gy", 1), ("gz", 2)), 1)
        residual = source - (6.0 * correction - neighbours(padded)) / factor
        stored.append((correction, source, colours))
        source = restrict(residual)
    coarse_factor = 4.0 ** (LEVELS - 1)
    gathered = gathered_copies(source, "gz", 2)
    gathered = gathered_copies(gathered, "gy", 1)
    gathered = gathered_copies(gathered, "gx", 0)
    colours = parity(gathered.shape, (0, 0, 0))
    whole = jnp.zeros_like(gathered)
    for pass_index in range(CSWEEPS):
        for colour in (0, 1):
            beside_all = neighbours(jnp.pad(whole, 1))
            whole = jnp.where(
                colours == colour, (coarse_factor * gathered + beside_all) / 6.0, whole
            )
    corner = anchor(source.shape)
    correction = lax.dynamic_slice(whole, (corner[0], corner[1], corner[2]), source.shape)
    for depth in reversed(range(LEVELS - 1)):
        fine_value, fine_source, colours = stored[depth]
        correction = smooth(fine_value + prolong(correction), fine_source, 4.0**depth, colours)
    return correction


def solution(mesh):
    in_specs = (P("gx", "gy", "gz"), P("gx", "gy", "gz"))
    out_specs = P("gx", "gy", "gz")
    return jax.shard_map(local, mesh=mesh, in_specs=in_specs, out_specs=out_specs, check_vma=False)
```

profile of v0, /device:TPU:96, one launch (start us, length us, event | category | flops | bytes accessed | tf_op | source)
XLA Modules:
  0.0 639.8 jit_solution(11579682704189532795)
XLA Ops:
  5.9 4.5 collective-permute-start.3
  14.9 5.0 collective-permute-start.5
  30.4 4.6 collective-permute-start.9
  54.7 4.6 collective-permute-start.15
  68.7 5.1 collective-permute-start.17
  79.2 4.6 collective-permute-start.21
  91.9 5.1 collective-permute-start.23
  98.5 4.5 collective-permute-start.33
  107.2 4.6 collective-permute-start.27
  126.5 4.9 collective-permute-start.35
  137.8 18.1 %reshape.48 = f32[4,2,32,2,64,2]{5,4,3,2,1,0:T(8,128)} reshape(f32[8,64,128]{2,1,0:T(8,128)S(1)} %copy.471) | data formatting | bytes 524288 | tf_op jit(solution)/shard_map/reshape | solution.py:80
  155.9 7.0 %reduce_sum.34 = f32[4,32,64]{2,1,0:T(8,128)S(1)} reduce(f32[4,2,32,2,64,2]{5,4,3,2,1,0:T(8,128)} %reshape.48, f32[]{:T(128)} %constant.142.clone.1), dimensions={1,3,5}, to_apply=%region_0.1 | reduce | flops 57344 | bytes 294916 | tf_op jit(solution)/shard_map/reduce_sum | solution.py:80
  169.2 4.5 collective-permute-start.39
  175.7 5.1 collective-permute-start.41
  186.8 5.6 collective-permute-start.47
  196.7 4.5 collective-permute-start.45
  206.1 5.1 collective-permute-start.53
  215.6 4.8 collective-permute-start.51
  223.0 4.8 collective-permute-start.63
  231.3 5.1 collective-permute-start.59
  240.8 4.6 collective-permute-start.57
  248.6 5.1 collective-permute-start.65
  266.7 4.8 collective-permute-start.69
  273.4 5.1 collective-permute-start.71
  292.3 5.4 collective-permute-start.77
  305.0 4.6 collective-permute-start.81
  311.6 5.6 collective-permute-start.83
  330.9 5.5 collective-permute-start.89
  338.3 23.8 %all_to_all.15 = f32[16,1,128]{2,1,0:T(1,128)S(1)} all-to-all(f32[16,1,128]{2,1,0:T(1,128)S(1)} %reshape.57), channel_id=1, replica_groups=mesh['gx'=8,'gy'=4,'gz'=16] {'gz'}, dimensions={0} | all-to-all | bytes 16384 | tf_op jit(solution)/shard_map/all_to_all | solution.py:33
  363.5 10.4 %all_to_all.16 = f32[4,1,8,256]{3,2,1,0:T(8,128)S(1)} all-to-all(f32[4,1,8,256]{3,2,1,0:T(8,128)S(1)} %broadcast_in_dim.52), channel_id=1, replica_groups=mesh['gx'=8,'gy'=4,'gz'=16] {'gy'}, dimensions={0} | all-to-all | bytes 65536 | tf_op jit(solution)/shard_map/all_to_all | solution.py:33
  378.3 7.4 %all-to-all-done.2 = f32[8,1,32,256]{3,2,1,0:T(8,128)S(1)} async-done(((f32[8,1,32,256]{3,2,1,0:T(8,128)}), f32[8,1,32,256]{3,2,1,0:T(8,128)S(1)}, u32[]{:S(2)}, u32[]{:S(2)}) %all-to-all-start.2) | async-done | bytes 262176 | tf_op jit(solution)/shard_map/all_to_all | solution.py:33
  460.3 5.1 collective-permute-start.113
  472.9 4.5 collective-permute-start.117
  479.5 5.4 collective-permute-start.119
  492.6 4.5 collective-permute-start.123
  499.2 5.5 collective-permute-start.125
  512.4 4.5 collective-permute-start.129
  519.0 5.5 collective-permute-start.131
  532.1 4.5 collective-permute-start.135
  538.7 5.5 collective-permute-start.137
  548.2 4.6 collective-permute-start.141
  561.5 5.2 collective-permute-start.143
  572.0 4.6 collective-permute-start.147
  583.7 5.3 collective-permute-start.149
  594.2 4.6 collective-permute-start.153
  607.6 5.1 collective-permute-start.155
  618.1 4.6 collective-permute-start.159
  629.8 5.1 collective-permute-start.161
  (519 shorter events, 357.4 us)
Async XLA Ops:
  0.8 19.2 %collective-permute-start.1 = (f32[1,64,128]{2,1,0:T(8,128)S(1)}, f32[1,64,128]{2,1,0:T(8,128)S(1)}, u32[]{:S(2)}, u32[]{:S(2)}) collective-permute-start(f32[1,64,128]{2,1,0:T(8,128)S(1)} %get-tuple-element.67), channel_id=1, source_target_pairs={{0,64},{64,128},{128,192},{192,256},{256,320},{320,384},{384,448},... | collective-permute-start | bytes 98312 | tf_op jit(solution)/shard_map/ppermute | solution.py:19
  2.5 17.5 %collective-permute-start = (f32[1,64,128]{2,1,0:T(8,128)S(1)}, f32[1,64,128]{2,1,0:T(8,128)S(1)}, u32[]{:S(2)}, u32[]{:S(2)}) collective-permute-start(f32[1,64,128]{2,1,0:T(8,128)S(1)} %get-tuple-element.66), channel_id=1, source_target_pairs={{64,0},{128,64},{192,128},{256,192},{320,256},{384,320},{448,384},... | collective-permute-start | bytes 98312 | tf_op jit(solution)/shard_map/ppermute | solution.py:20
  30.4 18.8 %collective-permute-start.9 = (f32[8,1,128]{1,0,2:T(8,128)S(1)}, f32[8,1,128]{1,0,2:T(8,128)S(1)}, u32[]{:S(2)}, u32[]{:S(2)}) collective-permute-start(f32[8,1,128]{1,0,2:T(8,128)S(1)} %get-tuple-element.51), channel_id=1, source_target_pairs={{0,16},{16,32},{32,48},{1,17},{17,33},{33,49},{2,18},{18,34},{34,5... | collective-permute-start | bytes 12296 | tf_op jit(solution)/shard_map/ppermute | solution.py:19
  54.7 19.2 %collective-permute-start.15 = (f32[8,1,128]{1,0,2:T(8,128)S(1)}, f32[8,1,128]{1,0,2:T(8,128)S(1)}, u32[]{:S(2)}, u32[]{:S(2)}) collective-permute-start(f32[8,1,128]{1,0,2:T(8,128)S(1)} %get-tuple-element.45), channel_id=1, source_target_pairs={{0,16},{16,32},{32,48},{1,17},{17,33},{33,49},{2,18},{18,34},{34,5... | collective-permute-start | bytes 12296 | tf_op jit(solution)/shard_map/ppermute | solution.py:19
  79.2 17.9 %collective-permute-start.21 = (f32[8,1,128]{1,0,2:T(8,128)S(1)}, f32[8,1,128]{1,0,2:T(8,128)S(1)}, u32[]{:S(2)}, u32[]{:S(2)}) collective-permute-start(f32[8,1,128]{1,0,2:T(8,128)S(1)} %get-tuple-element.39), channel_id=1, source_target_pairs={{0,16},{16,32},{32,48},{1,17},{17,33},{33,49},{2,18},{18,34},{34,5... | collective-permute-start | bytes 12296 | tf_op jit(solution)/shard_map/ppermute | solution.py:19
  83.7 19.3 %collective-permute-start.18 = (f32[1,64,128]{1,0,2:T(1,128)S(1)}, f32[1,64,128]{1,0,2:T(1,128)S(1)}, u32[]{:S(2)}, u32[]{:S(2)}) collective-permute-start(f32[1,64,128]{1,0,2:T(1,128)S(1)} %get-tuple-element.38), channel_id=1, source_target_pairs={{64,0},{128,64},{192,128},{256,192},{320,256},{384,320},{448,384},... | collective-permute-start | bytes 98312 | tf_op jit(solution)/shard_map/ppermute | solution.py:20
  85.0 18.1 %collective-permute-start.19 = (f32[1,64,128]{1,0,2:T(1,128)S(1)}, f32[1,64,128]{1,0,2:T(1,128)S(1)}, u32[]{:S(2)}, u32[]{:S(2)}) collective-permute-start(f32[1,64,128]{1,0,2:T(1,128)S(1)} %get-tuple-element.37), channel_id=1, source_target_pairs={{0,64},{64,128},{128,192},{192,256},{256,320},{320,384},{384,448},... | collective-permute-start | bytes 98312 | tf_op jit(solution)/shard_map/ppermute | solution.py:19
  98.5 17.6 %collective-permute-start.33 = (f32[4,1,64]{2,1,0:T(1,128)S(1)}, f32[4,1,64]{2,1,0:T(1,128)S(1)}, u32[]{:S(2)}, u32[]{:S(2)}) collective-permute-start(f32[4,1,64]{2,1,0:T(1,128)S(1)} %broadcast.419), channel_id=1, source_target_pairs={{0,16},{16,32},{32,48},{1,17},{17,33},{33,49},{2,18},{18,34},{34,5... | collective-permute-start | bytes 3080 | tf_op jit(solution)/shard_map/ppermute | solution.py:19
  111.7 21.0 %collective-permute-start.24 = (f32[1,64,128]{1,0,2:T(1,128)S(1)}, f32[1,64,128]{1,0,2:T(1,128)S(1)}, u32[]{:S(2)}, u32[]{:S(2)}) collective-permute-start(f32[1,64,128]{1,0,2:T(1,128)S(1)} %get-tuple-element.32), channel_id=1, source_target_pairs={{64,0},{128,64},{192,128},{256,192},{320,256},{384,320},{448,384},... | collective-permute-start | bytes 98312 | tf_op jit(solution)/shard_map/ppermute | solution.py:20
  113.1 23.2 %collective-permute-start.25 = (f32[1,64,128]{1,0,2:T(1,128)S(1)}, f32[1,64,128]{1,0,2:T(1,128)S(1)}, u32[]{:S(2)}, u32[]{:S(2)}) collective-permute-start(f32[1,64,128]{1,0,2:T(1,128)S(1)} %get-tuple-element.31), channel_id=1, source_target_pairs={{0,64},{64,128},{128,192},{192,256},{256,320},{320,384},{384,448},... | collective-permute-start | bytes 98312 | tf_op jit(solution)/shard_map/ppermute | solution.py:19
  124.2 38.7 %collective-permute-start.34 = (f32[4,32,1]{2,1,0:T(8,128)S(1)}, f32[4,32,1]{2,1,0:T(8,128)S(1)}, u32[]{:S(2)}, u32[]{:S(2)}) collective-permute-start(f32[4,32,1]{2,1,0:T(8,128)S(1)} %broadcast.420), channel_id=1, source_target_pairs={{1,0},{2,1},{3,2},{4,3},{5,4},{6,5},{7,6},{8,7},{9,8},{10,9},{11,1... | collective-permute-start | bytes 1544 | tf_op jit(solution)/shard_map/ppermute | solution.py:20
  126.5 36.4 %collective-permute-start.35 = (f32[4,32,1]{2,1,0:T(8,128)S(1)}, f32[4,32,1]{2,1,0:T(8,128)S(1)}, u32[]{:S(2)}, u32[]{:S(2)}) collective-permute-start(f32[4,32,1]{2,1,0:T(8,128)S(1)} %broadcast.420), channel_id=1, source_target_pairs={{0,1},{1,2},{2,3},{3,4},{4,5},{5,6},{6,7},{7,8},{8,9},{9,10},{10,1... | collective-permute-start | bytes 1544 | tf_op jit(solution)/shard_map/ppermute | solution.py:19
  131.4 31.5 %collective-permute-start.30 = (f32[1,32,64]{2,1,0:T(8,128)S(1)}, f32[1,32,64]{2,1,0:T(8,128)S(1)}, u32[]{:S(2)}, u32[]{:S(2)}) collective-permute-start(f32[1,32,64]{2,1,0:T(8,128)S(1)} %broadcast.418), channel_id=1, source_target_pairs={{64,0},{128,64},{192,128},{256,192},{320,256},{384,320},{448,384},... | collective-permute-start | bytes 24584 | tf_op jit(solution)/shard_map/ppermute | solution.py:20
  132.7 30.2 %collective-permute-start.31 = (f32[1,32,64]{2,1,0:T(8,128)S(1)}, f32[1,32,64]{2,1,0:T(8,128)S(1)}, u32[]{:S(2)}, u32[]{:S(2)}) collective-permute-start(f32[1,32,64]{2,1,0:T(8,128)S(1)} %broadcast.418), channel_id=1, source_target_pairs={{0,64},{64,128},{128,192},{192,256},{256,320},{320,384},{384,448},... | collective-permute-start | bytes 24584 | tf_op jit(solution)/shard_map/ppermute | solution.py:19
  163.1 20.2 %collective-permute-start.36 = (f32[1,32,64]{2,1,0:T(8,128)S(1)}, f32[1,32,64]{2,1,0:T(8,128)S(1)}, u32[]{:S(2)}, u32[]{:S(2)}) collective-permute-start(f32[1,32,64]{2,1,0:T(8,128)S(1)} %get-tuple-element.113), channel_id=1, source_target_pairs={{64,0},{128,64},{192,128},{256,192},{320,256},{384,320},{448,384},... | collective-permute-start | bytes 24584 | tf_op jit(solution)/shard_map/ppermute | solution.py:20
  164.4 18.9 %collective-permute-start.37 = (f32[1,32,64]{2,1,0:T(8,128)S(1)}, f32[1,32,64]{2,1,0:T(8,128)S(1)}, u32[]{:S(2)}, u32[]{:S(2)}) collective-permute-start(f32[1,32,64]{2,1,0:T(8,128)S(1)} %get-tuple-element.112), channel_id=1, source_target_pairs={{0,64},{64,128},{128,192},{192,256},{256,320},{320,384},{384,448},... | collective-permute-start | bytes 24584 | tf_op jit(solution)/shard_map/ppermute | solution.py:19
  184.8 17.7 %collective-permute-start.46 = (f32[4,32,1]{2,1,0:T(8,128)S(1)}, f32[4,32,1]{2,1,0:T(8,128)S(1)}, u32[]{:S(2)}, u32[]{:S(2)}) collective-permute-start(f32[4,32,1]{2,1,0:T(8,128)S(1)} %get-tuple-element.104), channel_id=1, source_target_pairs={{1,0},{2,1},{3,2},{4,3},{5,4},{6,5},{7,6},{8,7},{9,8},{10,9},{11,1... | collective-permute-start | bytes 1544 | tf_op jit(solution)/shard_map/ppermute | solution.py:20
  204.1 18.8 %collective-permute-start.52 = (f32[4,32,1]{2,1,0:T(8,128)S(1)}, f32[4,32,1]{2,1,0:T(8,128)S(1)}, u32[]{:S(2)}, u32[]{:S(2)}) collective-permute-start(f32[4,32,1]{2,1,0:T(8,128)S(1)} %get-tuple-element.98), channel_id=1, source_target_pairs={{1,0},{2,1},{3,2},{4,3},{5,4},{6,5},{7,6},{8,7},{9,8},{10,9},{11,1... | collective-permute-start | bytes 1544 | tf_op jit(solution)/shard_map/ppermute | solution.py:20
  206.1 21.7 %collective-permute-start.53 = (f32[4,32,1]{2,1,0:T(8,128)S(1)}, f32[4,32,1]{2,1,0:T(8,128)S(1)}, u32[]{:S(2)}, u32[]{:S(2)}) collective-permute-start(f32[4,32,1]{2,1,0:T(8,128)S(1)} %get-tuple-element.99), channel_id=1, source_target_pairs={{0,1},{1,2},{2,3},{3,4},{4,5},{5,6},{6,7},{7,8},{8,9},{9,10},{10,1... | collective-permute-start | bytes 1544 | tf_op jit(solution)/shard_map/ppermute | solution.py:19
  229.4 19.2 %collective-permute-start.58 = (f32[4,32,1]{2,1,0:T(8,128)S(1)}, f32[4,32,1]{2,1,0:T(8,128)S(1)}, u32[]{:S(2)}, u32[]{:S(2)}) collective-permute-start(f32[4,32,1]{2,1,0:T(8,128)S(1)} %get-tuple-element.92), channel_id=1, source_target_pairs={{1,0},{2,1},{3,2},{4,3},{5,4},{6,5},{7,6},{8,7},{9,8},{10,9},{11,1... | collective-permute-start | bytes 1544 | tf_op jit(solution)/shard_map/ppermute | solution.py:20
  231.3 22.4 %collective-permute-start.59 = (f32[4,32,1]{2,1,0:T(8,128)S(1)}, f32[4,32,1]{2,1,0:T(8,128)S(1)}, u32[]{:S(2)}, u32[]{:S(2)}) collective-permute-start(f32[4,32,1]{2,1,0:T(8,128)S(1)} %get-tuple-element.93), channel_id=1, source_target_pairs={{0,1},{1,2},{2,3},{3,4},{4,5},{5,6},{6,7},{7,8},{8,9},{9,10},{10,1... | collective-permute-start | bytes 1544 | tf_op jit(solution)/shard_map/ppermute | solution.py:19
  236.5 18.6 %collective-permute-start.54 = (f32[1,32,64]{2,1,0:T(8,128)S(1)}, f32[1,32,64]{2,1,0:T(8,128)S(1)}, u32[]{:S(2)}, u32[]{:S(2)}) collective-permute-start(f32[1,32,64]{2,1,0:T(8,128)S(1)} %get-tuple-element.95), channel_id=1, source_target_pairs={{64,0},{128,64},{192,128},{256,192},{320,256},{384,320},{448,384},... | collective-permute-start | bytes 24584 | tf_op jit(solution)/shard_map/ppermute | solution.py:20
  237.8 20.4 %collective-permute-start.55 = (f32[1,32,64]{2,1,0:T(8,128)S(1)}, f32[1,32,64]{2,1,0:T(8,128)S(1)}, u32[]{:S(2)}, u32[]{:S(2)}) collective-permute-start(f32[1,32,64]{2,1,0:T(8,128)S(1)} %get-tuple-element.94), channel_id=1, source_target_pairs={{0,64},{64,128},{128,192},{192,256},{256,320},{320,384},{384,448},... | collective-permute-start | bytes 24584 | tf_op jit(solution)/shard_map/ppermute | solution.py:19
  260.8 19.2 %collective-permute-start.66 = (f32[1,16,32]{2,1,0:T(8,128)S(1)}, f32[1,16,32]{2,1,0:T(8,128)S(1)}, u32[]{:S(2)}, u32[]{:S(2)}) collective-permute-start(f32[1,16,32]{2,1,0:T(8,128)S(1)} %get-tuple-element.161), channel_id=1, source_target_pairs={{64,0},{128,64},{192,128},{256,192},{320,256},{384,320},{448,384},... | collective-permute-start | bytes 6152 | tf_op jit(solution)/shard_map/ppermute | solution.py:20
  262.1 17.9 %collective-permute-start.67 = (f32[1,16,32]{2,1,0:T(8,128)S(1)}, f32[1,16,32]{2,1,0:T(8,128)S(1)}, u32[]{:S(2)}, u32[]{:S(2)}) collective-permute-start(f32[1,16,32]{2,1,0:T(8,128)S(1)} %get-tuple-element.160), channel_id=1, source_target_pairs={{0,64},{64,128},{128,192},{192,256},{256,320},{320,384},{384,448},... | collective-permute-start | bytes 6152 | tf_op jit(solution)/shard_map/ppermute | solution.py:19
  280.1 19.0 %collective-permute-start.72 = (f32[1,16,32]{2,1,0:T(8,128)S(1)}, f32[1,16,32]{2,1,0:T(8,128)S(1)}, u32[]{:S(2)}, u32[]{:S(2)}) collective-permute-start(f32[1,16,32]{2,1,0:T(8,128)S(1)} %get-tuple-element.155), channel_id=1, source_target_pairs={{64,0},{128,64},{192,128},{256,192},{320,256},{384,320},{448,384},... | collective-permute-start | bytes 6152 | tf_op jit(solution)/shard_map/ppermute | solution.py:20
  281.4 17.7 %collective-permute-start.73 = (f32[1,16,32]{2,1,0:T(8,128)S(1)}, f32[1,16,32]{2,1,0:T(8,128)S(1)}, u32[]{:S(2)}, u32[]{:S(2)}) collective-permute-start(f32[1,16,32]{2,1,0:T(8,128)S(1)} %get-tuple-element.154), channel_id=1, source_target_pairs={{0,64},{64,128},{128,192},{192,256},{256,320},{320,384},{384,448},... | collective-permute-start | bytes 6152 | tf_op jit(solution)/shard_map/ppermute | solution.py:19
  299.3 19.3 %collective-permute-start.78 = (f32[1,16,32]{2,1,0:T(8,128)S(1)}, f32[1,16,32]{2,1,0:T(8,128)S(1)}, u32[]{:S(2)}, u32[]{:S(2)}) collective-permute-start(f32[1,16,32]{2,1,0:T(8,128)S(1)} %get-tuple-element.149), channel_id=1, source_target_pairs={{64,0},{128,64},{192,128},{256,192},{320,256},{384,320},{448,384},... | collective-permute-start | bytes 6152 | tf_op jit(solution)/shard_map/ppermute | solution.py:20
  300.6 18.0 %collective-permute-start.79 = (f32[1,16,32]{2,1,0:T(8,128)S(1)}, f32[1,16,32]{2,1,0:T(8,128)S(1)}, u32[]{:S(2)}, u32[]{:S(2)}) collective-permute-start(f32[1,16,32]{2,1,0:T(8,128)S(1)} %get-tuple-element.148), channel_id=1, source_target_pairs={{0,64},{64,128},{128,192},{192,256},{256,320},{320,384},{384,448},... | collective-permute-start | bytes 6152 | tf_op jit(solution)/shard_map/ppermute | solution.py:19
  318.7 19.1 %collective-permute-start.84 = (f32[1,16,32]{2,1,0:T(8,128)S(1)}, f32[1,16,32]{2,1,0:T(8,128)S(1)}, u32[]{:S(2)}, u32[]{:S(2)}) collective-permute-start(f32[1,16,32]{2,1,0:T(8,128)S(1)} %get-tuple-element.143), channel_id=1, source_target_pairs={{64,0},{128,64},{192,128},{256,192},{320,256},{384,320},{448,384},... | collective-permute-start | bytes 6152 | tf_op jit(solution)/shard_map/ppermute | solution.py:20
  320.0 17.8 %collective-permute-start.85 = (f32[1,16,32]{2,1,0:T(8,128)S(1)}, f32[1,16,32]{2,1,0:T(8,128)S(1)}, u32[]{:S(2)}, u32[]{:S(2)}) collective-permute-start(f32[1,16,32]{2,1,0:T(8,128)S(1)} %get-tuple-element.142), channel_id=1, source_target_pairs={{0,64},{64,128},{128,192},{192,256},{256,320},{320,384},{384,448},... | collective-permute-start | bytes 6152 | tf_op jit(solution)/shard_map/ppermute | solution.py:19
  389.9 19.2 %collective-permute-start.90 = (f32[1,16,32]{2,1,0:T(8,128)S(1)}, f32[1,16,32]{2,1,0:T(8,128)S(1)}, u32[]{:S(2)}, u32[]{:S(2)}) collective-permute-start(f32[1,16,32]{2,1,0:T(8,128)S(1)} %get-tuple-element.137), channel_id=1, source_target_pairs={{64,0},{128,64},{192,128},{256,192},{320,256},{384,320},{448,384},... | collective-permute-start | bytes 6152 | tf_op jit(solution)/shard_map/ppermute | solution.py:20
  391.2 17.9 %collective-permute-start.91 = (f32[1,16,32]{2,1,0:T(8,128)S(1)}, f32[1,16,32]{2,1,0:T(8,128)S(1)}, u32[]{:S(2)}, u32[]{:S(2)}) collective-permute-start(f32[1,16,32]{2,1,0:T(8,128)S(1)} %get-tuple-element.136), channel_id=1, source_target_pairs={{0,64},{64,128},{128,192},{192,256},{256,320},{320,384},{384,448},... | collective-permute-start | bytes 6152 | tf_op jit(solution)/shard_map/ppermute | solution.py:19
  409.2 19.3 %collective-permute-start.96 = (f32[1,16,32]{2,1,0:T(8,128)S(1)}, f32[1,16,32]{2,1,0:T(8,128)S(1)}, u32[]{:S(2)}, u32[]{:S(2)}) collective-permute-start(f32[1,16,32]{2,1,0:T(8,128)S(1)} %get-tuple-element.131), channel_id=1, source_target_pairs={{64,0},{128,64},{192,128},{256,192},{320,256},{384,320},{448,384},... | collective-permute-start | bytes 6152 | tf_op jit(solution)/shard_map/ppermute | solution.py:20
  410.5 18.0 %collective-permute-start.97 = (f32[1,16,32]{2,1,0:T(8,128)S(1)}, f32[1,16,32]{2,1,0:T(8,128)S(1)}, u32[]{:S(2)}, u32[]{:S(2)}) collective-permute-start(f32[1,16,32]{2,1,0:T(8,128)S(1)} %get-tuple-element.130), channel_id=1, source_target_pairs={{0,64},{64,128},{128,192},{192,256},{256,320},{320,384},{384,448},... | collective-permute-start | bytes 6152 | tf_op jit(solution)/shard_map/ppermute | solution.py:19
  428.7 19.3 %collective-permute-start.102 = (f32[1,16,32]{2,1,0:T(8,128)S(1)}, f32[1,16,32]{2,1,0:T(8,128)S(1)}, u32[]{:S(2)}, u32[]{:S(2)}) collective-permute-start(f32[1,16,32]{2,1,0:T(8,128)S(1)} %get-tuple-element.125), channel_id=1, source_target_pairs={{64,0},{128,64},{192,128},{256,192},{320,256},{384,320},{448,384},... | collective-permute-start | bytes 6152 | tf_op jit(solution)/shard_map/ppermute | solution.py:20
  430.0 18.0 %collective-permute-start.103 = (f32[1,16,32]{2,1,0:T(8,128)S(1)}, f32[1,16,32]{2,1,0:T(8,128)S(1)}, u32[]{:S(2)}, u32[]{:S(2)}) collective-permute-start(f32[1,16,32]{2,1,0:T(8,128)S(1)} %get-tuple-element.124), channel_id=1, source_target_pairs={{0,64},{64,128},{128,192},{192,256},{256,320},{320,384},{384,448},... | collective-permute-start | bytes 6152 | tf_op jit(solution)/shard_map/ppermute | solution.py:19
  448.1 18.8 %collective-permute-start.108 = (f32[1,16,32]{2,1,0:T(8,128)S(1)}, f32[1,16,32]{2,1,0:T(8,128)S(1)}, u32[]{:S(2)}, u32[]{:S(2)}) collective-permute-start(f32[1,16,32]{2,1,0:T(8,128)S(1)} %get-tuple-element.119), channel_id=1, source_target_pairs={{64,0},{128,64},{192,128},{256,192},{320,256},{384,320},{448,384},... | collective-permute-start | bytes 6152 | tf_op jit(solution)/shard_map/ppermute | solution.py:20
  467.3 19.5 %collective-permute-start.114 = (f32[1,32,64]{2,1,0:T(8,128)S(1)}, f32[1,32,64]{2,1,0:T(8,128)S(1)}, u32[]{:S(2)}, u32[]{:S(2)}) collective-permute-start(f32[1,32,64]{2,1,0:T(8,128)S(1)} %get-tuple-element.89), channel_id=1, source_target_pairs={{64,0},{128,64},{192,128},{256,192},{320,256},{384,320},{448,384},... | collective-permute-start | bytes 24584 | tf_op jit(solution)/shard_map/ppermute | solution.py:20
  468.6 18.2 %collective-permute-start.115 = (f32[1,32,64]{2,1,0:T(8,128)S(1)}, f32[1,32,64]{2,1,0:T(8,128)S(1)}, u32[]{:S(2)}, u32[]{:S(2)}) collective-permute-start(f32[1,32,64]{2,1,0:T(8,128)S(1)} %get-tuple-element.88), channel_id=1, source_target_pairs={{0,64},{64,128},{128,192},{192,256},{256,320},{320,384},{384,448},... | collective-permute-start | bytes 24584 | tf_op jit(solution)/shard_map/ppermute | solution.py:19
  487.0 19.6 %collective-permute-start.120 = (f32[1,32,64]{2,1,0:T(8,128)S(1)}, f32[1,32,64]{2,1,0:T(8,128)S(1)}, u32[]{:S(2)}, u32[]{:S(2)}) collective-permute-start(f32[1,32,64]{2,1,0:T(8,128)S(1)} %get-tuple-element.83), channel_id=1, source_target_pairs={{64,0},{128,64},{192,128},{256,192},{320,256},{384,320},{448,384},... | collective-permute-start | bytes 24584 | tf_op jit(solution)/shard_map/ppermute | solution.py:20
  488.3 18.3 %collective-permute-start.121 = (f32[1,32,64]{2,1,0:T(8,128)S(1)}, f32[1,32,64]{2,1,0:T(8,128)S(1)}, u32[]{:S(2)}, u32[]{:S(2)}) collective-permute-start(f32[1,32,64]{2,1,0:T(8,128)S(1)} %get-tuple-element.82), channel_id=1, source_target_pairs={{0,64},{64,128},{128,192},{192,256},{256,320},{320,384},{384,448},... | collective-permute-start | bytes 24584 | tf_op jit(solution)/shard_map/ppermute | solution.py:19
  506.7 19.6 %collective-permute-start.126 = (f32[1,32,64]{2,1,0:T(8,128)S(1)}, f32[1,32,64]{2,1,0:T(8,128)S(1)}, u32[]{:S(2)}, u32[]{:S(2)}) collective-permute-start(f32[1,32,64]{2,1,0:T(8,128)S(1)} %get-tuple-element.77), channel_id=1, source_target_pairs={{64,0},{128,64},{192,128},{256,192},{320,256},{384,320},{448,384},... | collective-permute-start | bytes 24584 | tf_op jit(solution)/shard_map/ppermute | solution.py:20
  508.0 18.3 %collective-permute-start.127 = (f32[1,32,64]{2,1,0:T(8,128)S(1)}, f32[1,32,64]{2,1,0:T(8,128)S(1)}, u32[]{:S(2)}, u32[]{:S(2)}) collective-permute-start(f32[1,32,64]{2,1,0:T(8,128)S(1)} %get-tuple-element.76), channel_id=1, source_target_pairs={{0,64},{64,128},{128,192},{192,256},{256,320},{320,384},{384,448},... | collective-permute-start | bytes 24584 | tf_op jit(solution)/shard_map/ppermute | solution.py:19
  526.5 19.6 %collective-permute-start.132 = (f32[1,32,64]{2,1,0:T(8,128)S(1)}, f32[1,32,64]{2,1,0:T(8,128)S(1)}, u32[]{:S(2)}, u32[]{:S(2)}) collective-permute-start(f32[1,32,64]{2,1,0:T(8,128)S(1)} %get-tuple-element.71), channel_id=1, source_target_pairs={{64,0},{128,64},{192,128},{256,192},{320,256},{384,320},{448,384},... | collective-permute-start | bytes 24584 | tf_op jit(solution)/shard_map/ppermute | solution.py:20
  527.8 18.3 %collective-permute-start.133 = (f32[1,32,64]{2,1,0:T(8,128)S(1)}, f32[1,32,64]{2,1,0:T(8,128)S(1)}, u32[]{:S(2)}, u32[]{:S(2)}) collective-permute-start(f32[1,32,64]{2,1,0:T(8,128)S(1)} %get-tuple-element.70), channel_id=1, source_target_pairs={{0,64},{64,128},{128,192},{192,256},{256,320},{320,384},{384,448},... | collective-permute-start | bytes 24584 | tf_op jit(solution)/shard_map/ppermute | solution.py:19
  548.2 18.6 %collective-permute-start.141 = (f32[8,1,128]{1,0,2:T(8,128)S(1)}, f32[8,1,128]{1,0,2:T(8,128)S(1)}, u32[]{:S(2)}, u32[]{:S(2)}) collective-permute-start(f32[8,1,128]{1,0,2:T(8,128)S(1)} %get-tuple-element.27), channel_id=1, source_target_pairs={{0,16},{16,32},{32,48},{1,17},{17,33},{33,49},{2,18},{18,34},{34,5... | collective-permute-start | bytes 12296 | tf_op jit(solution)/shard_map/ppermute | solution.py:19
  594.2 18.6 %collective-permute-start.153 = (f32[8,1,128]{1,0,2:T(8,128)S(1)}, f32[8,1,128]{1,0,2:T(8,128)S(1)}, u32[]{:S(2)}, u32[]{:S(2)}) collective-permute-start(f32[8,1,128]{1,0,2:T(8,128)S(1)} %get-tuple-element.15), channel_id=1, source_target_pairs={{0,16},{16,32},{32,48},{1,17},{17,33},{33,49},{2,18},{18,34},{34,5... | collective-permute-start | bytes 12296 | tf_op jit(solution)/shard_map/ppermute | solution.py:19
  (115 other events, 1206.7 us)
where the time goes:
time: 653 us; the launch traced here: 640 us
  starting transfers between devices  470 us (72%)
  waiting for transfers between devices  57.8 us (9%)
  local copies, waits for them, and re-layouts  37.9 us (6%)
  other arithmetic  36.6 us (6%)
  blocking collectives  34.2 us (5%)
    ppermute x81, starting transfers between devices, extended(): lax.ppermute(last, axis, up)  340 us
    ppermute x81, starting transfers between devices, extended(): lax.ppermute(initial, axis, [(b, a) for a, b in up])  126 us
    all_to_all x2, blocking collectives, sent_to_all(): return lax.all_to_all(copies, axis, split_axis=0, concat_axis=0, tiled=True)  34.2 us
    ppermute x81, waiting for transfers between devices, extended(): lax.ppermute(last, axis, up)  31 us
    select_n x24, other arithmetic, smooth(): jnp.where(colours == colour, (factor * source + neighbours(padded)) / 6.0...  20.8 us
    reshape x2, local copies, waits for them, and re-layouts, restrict(): residual.reshape(sx // 2, 2, sy // 2, 2, sz // 2, 2).mean(axis=(1, 3, 5))  20.2 us
    ppermute x81, waiting for transfers between devices, extended(): lax.ppermute(initial, axis, [(b, a) for a, b in up])  19.5 us
  transfers between devices with their start and end apart: 163, of which 36 were waited for; matrix products, arithmetic and copies ran while one was open for 7% of the time, Pallas kernels for 0%

commit v1 on v0

v1 whole, which is shorter than its diff:
```python
import functools

import jax
import jax.numpy as jnp
from jax import lax
from jax.experimental import pallas as pl
from jax.experimental.pallas import tpu as pltpu
from jax.sharding import PartitionSpec as P

F32 = jnp.float32
SIXTH = 1.0 / 6.0
EY = 24
ROWS0 = 64 + 2 * EY
ROWS1 = ROWS0 // 2
UP0 = EY - 8
VMEM_LIMIT = 40 * 1024 * 1024


def call(kernel, outs, scratch=(), flops=0):
    shapes = [jax.ShapeDtypeStruct(s, F32) for s in outs]
    return pl.pallas_call(
        kernel,
        out_shape=shapes,
        scratch_shapes=[pltpu.VMEM(s, F32) for s in scratch],
        compiler_params=pltpu.CompilerParams(vmem_limit_bytes=VMEM_LIMIT),
    )


def even_mask(shape):
    rows = lax.broadcasted_iota(jnp.int32, shape, 0)
    lanes = lax.broadcasted_iota(jnp.int32, shape, 1)
    return ((rows + lanes) & 1) == 0


def lane_of(shape):
    return lax.broadcasted_iota(jnp.int32, shape, 1)


def domain(shape, row0, rows, lane0, lanes, lane_limit=None):
    y = lax.broadcasted_iota(jnp.int32, shape, 0) + row0
    z = lax.broadcasted_iota(jnp.int32, shape, 1)
    inside = (y >= 0) & (y < rows) & (z + lane0 >= 0) & (z + lane0 < lanes)
    if lane_limit is not None:
        inside = inside & (z < lane_limit)
    return jnp.where(inside, F32(SIXTH), F32(0.0))


def beside(src, i, even, red):
    c = src[i]
    y, z = c.shape
    below, above = src[i - 1], src[i + 1]
    s = c + (jnp.where(even, below, above) if red else jnp.where(even, above, below))
    s = s + (pltpu.roll(c, 1, 0) + pltpu.roll(c, y - 1, 0))
    return s + (pltpu.roll(c, 1, 1) + pltpu.roll(c, z - 1, 1))


def half(dst, src, b, shift, weight, even, red, lo, hi):
    def body(i, carry):
        dst[i + 1] = (b[i + shift] + beside(src, i + 1, even, red)) * weight[...]
        return carry

    lax.fori_loop(lo, hi, body, 0)


def pair_sum(mat_rows, mat_cols, of):
    k = lax.broadcasted_iota(jnp.int32, (mat_rows, mat_cols), 0)
    c = lax.broadcasted_iota(jnp.int32, (mat_rows, mat_cols), 1)
    return of(k, c)


def dot(a, b):
    return jnp.dot(a, b, precision=lax.Precision.HIGHEST, preferred_element_type=F32)


def pack_kernel(start, right, s, up, down):
    even = even_mask((64, 128))
    low = lane_of((64, 128)) < 64
    planes = []
    for p in range(4):
        planes.append(jnp.where(even, start[2 * p + 1], start[2 * p]))
    for p in range(4):
        planes.append(jnp.where(even, right[2 * p], right[2 * p + 1]))
    for p in range(4):
        planes.append(jnp.where(even, right[2 * p + 1], right[2 * p]))
    for p in range(12):
        s[p] = planes[p]
    for p in range(6):
        a, b = planes[p], planes[p + 6]
        up[p] = jnp.where(low, pltpu.roll(a, 64, 1), b)
        down[p] = jnp.where(low, a, pltpu.roll(b, 64, 1))


def widen_kernel(s, left, right, z, first, last):
    low = lane_of((64, 128)) < 64
    for p in range(12):
        own = pltpu.roll(s[p], 64, 1)
        if p < 6:
            a, b = left[p], pltpu.roll(right[p], 64, 1)
        else:
            a, b = pltpu.roll(left[p - 6], 64, 1), right[p - 6]
        v0 = jnp.where(low, a, own)
        v1 = jnp.where(low, own, b)
        z[p, :, :128] = v0
        z[p, :, 128:] = v1
        first[p, :, :128] = v0[:EY]
        first[p, :, 128:] = v1[:EY]
        last[p, :, :128] = v0[64 - EY :]
        last[p, :, 128:] = v1[64 - EY :]


def lengthen_kernel(z, before, after, a):
    a[:, :EY] = before[...]
    a[:, EY : EY + 64] = z[...]
    a[:, EY + 64 :] = after[...]


def fine_down_kernel(n, own, left, right, coarse, black_out, red_b_out, black_b_out, red, black, rb, bb, weight, pairs):
    gx, gy, gz = (lax.axis_index(a) for a in ("gx", "gy", "gz"))
    shape = (ROWS0, 256)
    even = even_mask(shape)
    weight[...] = domain(shape, 64 * gy - EY, 64 * n[1], 128 * gz - 64, 128 * n[2])
    zero = jnp.zeros(shape, F32)
    for i in (0, 13):
        black[i] = zero
        red[i] = zero
    has_left, has_right = gx > 0, gx < n[0] - 1
    for p in range(4):
        black[p + 5] = own[p]
        rb[p + 4] = own[p + 4]
        bb[p + 4] = own[p + 8]
        rb[p] = left[p + 4]
        bb[p] = left[p + 8]
        rb[p + 8] = right[p + 4]
        bb[p + 8] = right[p + 8]
        black[p + 1] = jnp.where(has_left, left[p], zero)
        black[p + 9] = jnp.where(has_right, right[p], zero)
        red[p + 1] = zero
        red[p + 9] = zero
    first = jnp.where(has_left, 0, 4)
    end = jnp.where(has_right, 12, 8)
    for dst, src, b, is_red, lo in ((red, black, rb, True, 0), (black, red, bb, False, 1), (red, black, rb, True, 1), (black, red, bb, False, 2)):
        half(dst, src, b, 0, weight, even, is_red, jnp.maximum(first, lo), jnp.minimum(end, 12 - lo))

    def residual(p, carry):
        i = p + 5
        r = (rb[p + 4] - 6.0 * red[i] + beside(black, i, even, True)) + (bb[p + 4] - 6.0 * black[i] + beside(red, i, even, False))
        pairs[2 * p] = r[:, :128]
        pairs[2 * p + 1] = r[:, 128:]
        return carry

    lax.fori_loop(0, 4, residual, 0)
    rows = []
    for p in range(4):
        parts = [pairs[2 * p + h, pl.ds(0, ROWS1, stride=2), :] + pairs[2 * p + h, pl.ds(1, ROWS1, stride=2), :] for h in (0, 1)]
        rows.append(jnp.concatenate(parts, axis=1))
    take = pair_sum(256, 128, lambda k, c: jnp.where((k >> 1) == c, F32(0.5), F32(0.0)))
    result = dot(jnp.concatenate(rows, axis=0), take)
    for p in range(4):
        coarse[p] = result[p * ROWS1 : (p + 1) * ROWS1]
    for p in range(8):
        black_out[p] = black[p + 3, UP0 : UP0 + 80]
        red_b_out[p] = rb[p + 2, UP0 : UP0 + 80]
        black_b_out[p] = bb[p + 2, UP0 : UP0 + 80]


def middle_down_kernel(n, b1, coarse, black_out, red_b, black_b, red, black, weight, pairs):
    gy, gz = lax.axis_index("gy"), lax.axis_index("gz")
    shape = (ROWS1, 128)
    count = 2 * n[0]
    even = even_mask(shape)
    weight[...] = domain(shape, 32 * gy - EY // 2, 32 * n[1], 64 * gz - 32, 64 * n[2])
    zero = jnp.zeros(shape, F32)
    for i in (0, count + 1):
        red[i] = zero
        black[i] = zero

    def begin(i, carry):
        a, b = b1[2 * i], b1[2 * i + 1]
        r = jnp.where(even, a, b)
        red_b[i] = r
        black_b[i] = jnp.where(even, b, a)
        red[i + 1] = r * weight[...]
        return carry

    lax.fori_loop(0, count, begin, 0)
    half(black, red, black_b, 0, weight, even, False, 0, count)
    half(red, black, red_b, 0, weight, even, True, 0, count)
    half(black, red, black_b, 0, weight, even, False, 0, count)

    def residual(i, carry):
        r = (red_b[i] - 6.0 * red[i + 1] + beside(black, i + 1, even, True)) + (black_b[i] - 6.0 * black[i + 1] + beside(red, i + 1, even, False))
        pairs[i] = r
        black_out[i] = black[i + 1]
        return carry

    lax.fori_loop(0, count, residual, 0)
    top = EY // 2
    sums = [pairs[i, pl.ds(top, 16, stride=2), :] + pairs[i, pl.ds(top + 1, 16, stride=2), :] for i in range(count)]
    left = jnp.concatenate(sums[: n[0]], axis=0)
    right = jnp.concatenate(sums[n[0] :], axis=0)
    take_low = pair_sum(128, 128, lambda k, c: jnp.where((k >> 1) == c, F32(0.5), F32(0.0)))
    take_high = pair_sum(128, 128, lambda k, c: jnp.where((k >> 1) == c - 64, F32(0.5), F32(0.0)))
    result = dot(left, take_low) + dot(right, take_high)
    for i in range(n[0]):
        coarse[i] = result[16 * i : 16 * i + 16]


def widen_coarse_kernel(n, own, left, right, wide):
    lanes = lane_of((16, 128))
    is_left, is_own = lanes < 48, lanes < 80
    for i in range(n[0]):
        w, a, b = own[i], left[i], right[i]
        wide[i] = jnp.where(is_left, a, jnp.where(is_own, pltpu.roll(w, 32, 1), pltpu.roll(b, 64, 1)))
        wide[i + n[0]] = jnp.where(is_left, pltpu.roll(a, 64, 1), jnp.where(is_own, pltpu.roll(w, 96, 1), b))


def up_kernel(
    n, b2, black1, red_b1, black_b1, black0, red_b0, black_b0, out,
    rb2, bb2, red2, black2, weight2, pairs2,
    rb3, bb3, red3, black3, weight3, add2,
    win2, exp2, add1, red1, weight1, add0,
    red0, weight0, bl1, bl0,
):
    gx, gy, gz = (lax.axis_index(a) for a in ("gx", "gy", "gz"))
    rows2, rows3 = 16 * n[1], 8 * n[1]
    shape2 = (rows2 + 8, 128)
    even2 = even_mask(shape2)
    weight2[...] = domain(shape2, 0, rows2, 32 * gz - 48, 32 * n[2])
    zero2 = jnp.zeros(shape2, F32)
    pairs_2 = n[0]
    for i in (0, pairs_2 + 1):
        red2[i] = zero2
        black2[i] = zero2
    even16 = even_mask((16, 128))
    for i in range(pairs_2):
        for g in range(n[1]):
            a, b = b2[g, 2 * i], b2[g, 2 * i + 1]
            rb2[i, 16 * g : 16 * g + 16] = jnp.where(even16, a, b)
            bb2[i, 16 * g : 16 * g + 16] = jnp.where(even16, b, a)
        rb2[i, rows2:] = jnp.zeros((8, 128), F32)
        bb2[i, rows2:] = jnp.zeros((8, 128), F32)

    def begin2(i, carry):
        red2[i + 1] = rb2[i] * weight2[...]
        return carry

    lax.fori_loop(0, pairs_2, begin2, 0)
    half(black2, red2, bb2, 0, weight2, even2, False, 0, pairs_2)
    half(red2, black2, rb2, 0, weight2, even2, True, 0, pairs_2)
    half(black2, red2, bb2, 0, weight2, even2, False, 0, pairs_2)

    def residual2(i, carry):
        pairs2[i] = (rb2[i] - 6.0 * red2[i + 1] + beside(black2, i + 1, even2, True)) + (bb2[i] - 6.0 * black2[i + 1] + beside(red2, i + 1, even2, False))
        return carry

    lax.fori_loop(0, pairs_2, residual2, 0)
    sums = [pairs2[i, pl.ds(0, rows3, stride=2), :] + pairs2[i, pl.ds(1, rows3, stride=2), :] for i in range(pairs_2)]
    take = pair_sum(128, 128, lambda k, c: jnp.where((k >> 1) == c, F32(0.5), F32(0.0)))
    b3 = dot(jnp.concatenate(sums, axis=0), take)

    shape3 = (rows3 + 8, 128)
    even3 = even_mask(shape3)
    even3s = even_mask((rows3, 128))
    weight3[...] = domain(shape3, 0, rows3, 16 * gz - 24, 16 * n[2], 64)
    zero3 = jnp.zeros(shape3, F32)
    pairs_3 = n[0] // 2
    for i in (0, pairs_3 + 1):
        red3[i] = zero3
        black3[i] = zero3
    for i in range(pairs_3):
        a = b3[2 * i * rows3 : (2 * i + 1) * rows3]
        b = b3[(2 * i + 1) * rows3 : (2 * i + 2) * rows3]
        rb3[i, :rows3] = jnp.where(even3s, a, b)
        bb3[i, :rows3] = jnp.where(even3s, b, a)
        rb3[i, rows3:] = jnp.zeros((8, 128), F32)
        bb3[i, rows3:] = jnp.zeros((8, 128), F32)
        red3[i + 1] = rb3[i] * weight3[...]

    def half3(dst, src, b, red):
        for i in range(pairs_3):
            dst[i + 1] = (b[i] + beside(src, i + 1, even3, red)) * weight3[...]

    half3(black3, red3, bb3, False)

    def sweep3(_, carry):
        half3(red3, black3, rb3, True)
        half3(black3, red3, bb3, False)
        return carry

    lax.fori_loop(0, 7, sweep3, 0)
    planes = []
    for i in range(pairs_3):
        r, b = red3[i + 1, :rows3], black3[i + 1, :rows3]
        planes += [jnp.where(even3s, r, b), jnp.where(even3s, b, r)]
    spread3 = pair_sum(128, 128, lambda k, c: jnp.where(k == (c >> 1), F32(1.0), F32(0.0)))
    wide = dot(jnp.concatenate(planes, axis=0), spread3)
    for i in range(pairs_2):
        w = wide[i * rows3 : (i + 1) * rows3]
        add2[i, pl.ds(0, rows3, stride=2), :] = w
        add2[i, pl.ds(1, rows3, stride=2), :] = w
        black2[i + 1, :rows2] = black2[i + 1, :rows2] + add2[i]
    for dst, src, b, is_red in ((red2, black2, rb2, True), (black2, red2, bb2, False)) * 2:
        half(dst, src, b, 0, weight2, even2, is_red, 0, pairs_2)

    even2s = even_mask((rows2, 128))
    for i in range(pairs_2):
        r, b = red2[i + 1, :rows2], black2[i + 1, :rows2]
        for q, v in ((2 * i, jnp.where(even2s, r, b)), (2 * i + 1, jnp.where(even2s, b, r))):
            win2[q, :8] = jnp.zeros((8, 128), F32)
            win2[q, 8 : 8 + rows2] = v
            win2[q, 8 + rows2 :] = jnp.zeros((24, 128), F32)
    count = 2 * n[0]
    top = pl.multiple_of(16 * gy, 8)
    cut = jnp.concatenate([win2[q, pl.ds(top, 40), :] for q in range(count)], axis=0)
    spread2 = pair_sum(128, 128, lambda k, c: jnp.where(k == (c >> 1) + 32, F32(1.0), F32(0.0)))
    wide = dot(cut, spread2)
    shape1 = (ROWS1, 128)
    even1 = even_mask(shape1)
    weight1[...] = domain(shape1, 32 * gy - EY // 2, 32 * n[1], 64 * gz - 32, 64 * n[2])
    zero1 = jnp.zeros(shape1, F32)
    skip = 8 - EY // 4
    for i in (0, count + 1):
        red1[i] = zero1
        bl1[i] = zero1
    for i in range(count):
        w = wide[40 * i + skip : 40 * i + skip + ROWS1 // 2]
        add1[i, pl.ds(0, ROWS1 // 2, stride=2), :] = w
        add1[i, pl.ds(1, ROWS1 // 2, stride=2), :] = w
        bl1[i + 1] = black1[i] + add1[i]
    for dst, src, b, is_red in ((red1, bl1, red_b1, True), (bl1, red1, black_b1, False)) * 2:
        half(dst, src, b, 0, weight1, even1, is_red, 0, count)

    low1 = UP0 // 2
    even40 = even_mask((40, 128))
    planes = []
    for i in range(8):
        q = 2 * gx + i // 2
        r, b = red1[q, low1 : low1 + 40], bl1[q, low1 : low1 + 40]
        planes.append(jnp.where(even40, r, b) if i % 2 == 0 else jnp.where(even40, b, r))
    stacked = jnp.concatenate(planes, axis=0)
    shape0 = (80, 256)
    even0 = even_mask(shape0)
    weight0[...] = domain(shape0, 64 * gy - 8, 64 * n[1], 128 * gz - 64, 128 * n[2])
    zero0 = jnp.zeros(shape0, F32)
    for h in (0, 1):
        spread1 = pair_sum(128, 128, lambda k, c: jnp.where(k == (c >> 1) + 64 * h, F32(1.0), F32(0.0)))
        wide = dot(stacked, spread1)
        for i in range(8):
            w = wide[40 * i : 40 * i + 40]
            add0[2 * i + h, pl.ds(0, 40, stride=2), :] = w
            add0[2 * i + h, pl.ds(1, 40, stride=2), :] = w
    for i in range(10):
        red0[i] = zero0
    bl0[0] = zero0
    bl0[9] = zero0
    for i in range(8):
        bl0[i + 1] = black0[i] + jnp.concatenate([add0[2 * i], add0[2 * i + 1]], axis=1)
    first = jnp.where(gx > 0, 0, 2)
    end = jnp.where(gx < n[0] - 1, 8, 6)
    for dst, src, b, is_red, lo in ((red0, bl0, red_b0, True, 0), (bl0, red0, black_b0, False, 1), (red0, bl0, red_b0, True, 1), (bl0, red0, black_b0, False, 2)):
        half(dst, src, b, 0, weight0, even0, is_red, jnp.maximum(first, lo), jnp.minimum(end, 8 - lo))
    even64 = even_mask((64, 128))
    for p in range(4):
        r = pltpu.roll(red0[p + 3, 8:72], 192, 1)[:, :128]
        b = pltpu.roll(bl0[p + 3, 8:72], 192, 1)[:, :128]
        out[2 * p] = jnp.where(even64, r, b)
        out[2 * p + 1] = jnp.where(even64, b, r)


def from_both(up_value, down_value, axis):
    size = lax.axis_size(axis)
    up = [(i, i + 1) for i in range(size - 1)]
    return lax.ppermute(up_value, axis, up), lax.ppermute(down_value, axis, [(b, a) for a, b in up])


def from_both_round(value, axis):
    size = lax.axis_size(axis)
    up = [(i, (i + 1) % size) for i in range(size)]
    return lax.ppermute(value, axis, up), lax.ppermute(value, axis, [(b, a) for a, b in up])


def gathered(value, axis):
    copies = jnp.broadcast_to(value, (lax.axis_size(axis), *value.shape))
    return lax.all_to_all(copies, axis, split_axis=0, concat_axis=0, tiled=True)


def local(right_side, start):
    n = tuple(lax.axis_size(a) for a in ("gx", "gy", "gz"))
    s, up, down = call(pack_kernel, [(12, 64, 128), (6, 64, 128), (6, 64, 128)])(start, right_side)
    left, right = from_both(up, down, "gz")
    z, first, last = call(widen_kernel, [(12, 64, 256), (12, EY, 256), (12, EY, 256)])(s, left, right)
    before, after = from_both(last, first, "gy")
    (own,) = call(lengthen_kernel, [(12, ROWS0, 256)])(z, before, after)
    left, right = from_both_round(own, "gx")
    wide0 = (ROWS0, 256)
    up0 = (8, 80, 256)
    b1, black0, red_b0, black_b0 = call(
        functools.partial(fine_down_kernel, n),
        [(4, ROWS1, 128), up0, up0, up0],
        [(14, *wide0), (14, *wide0), (12, *wide0), (12, *wide0), wide0, (8, ROWS0, 128)],
    )(own, left, right)
    b1 = gathered(b1, "gx").reshape(4 * n[0], ROWS1, 128)
    all1 = (2 * n[0], ROWS1, 128)
    pad1 = (2 * n[0] + 2, ROWS1, 128)
    b2, black1, red_b1, black_b1 = call(
        functools.partial(middle_down_kernel, n),
        [(n[0], 16, 128), all1, all1, all1],
        [pad1, pad1, (ROWS1, 128), all1],
    )(b1)
    left, right = from_both(b2, b2, "gz")
    (b2,) = call(functools.partial(widen_coarse_kernel, n), [(2 * n[0], 16, 128)])(b2, left, right)
    b2 = gathered(b2, "gy").reshape(n[1], 2 * n[0], 16, 128)
    rows2, rows3 = 16 * n[1], 8 * n[1]
    p2, p3 = n[0], n[0] // 2
    w2, w3 = (rows2 + 8, 128), (rows3 + 8, 128)
    (out,) = call(
        functools.partial(up_kernel, n),
        [(8, 64, 128)],
        [
            (p2, *w2), (p2, *w2), (p2 + 2, *w2), (p2 + 2, *w2), w2, (p2, *w2),
            (p3, *w3), (p3, *w3), (p3 + 2, *w3), (p3 + 2, *w3), w3, (p2, rows2, 128),
            (2 * n[0], rows2 + 32, 128), (2 * n[0], 40, 128), all1, pad1, (ROWS1, 128), (16, 80, 128),
            (10, 80, 256), (80, 256), pad1, (10, 80, 256),
        ],
    )(b2, black1, red_b1, black_b1, black0, red_b0, black_b0)
    return out


def solution(mesh):
    in_specs = (P("gx", "gy", "gz"), P("gx", "gy", "gz"))
    out_specs = P("gx", "gy", "gz")
    return jax.shard_map(local, mesh=mesh, in_specs=in_specs, out_specs=out_specs, check_vma=False)
```

time: 653 us -> 121 us (0.19)
  the two profiles are of different devices: /device:TPU:96 before, /device:TPU:384 now
where the time goes in v1:
time: 121 us
  waiting for transfers between devices  36 us (30%)
  Pallas kernels  31.8 us (26%)
  blocking collectives  31.3 us (26%)
  starting transfers between devices  19.5 us (16%)
  local copies, waits for them, and re-layouts  2 us (2%)
    all_to_all x2, blocking collectives, gathered(): return lax.all_to_all(copies, axis, split_axis=0, concat_axis=0, tiled=True)  31.3 us
    pallas_call x1, Pallas kernels, local(): call(functools.partial(up_kernel, n), [(8, 64, 128)], [(p2, *w2), (p2, *w...  18.8 us
    ppermute x1, waiting for transfers between devices, from_both_round(): lax.ppermute(value, axis, [(b, a) for a, b in up])  15.4 us
    ppermute x3, waiting for transfers between devices, from_both(): lax.ppermute(up_value, axis, up)  11.8 us
    ppermute x3, starting transfers between devices, from_both(): lax.ppermute(down_value, axis, [(b, a) for a, b in up])  10.8 us
    ppermute x3, starting transfers between devices, from_both(): lax.ppermute(up_value, axis, up)  8.26 us
    pallas_call x1, Pallas kernels, local(): call(functools.partial(middle_down_kernel, n), [(n[0], 16, 128), all1, al...  6.23 us
    pallas_call x1, Pallas kernels, local(): call(functools.partial(fine_down_kernel, n), [(4, ROWS1, 128), up0, up0,...  6.13 us
  transfers between devices with their start and end apart: 8, of which 7 were waited for; matrix products, arithmetic and copies ran while one was open for 0% of the time, Pallas kernels for 0%

profile of v1, /device:TPU:384, one launch (start us, length us, event | category | flops | bytes accessed | tf_op | source)
XLA Modules:
  0.0 120.8 jit_solution(14762410141154899390)
XLA Ops:
  0.0 0.0 copy-start
  0.0 0.9 copy-done
  1.0 0.0 copy-start.1
  1.0 0.9 copy-done.1
  1.9 0.2 shard_map.28
  2.1 2.9 %collective-permute-start = (f32[6,64,128]{2,1,0:T(8,128)S(1)}, f32[6,64,128]{2,1,0:T(8,128)S(1)}, u32[]{:S(2)}, u32[]{:S(2)}) collective-permute-start(f32[6,64,128]{2,1,0:T(8,128)S(1)} %get-tuple-element.20), channel_id=1, source_target_pairs={{0,1},{1,2},{2,3},{3,4},{4,5},{5,6},{6,7},{7,8},{8,9},{9,10},{10,1... | collective-permute-start | bytes 589832 | tf_op jit(solution)/shard_map/ppermute | solution.py:373
  5.0 4.1 %collective-permute-start.1 = (f32[6,64,128]{2,1,0:T(8,128)S(1)}, f32[6,64,128]{2,1,0:T(8,128)S(1)}, u32[]{:S(2)}, u32[]{:S(2)}) collective-permute-start(f32[6,64,128]{2,1,0:T(8,128)S(1)} %get-tuple-element.21), channel_id=1, source_target_pairs={{1,0},{2,1},{3,2},{4,3},{5,4},{6,5},{7,6},{8,7},{9,8},{10,9},{11,1... | collective-permute-start | bytes 589832 | tf_op jit(solution)/shard_map/ppermute | solution.py:373
  9.2 2.7 %collective-permute-done.left = f32[6,64,128]{2,1,0:T(8,128)S(1)} collective-permute-done((f32[6,64,128]{2,1,0:T(8,128)S(1)}, f32[6,64,128]{2,1,0:T(8,128)S(1)}, u32[]{:S(2)}, u32[]{:S(2)}) %collective-permute-start) | collective-permute-done | bytes 196640 | tf_op jit(solution)/shard_map/ppermute | solution.py:373
  11.8 1.4 %collective-permute-done.1.right = f32[6,64,128]{2,1,0:T(8,128)S(1)} collective-permute-done((f32[6,64,128]{2,1,0:T(8,128)S(1)}, f32[6,64,128]{2,1,0:T(8,128)S(1)}, u32[]{:S(2)}, u32[]{:S(2)}) %collective-permute-start.1) | collective-permute-done | bytes 196640 | tf_op jit(solution)/shard_map/ppermute | solution.py:373
  13.3 0.3 shard_map.29
  13.6 3.4 %collective-permute-start.2 = (f32[12,24,256]{2,1,0:T(8,128)S(1)}, f32[12,24,256]{2,1,0:T(8,128)S(1)}, u32[]{:S(2)}, u32[]{:S(2)}) collective-permute-start(f32[12,24,256]{2,1,0:T(8,128)S(1)} %get-tuple-element.23), channel_id=1, source_target_pairs={{0,16},{16,32},{32,48},{1,17},{17,33},{33,49},{2,18},{18,34},{34,5... | collective-permute-start | bytes 884744 | tf_op jit(solution)/shard_map/ppermute | solution.py:373
  17.0 1.3 %collective-permute-start.3 = (f32[12,24,256]{2,1,0:T(8,128)S(1)}, f32[12,24,256]{2,1,0:T(8,128)S(1)}, u32[]{:S(2)}, u32[]{:S(2)}) collective-permute-start(f32[12,24,256]{2,1,0:T(8,128)S(1)} %get-tuple-element.24), channel_id=1, source_target_pairs={{16,0},{32,16},{48,32},{17,1},{33,17},{49,33},{18,2},{34,18},{50,3... | collective-permute-start | bytes 884744 | tf_op jit(solution)/shard_map/ppermute | solution.py:373
  18.3 3.7 %collective-permute-done.2.before = f32[12,24,256]{2,1,0:T(8,128)S(1)} collective-permute-done((f32[12,24,256]{2,1,0:T(8,128)S(1)}, f32[12,24,256]{2,1,0:T(8,128)S(1)}, u32[]{:S(2)}, u32[]{:S(2)}) %collective-permute-start.2) | collective-permute-done | bytes 294944 | tf_op jit(solution)/shard_map/ppermute | solution.py:373
  22.0 4.1 %collective-permute-done.3.after = f32[12,24,256]{2,1,0:T(8,128)S(1)} collective-permute-done((f32[12,24,256]{2,1,0:T(8,128)S(1)}, f32[12,24,256]{2,1,0:T(8,128)S(1)}, u32[]{:S(2)}, u32[]{:S(2)}) %collective-permute-start.3) | collective-permute-done | bytes 294944 | tf_op jit(solution)/shard_map/ppermute | solution.py:373
  26.1 0.1 shard_map.30.own
  26.2 0.1 collective-permute-start.5
  26.3 0.4 collective-permute-start.4
  26.8 15.4 %collective-permute-done.5.right = f32[12,112,256]{2,1,0:T(8,128)S(1)} collective-permute-done((f32[12,112,256]{2,1,0:T(8,128)S(1)}, f32[12,112,256]{2,1,0:T(8,128)S(1)}, u32[]{:S(2)}, u32[]{:S(2)}) %collective-permute-start.5) | collective-permute-done | bytes 1376288 | tf_op jit(solution)/shard_map/ppermute | solution.py:379
  42.1 3.2 %collective-permute-done.4.left = f32[12,112,256]{2,1,0:T(8,128)S(1)} collective-permute-done((f32[12,112,256]{2,1,0:T(8,128)S(1)}, f32[12,112,256]{2,1,0:T(8,128)S(1)}, u32[]{:S(2)}, u32[]{:S(2)}) %collective-permute-start.4) | collective-permute-done | bytes 1376288 | tf_op jit(solution)/shard_map/ppermute | solution.py:379
  45.4 6.1 %shard_map.31 = (f32[4,56,128]{2,1,0:T(8,128)S(1)}, f32[8,80,256]{2,1,0:T(8,128)S(1)}, f32[8,80,256]{2,1,0:T(8,128)S(1)}, f32[8,80,256]{2,1,0:T(8,128)S(1)}) custom-call(f32[12,112,256]{2,1,0:T(8,128)S(1)} %shard_map.30.own, f32[12,112,256]{2,1,0:T(8,128)S(1)} %collective-permute-done.4.left, f32[12,112,256]{2,1,0:T(8,128)S(1)} %collective-permute-done.5.right), custom_call_target="tpu_custom_call" | custom-call | tf_op jit(solution)/shard_map/pallas_call | solution.py:397
  51.5 0.1 broadcast_in_dim.6
  51.6 19.5 %all_to_all.10 = f32[8,4,56,128]{3,2,1,0:T(8,128)S(1)} all-to-all(f32[8,4,56,128]{3,2,1,0:T(8,128)S(1)} %broadcast_in_dim.6), channel_id=1, replica_groups=mesh['gx'=8,'gy'=4,'gz'=16] {'gx'}, dimensions={0} | all-to-all | bytes 1835008 | tf_op jit(solution)/shard_map/all_to_all | solution.py:384
  71.0 6.2 %shard_map.32 = (f32[8,16,128]{2,1,0:T(8,128)S(1)}, f32[16,56,128]{2,1,0:T(8,128)S(1)}, f32[16,56,128]{2,1,0:T(8,128)S(1)}, f32[16,56,128]{2,1,0:T(8,128)S(1)}) custom-call(f32[32,56,128]{2,1,0:T(8,128)S(1)} %bitcast.1), custom_call_target="tpu_custom_call" | custom-call | tf_op jit(solution)/shard_map/pallas_call | solution.py:405
  77.3 5.3 %collective-permute-start.7 = (f32[8,16,128]{2,1,0:T(8,128)S(1)}, f32[8,16,128]{2,1,0:T(8,128)S(1)}, u32[]{:S(2)}, u32[]{:S(2)}) collective-permute-start(f32[8,16,128]{2,1,0:T(8,128)S(1)} %get-tuple-element.26.own), channel_id=1, source_target_pairs={{1,0},{2,1},{3,2},{4,3},{5,4},{6,5},{7,6},{8,7},{9,8},{10,9},{11,1... | collective-permute-start | bytes 196616 | tf_op jit(solution)/shard_map/ppermute | solution.py:373
  82.6 1.9 %collective-permute-start.6 = (f32[8,16,128]{2,1,0:T(8,128)S(1)}, f32[8,16,128]{2,1,0:T(8,128)S(1)}, u32[]{:S(2)}, u32[]{:S(2)}) collective-permute-start(f32[8,16,128]{2,1,0:T(8,128)S(1)} %get-tuple-element.26.own), channel_id=1, source_target_pairs={{0,1},{1,2},{2,3},{3,4},{4,5},{5,6},{6,7},{7,8},{8,9},{9,10},{10,1... | collective-permute-start | bytes 196616 | tf_op jit(solution)/shard_map/ppermute | solution.py:373
  84.6 0.0 collective-permute-done.7.right
  84.6 5.4 %collective-permute-done.6.left = f32[8,16,128]{2,1,0:T(8,128)S(1)} collective-permute-done((f32[8,16,128]{2,1,0:T(8,128)S(1)}, f32[8,16,128]{2,1,0:T(8,128)S(1)}, u32[]{:S(2)}, u32[]{:S(2)}) %collective-permute-start.6) | collective-permute-done | bytes 65568 | tf_op jit(solution)/shard_map/ppermute | solution.py:373
  90.0 0.1 shard_map.33
  90.2 11.9 %all_to_all.11.b2 = f32[4,16,16,128]{3,2,1,0:T(8,128)S(1)} all-to-all(f32[4,16,16,128]{3,2,1,0:T(8,128)S(1)} %broadcast_in_dim.7), channel_id=1, replica_groups=mesh['gx'=8,'gy'=4,'gz'=16] {'gy'}, dimensions={0} | all-to-all | bytes 1048576 | tf_op jit(solution)/shard_map/all_to_all | solution.py:384
  102.1 18.8 %shard_map.34 = f32[8,64,128]{2,1,0:T(8,128)} custom-call(f32[4,16,16,128]{3,2,1,0:T(8,128)S(1)} %all_to_all.11.b2, f32[16,56,128]{2,1,0:T(8,128)S(1)} %get-tuple-element.27.black1, f32[16,56,128]{2,1,0:T(8,128)S(1)} %get-tuple-element.28.red_b1, f32[16,56,128]{2,1,0:T(8,128)S(1)} %get-tuple-element.29.black_b1, f32[8,80,256]{2,1,0:T(8,128)S(1)} %get-tuple-element.30.black0, ...), custom_call_target="tpu_custom_call" | custom-call | tf_op jit(solution)/shard_map/pallas_call | solution.py:416
  (1 shorter events, 0.0 us)
Async XLA Ops:
  0.0 0.9 copy-start
  1.0 0.9 copy-start.1
  2.1 9.7 %collective-permute-start = (f32[6,64,128]{2,1,0:T(8,128)S(1)}, f32[6,64,128]{2,1,0:T(8,128)S(1)}, u32[]{:S(2)}, u32[]{:S(2)}) collective-permute-start(f32[6,64,128]{2,1,0:T(8,128)S(1)} %get-tuple-element.20), channel_id=1, source_target_pairs={{0,1},{1,2},{2,3},{3,4},{4,5},{5,6},{6,7},{7,8},{8,9},{9,10},{10,1... | collective-permute-start | bytes 589832 | tf_op jit(solution)/shard_map/ppermute | solution.py:373
  5.0 8.3 %collective-permute-start.1 = (f32[6,64,128]{2,1,0:T(8,128)S(1)}, f32[6,64,128]{2,1,0:T(8,128)S(1)}, u32[]{:S(2)}, u32[]{:S(2)}) collective-permute-start(f32[6,64,128]{2,1,0:T(8,128)S(1)} %get-tuple-element.21), channel_id=1, source_target_pairs={{1,0},{2,1},{3,2},{4,3},{5,4},{6,5},{7,6},{8,7},{9,8},{10,9},{11,1... | collective-permute-start | bytes 589832 | tf_op jit(solution)/shard_map/ppermute | solution.py:373
  13.6 8.5 %collective-permute-start.2 = (f32[12,24,256]{2,1,0:T(8,128)S(1)}, f32[12,24,256]{2,1,0:T(8,128)S(1)}, u32[]{:S(2)}, u32[]{:S(2)}) collective-permute-start(f32[12,24,256]{2,1,0:T(8,128)S(1)} %get-tuple-element.23), channel_id=1, source_target_pairs={{0,16},{16,32},{32,48},{1,17},{17,33},{33,49},{2,18},{18,34},{34,5... | collective-permute-start | bytes 884744 | tf_op jit(solution)/shard_map/ppermute | solution.py:373
  17.0 9.2 %collective-permute-start.3 = (f32[12,24,256]{2,1,0:T(8,128)S(1)}, f32[12,24,256]{2,1,0:T(8,128)S(1)}, u32[]{:S(2)}, u32[]{:S(2)}) collective-permute-start(f32[12,24,256]{2,1,0:T(8,128)S(1)} %get-tuple-element.24), channel_id=1, source_target_pairs={{16,0},{32,16},{48,32},{17,1},{33,17},{49,33},{18,2},{34,18},{50,3... | collective-permute-start | bytes 884744 | tf_op jit(solution)/shard_map/ppermute | solution.py:373
  26.2 15.9 %collective-permute-start.5 = (f32[12,112,256]{2,1,0:T(8,128)S(1)}, f32[12,112,256]{2,1,0:T(8,128)S(1)}, u32[]{:S(2)}, u32[]{:S(2)}) collective-permute-start(f32[12,112,256]{2,1,0:T(8,128)S(1)} %shard_map.30.own), channel_id=1, source_target_pairs={{64,0},{128,64},{192,128},{256,192},{320,256},{384,320},{448,384},... | collective-permute-start | bytes 4128776 | tf_op jit(solution)/shard_map/ppermute | solution.py:379
  26.3 19.1 %collective-permute-start.4 = (f32[12,112,256]{2,1,0:T(8,128)S(1)}, f32[12,112,256]{2,1,0:T(8,128)S(1)}, u32[]{:S(2)}, u32[]{:S(2)}) collective-permute-start(f32[12,112,256]{2,1,0:T(8,128)S(1)} %shard_map.30.own), channel_id=1, source_target_pairs={{0,64},{64,128},{128,192},{192,256},{256,320},{320,384},{384,448},... | collective-permute-start | bytes 4128776 | tf_op jit(solution)/shard_map/ppermute | solution.py:379
  77.3 7.3 %collective-permute-start.7 = (f32[8,16,128]{2,1,0:T(8,128)S(1)}, f32[8,16,128]{2,1,0:T(8,128)S(1)}, u32[]{:S(2)}, u32[]{:S(2)}) collective-permute-start(f32[8,16,128]{2,1,0:T(8,128)S(1)} %get-tuple-element.26.own), channel_id=1, source_target_pairs={{1,0},{2,1},{3,2},{4,3},{5,4},{6,5},{7,6},{8,7},{9,8},{10,9},{11,1... | collective-permute-start | bytes 196616 | tf_op jit(solution)/shard_map/ppermute | solution.py:373
  82.6 7.4 %collective-permute-start.6 = (f32[8,16,128]{2,1,0:T(8,128)S(1)}, f32[8,16,128]{2,1,0:T(8,128)S(1)}, u32[]{:S(2)}, u32[]{:S(2)}) collective-permute-start(f32[8,16,128]{2,1,0:T(8,128)S(1)} %get-tuple-element.26.own), channel_id=1, source_target_pairs={{0,1},{1,2},{2,3},{3,4},{4,5},{5,6},{6,7},{7,8},{8,9},{9,10},{10,1... | collective-permute-start | bytes 196616 | tf_op jit(solution)/shard_map/ppermute | solution.py:373

commit v2 on v0

v2 whole, which is shorter than its diff:
```python
import functools

import jax
import jax.numpy as jnp
from jax import lax
from jax.experimental import pallas as pl
from jax.experimental.pallas import tpu as pltpu
from jax.sharding import PartitionSpec as P

F32 = jnp.float32
BF16 = jnp.bfloat16
SIXTH = 1.0 / 6.0
EY = 24
ROWS0 = 64 + 2 * EY
ROWS1 = ROWS0 // 2
PAD = 8
UP0 = EY - 8
VMEM_LIMIT = 40 * 1024 * 1024


def call(kernel, outs, scratch=(), in_specs=None):
    shapes = [jax.ShapeDtypeStruct(s, F32) for s in outs]
    extra = {} if in_specs is None else {"in_specs": in_specs}
    return pl.pallas_call(
        kernel,
        out_shape=shapes,
        scratch_shapes=[pltpu.VMEM(s, F32) if isinstance(s, tuple) else s for s in scratch],
        compiler_params=pltpu.CompilerParams(vmem_limit_bytes=VMEM_LIMIT),
        **extra,
    )


def even_mask(shape):
    rows = lax.broadcasted_iota(jnp.int32, shape, 0)
    lanes = lax.broadcasted_iota(jnp.int32, shape, 1)
    return ((rows + lanes) & 1) == 0


def lane_of(shape):
    return lax.broadcasted_iota(jnp.int32, shape, 1)


def domain(shape, row0, rows, lane0, lanes, cut, unused=None):
    y = lax.broadcasted_iota(jnp.int32, shape, 0) + row0
    k = lane_of(shape)
    z = jnp.where(k < cut, k, k - shape[1]) + lane0
    inside = (y >= 0) & (y < rows) & (z >= 0) & (z < lanes)
    if unused is not None:
        inside = inside & ((k < unused[0]) | (k >= unused[1]))
    return jnp.where(inside, F32(SIXTH), F32(0.0))


def beside(src, i, r, rows, even, red):
    at = PAD + r
    c = src[i + 1, at : at + rows]
    below, above = src[i, at : at + rows], src[i + 2, at : at + rows]
    s = c + (jnp.where(even, below, above) if red else jnp.where(even, above, below))
    s = s + (src[i + 1, at - 1 : at - 1 + rows] + src[i + 1, at + 1 : at + 1 + rows])
    return s + (pltpu.roll(c, 1, 1) + pltpu.roll(c, c.shape[1] - 1, 1))


def half(dst, src, b, weight, red, pairs, rows, step):
    even = even_mask((step, dst.shape[2]))
    for i in pairs:
        for r in range(0, rows, step):
            value = (b[i, r : r + step] + beside(src, i, r, step, even, red)) * weight(i, r, step)
            dst[i + 1, PAD + r : PAD + r + step] = value


def residual_sum(red, black, red_b, black_b, i, r, step, even):
    at = PAD + r
    x = red_b[i, r : r + step] - 6.0 * red[i + 1, at : at + step] + beside(black, i, r, step, even, True)
    y = black_b[i, r : r + step] - 6.0 * black[i + 1, at : at + step] + beside(red, i, r, step, even, False)
    return x + y


def clear_pads(*colours):
    for ref in colours:
        pairs, rows, lanes = ref.shape
        for i in (0, pairs - 1):
            ref[i] = jnp.zeros((rows, lanes), F32)
        for i in range(1, pairs - 1):
            ref[i, :PAD] = jnp.zeros((PAD, lanes), F32)
            ref[i, rows - PAD :] = jnp.zeros((PAD, lanes), F32)


def table(rows, cols, of, value=1.0):
    k = lax.broadcasted_iota(jnp.int32, (rows, cols), 0)
    c = lax.broadcasted_iota(jnp.int32, (rows, cols), 1)
    return jnp.where(of(k, c), F32(value), F32(0.0)).astype(BF16)


def dot(a, m):
    high = a.astype(BF16)
    rest = a - high.astype(F32)
    middle = rest.astype(BF16)
    low = (rest - middle.astype(F32)).astype(BF16)
    parts = jnp.concatenate([high, middle, low], axis=1)
    return jnp.dot(parts, jnp.concatenate([m, m, m], axis=0), preferred_element_type=F32)


def pack_kernel(start_hbm, right_hbm, s, up, down, start, right, sem_a, sem_b):
    copy_a = pltpu.make_async_copy(start_hbm, start, sem_a)
    copy_b = pltpu.make_async_copy(right_hbm, right, sem_b)
    copy_a.start()
    copy_b.start()
    even = even_mask((64, 128))
    low = lane_of((64, 128)) < 64
    copy_a.wait()
    copy_b.wait()
    for p in range(4):
        s[p] = jnp.where(even, start[2 * p + 1], start[2 * p])
        s[p + 4] = jnp.where(even, right[2 * p], right[2 * p + 1])
        s[p + 8] = jnp.where(even, right[2 * p + 1], right[2 * p])
    for p in range(6):
        a, b = s[p], pltpu.roll(s[p + 6], 64, 1)
        up[p] = jnp.where(low, b, a)
        down[p] = jnp.where(low, a, b)


def widen_kernel(s, up, down, v, first, last):
    low = lane_of((64, 128)) < 64
    for p in range(6):
        v[p] = jnp.where(low, down[p], up[p])
        v[p + 6] = pltpu.roll(jnp.where(low, up[p], down[p]), 64, 1)
    for p in range(12):
        first[p, :, :128] = s[p, :EY]
        first[p, :, 128:] = v[p, :EY]
        last[p, :, :128] = s[p, 64 - EY :]
        last[p, :, 128:] = v[p, 64 - EY :]


def strips_kernel(before, after, up, down):
    for a in range(3):
        for q in range(2):
            for ref, near, far in ((up, 2 + q, q), (down, q, 2 + q)):
                j = 2 * a + q
                ref[j, :EY] = before[4 * a + near]
                ref[j, EY : 2 * EY] = after[4 * a + near]
                ref[j, 48:56] = before[4 * a + far, EY - 8 :]
                ref[j, 56:64] = after[4 * a + far, :8]


def fine_down_kernel(
    n, s, v, before, after, s_left, s_right, v_left, v_right, y_left, y_right,
    coarse, black_out, red_b_out, black_b_out, red, black, rb, bb, weight, pairs,
):
    gx, gy, gz = (lax.axis_index(a) for a in ("gx", "gy", "gz"))
    inner = domain((ROWS0, 256), 64 * gy - EY, 64 * n[1], 128 * gz, 128 * n[2], 192)
    has_left, has_right = gx > 0, gx < n[0] - 1
    weight[0] = jnp.where(has_left, inner, 0.0)
    weight[1] = inner
    weight[2] = jnp.where(has_right, inner, 0.0)
    clear_pads(black, red)
    zero8 = jnp.zeros((8, 256), F32)
    for a, ref in enumerate((black, rb, bb)):
        off, top = (1, PAD) if a == 0 else (0, 0)
        mid, end = top + EY, top + EY + 64

        def put(i, lo, value, keep, ref=ref, off=off, a=a):
            hi = lo + value.shape[0]
            lanes = slice(0, 256) if value.shape[1] == 256 else keep[1]
            if a == 0 and keep[0] is not None:
                value = jnp.where(keep[0], value, 0.0)
            ref[i + off, lo:hi, lanes] = value

        for p in range(4):
            j = 4 * a + p
            for base, centre, strip, there in ((4, s, v, None), (0, s_left, v_left, has_left), (8, s_right, v_right, has_right)):
                put(base + p, mid, centre[j], (there, slice(0, 128)))
                put(base + p, mid, strip[j], (there, slice(128, 256)))
            put(4 + p, top, before[j], (None, None))
            put(4 + p, end, after[j], (None, None))
        for q in range(2):
            j = 2 * a + q
            for base, y, near, far, there in ((0, y_left, 2 + q, q, has_left), (8, y_right, q, 2 + q, has_right)):
                put(base + near, top, y[j, :EY], (there, None))
                put(base + near, end, y[j, EY : 2 * EY], (there, None))
                for k in range(2):
                    put(base + far, top + 8 * k, zero8, (None, None))
                    put(base + far, end + 8 + 8 * k, zero8, (None, None))
                put(base + far, mid - 8, y[j, 48:56], (there, None))
                put(base + far, end, y[j, 56:64], (there, None))

    def weights(i, r, step):
        return weight[i // 4, r : r + step]

    half(red, black, rb, weights, True, range(0, 12), ROWS0, 16)
    half(black, red, bb, weights, False, range(1, 11), ROWS0, 16)
    half(red, black, rb, weights, True, range(1, 11), ROWS0, 16)
    half(black, red, bb, weights, False, range(2, 10), ROWS0, 16)
    even = even_mask((16, 256))
    for p in range(4):
        for r in range(0, ROWS0, 16):
            value = residual_sum(red, black, rb, bb, p + 4, r, 16, even)
            pairs[2 * p, r : r + 16] = value[:, :128]
            pairs[2 * p + 1, r : r + 16] = value[:, 128:]
    rows = []
    for p in range(4):
        parts = [pairs[2 * p + h, pl.ds(0, ROWS1, stride=2), :] + pairs[2 * p + h, pl.ds(1, ROWS1, stride=2), :] for h in (0, 1)]
        rows.append(jnp.concatenate(parts, axis=1))
    result = dot(jnp.concatenate(rows, axis=0), table(256, 128, lambda k, c: (k >> 1) == c, 0.5))
    for p in range(4):
        coarse[p] = result[p * ROWS1 : (p + 1) * ROWS1]
    for p in range(8):
        black_out[p] = black[p + 3, PAD + UP0 : PAD + UP0 + 80]
        red_b_out[p] = rb[p + 2, UP0 : UP0 + 80]
        black_b_out[p] = bb[p + 2, UP0 : UP0 + 80]


def middle_down_kernel(n, b1, coarse, black_out, red_b_out, black_b_out, red, black, rb, bb, weight, pairs):
    gx, gy, gz = (lax.axis_index(a) for a in ("gx", "gy", "gz"))
    count = 2 * n[0]
    even = even_mask((ROWS1, 128))
    weight[...] = domain((ROWS1, 128), 32 * gy - EY // 2, 32 * n[1], 64 * gz, 64 * n[2], 96)
    clear_pads(red, black)
    for i in range(count):
        a, b = b1[2 * i], b1[2 * i + 1]
        r = jnp.where(even, a, b)
        rb[i] = r
        bb[i] = jnp.where(even, b, a)
        red[i + 1, PAD : PAD + ROWS1] = r * weight[...]

    def weights(i, r, step):
        return weight[r : r + step]

    every = range(count)
    half(black, red, bb, weights, False, every, ROWS1, ROWS1)
    half(red, black, rb, weights, True, every, ROWS1, ROWS1)
    half(black, red, bb, weights, False, every, ROWS1, ROWS1)
    for i in range(8):
        q = 2 * gx - 3 + i
        inside = jnp.clip(q, 0, count - 1)
        black_out[i] = black[jnp.clip(q + 1, 0, count + 1), PAD : PAD + ROWS1]
        red_b_out[i] = rb[inside]
        black_b_out[i] = bb[inside]
    top = EY // 2 - 4
    even40 = even_mask((40, 128))
    for i in every:
        pairs[i] = residual_sum(red, black, rb, bb, i, top, 40, even40)
    sums = [pairs[i, pl.ds(4, 16, stride=2), :] + pairs[i, pl.ds(5, 16, stride=2), :] for i in every]
    low = jnp.concatenate(sums[: n[0]], axis=0)
    high = jnp.concatenate(sums[n[0] :], axis=0)
    result = dot(jnp.concatenate([low, high], axis=1), table(256, 128, lambda k, c: (k >> 1) == c, 0.5))
    for i in range(n[0]):
        coarse[i] = result[16 * i : 16 * i + 16]


def widen_coarse_kernel(n, own, left, right, wide):
    lanes = lane_of((16, 128))
    for i in range(n[0]):
        w, a, b = own[i], left[i], right[i]
        a32, a96, b32, b96 = pltpu.roll(a, 32, 1), pltpu.roll(a, 96, 1), pltpu.roll(b, 32, 1), pltpu.roll(b, 96, 1)
        for k, x, y, z0, z1 in ((i, w, b32, a32, a96), (i + n[0], pltpu.roll(w, 64, 1), b96, a96, a32)):
            wide[k] = jnp.where(lanes < 32, x, jnp.where(lanes < 80, y, jnp.where(lanes < 96, z0, z1)))


def up_kernel(
    n, b2, black1, red_b1, black_b1, black0, red_b0, black_b0, out,
    rb2, bb2, red2, black2, weight2, pairs2,
    rb3, bb3, red3, black3, weight3, add2,
    add1, red1, bl1, weight1,
    add0, red0, bl0, weight0,
):
    gx, gy, gz = (lax.axis_index(a) for a in ("gx", "gy", "gz"))
    rows2, rows3 = 16 * n[1], 8 * n[1]
    pairs_2, pairs_3 = n[0], n[0] // 2

    weight2[...] = domain((rows2, 128), 0, rows2, 32 * gz, 32 * n[2], 80)
    clear_pads(red2, black2)
    even16 = even_mask((16, 128))
    for i in range(pairs_2):
        for g in range(n[1]):
            a, b = b2[g, 2 * i], b2[g, 2 * i + 1]
            at = 16 * g
            r = jnp.where(even16, a, b)
            rb2[i, at : at + 16] = r
            bb2[i, at : at + 16] = jnp.where(even16, b, a)
            red2[i + 1, PAD + at : PAD + at + 16] = r * weight2[at : at + 16]

    def weights2(i, r, step):
        return weight2[r : r + step]

    every2 = range(pairs_2)
    half(black2, red2, bb2, weights2, False, every2, rows2, rows2)
    half(red2, black2, rb2, weights2, True, every2, rows2, rows2)
    half(black2, red2, bb2, weights2, False, every2, rows2, rows2)
    even2 = even_mask((rows2, 128))
    for i in every2:
        pairs2[i] = residual_sum(red2, black2, rb2, bb2, i, 0, rows2, even2)
    sums = [pairs2[i, pl.ds(0, rows3, stride=2), :] + pairs2[i, pl.ds(1, rows3, stride=2), :] for i in every2]
    to3 = lambda k, c: jnp.where(k < 80, k >> 1, (k >> 1) + 64) == c
    b3 = dot(jnp.concatenate(sums, axis=0), table(128, 128, to3, 0.5))

    even3 = even_mask((rows3, 128))
    weight3[...] = domain((rows3, 128), 0, rows3, 16 * gz, 16 * n[2], 64, (40, 104))
    clear_pads(red3, black3)
    for i in range(pairs_3):
        a = b3[2 * i * rows3 : (2 * i + 1) * rows3]
        b = b3[(2 * i + 1) * rows3 : (2 * i + 2) * rows3]
        r = jnp.where(even3, a, b)
        rb3[i] = r
        bb3[i] = jnp.where(even3, b, a)
        red3[i + 1, PAD : PAD + rows3] = r * weight3[...]

    def weights3(i, r, step):
        return weight3[r : r + step]

    every3 = range(pairs_3)
    half(black3, red3, bb3, weights3, False, every3, rows3, rows3)

    def sweep3(_, carry):
        half(red3, black3, rb3, weights3, True, every3, rows3, rows3)
        half(black3, red3, bb3, weights3, False, every3, rows3, rows3)
        return carry

    lax.fori_loop(0, 7, sweep3, 0)
    planes = []
    for i in every3:
        r, b = red3[i + 1, PAD : PAD + rows3], black3[i + 1, PAD : PAD + rows3]
        planes += [jnp.where(even3, r, b), jnp.where(even3, b, r)]
    wide = dot(jnp.concatenate(planes, axis=0), table(128, 128, lambda k, c: to3(c, k)))
    for i in every2:
        w = wide[i * rows3 : (i + 1) * rows3]
        add2[i, pl.ds(0, rows3, stride=2), :] = w
        add2[i, pl.ds(1, rows3, stride=2), :] = w
        black2[i + 1, PAD : PAD + rows2] = black2[i + 1, PAD : PAD + rows2] + add2[i]
    for _ in range(2):
        half(red2, black2, rb2, weights2, True, every2, rows2, rows2)
        half(black2, red2, bb2, weights2, False, every2, rows2, rows2)

    even32 = even_mask((32, 128))
    top = pl.multiple_of(16 * gy, 8)
    planes = []
    for i in range(8):
        q = jnp.clip(gx - 1 + (i + 1) // 2, 0, n[0] + 1)
        r, b = red2[q, pl.ds(top, 32), :], black2[q, pl.ds(top, 32), :]
        planes.append(jnp.where(even32, r, b) if i % 2 == 1 else jnp.where(even32, b, r))
    to2 = lambda k, c: jnp.where(c < 96, c >> 1, (c >> 1) + 64) == k
    wide = dot(jnp.concatenate(planes, axis=0), table(128, 128, to2))
    inner = domain((ROWS1, 128), 32 * gy - EY // 2, 32 * n[1], 64 * gz, 64 * n[2], 96)
    clear_pads(red1, bl1)
    skip = PAD - EY // 4
    for i in range(8):
        q = 2 * gx - 3 + i
        weight1[i] = jnp.where((q >= 0) & (q < 2 * n[0]), inner, 0.0)
        w = wide[32 * i + skip : 32 * i + skip + ROWS1 // 2]
        add1[i, pl.ds(0, ROWS1 // 2, stride=2), :] = w
        add1[i, pl.ds(1, ROWS1 // 2, stride=2), :] = w
        bl1[i + 1, PAD : PAD + ROWS1] = black1[i] + add1[i]

    def weights1(i, r, step):
        return weight1[i, r : r + step]

    half(red1, bl1, red_b1, weights1, True, range(0, 8), ROWS1, ROWS1)
    half(bl1, red1, black_b1, weights1, False, range(1, 7), ROWS1, ROWS1)
    half(red1, bl1, red_b1, weights1, True, range(1, 7), ROWS1, ROWS1)
    half(bl1, red1, black_b1, weights1, False, range(2, 6), ROWS1, ROWS1)

    low1 = PAD + UP0 // 2
    even40 = even_mask((40, 128))
    planes = []
    for i in range(8):
        r, b = red1[3 + i // 2, low1 : low1 + 40], bl1[3 + i // 2, low1 : low1 + 40]
        planes.append(jnp.where(even40, r, b) if i % 2 == 0 else jnp.where(even40, b, r))
    wide = dot(jnp.concatenate(planes, axis=0), table(128, 256, lambda k, c: (c >> 1) == k))
    inner = domain((80, 256), 64 * gy - 8, 64 * n[1], 128 * gz, 128 * n[2], 192)
    weight0[0] = jnp.where(gx > 0, inner, 0.0)
    weight0[1] = inner
    weight0[2] = jnp.where(gx < n[0] - 1, inner, 0.0)
    clear_pads(red0, bl0)
    for i in range(8):
        for h in (0, 1):
            w = wide[40 * i : 40 * i + 40, 128 * h : 128 * h + 128]
            add0[2 * i + h, pl.ds(0, 40, stride=2), :] = w
            add0[2 * i + h, pl.ds(1, 40, stride=2), :] = w
            bl0[i + 1, PAD : PAD + 80, 128 * h : 128 * h + 128] = black0[i, :, 128 * h : 128 * h + 128] + add0[2 * i + h]

    def weights0(i, r, step):
        return weight0[(i + 2) // 4, r : r + step]

    half(red0, bl0, red_b0, weights0, True, range(0, 8), 80, 16)
    half(bl0, red0, black_b0, weights0, False, range(1, 7), 80, 16)
    half(red0, bl0, red_b0, weights0, True, range(1, 7), 80, 16)
    half(bl0, red0, black_b0, weights0, False, range(2, 6), 80, 16)
    even64 = even_mask((64, 128))
    for p in range(4):
        r = red0[p + 3, PAD + 8 : PAD + 72, :128]
        b = bl0[p + 3, PAD + 8 : PAD + 72, :128]
        out[2 * p] = jnp.where(even64, r, b)
        out[2 * p + 1] = jnp.where(even64, b, r)


def from_both(up_value, down_value, axis):
    size = lax.axis_size(axis)
    up = [(i, i + 1) for i in range(size - 1)]
    return lax.ppermute(up_value, axis, up), lax.ppermute(down_value, axis, [(b, a) for a, b in up])


def from_both_round(up_value, down_value, axis):
    size = lax.axis_size(axis)
    up = [(i, (i + 1) % size) for i in range(size)]
    return lax.ppermute(up_value, axis, up), lax.ppermute(down_value, axis, [(b, a) for a, b in up])


def gathered(value, axis):
    copies = jnp.broadcast_to(value, (lax.axis_size(axis), *value.shape))
    return lax.all_to_all(copies, axis, split_axis=0, concat_axis=0, tiled=True)


def local(right_side, start):
    n = tuple(lax.axis_size(a) for a in ("gx", "gy", "gz"))
    block = (12, 64, 128)
    s, up, down = call(
        pack_kernel,
        [block, (6, 64, 128), (6, 64, 128)],
        [(8, 64, 128), (8, 64, 128), pltpu.SemaphoreType.DMA, pltpu.SemaphoreType.DMA],
        [pl.BlockSpec(memory_space=pltpu.HBM)] * 2,
    )(start, right_side)
    s_left, s_right = from_both_round(s, s, "gx")
    up, down = from_both(up, down, "gz")
    v, first, last = call(widen_kernel, [block, (12, EY, 256), (12, EY, 256)])(s, up, down)
    v_left, v_right = from_both_round(v, v, "gx")
    before, after = from_both(last, first, "gy")
    up, down = call(strips_kernel, [(6, 64, 256)] * 2)(before, after)
    y_left, y_right = from_both_round(up, down, "gx")
    up0 = (8, 80, 256)
    b1, black0, red_b0, black_b0 = call(
        functools.partial(fine_down_kernel, n),
        [(4, ROWS1, 128), up0, up0, up0],
        [(14, ROWS0 + 2 * PAD, 256)] * 2 + [(12, ROWS0, 256)] * 2 + [(3, ROWS0, 256), (8, ROWS0, 128)],
    )(s, v, before, after, s_left, s_right, v_left, v_right, y_left, y_right)
    b1 = gathered(b1, "gx").reshape(4 * n[0], ROWS1, 128)
    all1 = (2 * n[0], ROWS1, 128)
    colour1 = (2 * n[0] + 2, ROWS1 + 2 * PAD, 128)
    window1 = (8, ROWS1, 128)
    b2, black1, red_b1, black_b1 = call(
        functools.partial(middle_down_kernel, n),
        [(n[0], 16, 128), window1, window1, window1],
        [colour1, colour1, all1, all1, (ROWS1, 128), (2 * n[0], 40, 128)],
    )(b1)
    left, right = from_both(b2, b2, "gz")
    (b2,) = call(functools.partial(widen_coarse_kernel, n), [(2 * n[0], 16, 128)])(b2, left, right)
    b2 = gathered(b2, "gy").reshape(n[1], 2 * n[0], 16, 128)
    rows2, rows3 = 16 * n[1], 8 * n[1]
    p2, p3 = n[0], n[0] // 2
    colour2, colour3 = (p2 + 2, rows2 + 2 * PAD, 128), (p3 + 2, rows3 + 2 * PAD, 128)
    (out,) = call(
        functools.partial(up_kernel, n),
        [(8, 64, 128)],
        [
            (p2, rows2, 128), (p2, rows2, 128), colour2, colour2, (rows2, 128), (p2, rows2, 128),
            (p3, rows3, 128), (p3, rows3, 128), colour3, colour3, (rows3, 128), (p2, rows2, 128),
            window1, (10, ROWS1 + 2 * PAD, 128), (10, ROWS1 + 2 * PAD, 128), window1,
            (16, 80, 128), (10, 80 + 2 * PAD, 256), (10, 80 + 2 * PAD, 256), (3, 80, 256),
        ],
    )(b2, black1, red_b1, black_b1, black0, red_b0, black_b0)
    return out


def solution(mesh):
    in_specs = (P("gx", "gy", "gz"), P("gx", "gy", "gz"))
    out_specs = P("gx", "gy", "gz")
    return jax.shard_map(local, mesh=mesh, in_specs=in_specs, out_specs=out_specs, check_vma=False)
```

time: 653 us -> 90.1 us (0.14)
  the two profiles are of different devices: /device:TPU:96 before, /device:TPU:384 now
where the time goes in v2:
time: 90.1 us; the launch traced here: 89.7 us
  blocking collectives  31 us (34%)
  starting transfers between devices  26.8 us (30%)
  waiting for transfers between devices  18.5 us (21%)
  Pallas kernels  11.2 us (12%)
  local copies, waits for them, and re-layouts  2 us (2%)
    all_to_all x2, blocking collectives, gathered(): return lax.all_to_all(copies, axis, split_axis=0, concat_axis=0, tiled=True)  31 us
    ppermute x3, starting transfers between devices, from_both(): lax.ppermute(down_value, axis, [(b, a) for a, b in up])  10.8 us
    ppermute x3, starting transfers between devices, from_both(): lax.ppermute(up_value, axis, up)  8.26 us
    ppermute x3, starting transfers between devices, from_both_round(): lax.ppermute(down_value, axis, [(b, a) for a, b in up])  7.79 us
    ppermute x3, waiting for transfers between devices, from_both(): lax.ppermute(up_value, axis, up)  6.97 us
    ppermute x3, waiting for transfers between devices, from_both_round(): lax.ppermute(up_value, axis, up)  5.95 us
    pallas_call x1, Pallas kernels, local(): call(functools.partial(up_kernel, n), [(8, 64, 128)], [(p2, rows2, 128),...  5.88 us
    ppermute x3, waiting for transfers between devices, from_both(): lax.ppermute(down_value, axis, [(b, a) for a, b in up])  5.57 us
  transfers between devices with their start and end apart: 12, of which 7 were waited for; matrix products, arithmetic and copies ran while one was open for 0% of the time, Pallas kernels for 0%

profile of v2, /device:TPU:384, one launch (start us, length us, event | category | flops | bytes accessed | tf_op | source)
XLA Modules:
  0.0 89.7 jit_solution(7510017949667071192)
XLA Ops:
  0.0 0.0 copy-start
  0.0 0.9 %copy-done = f32[8,64,128]{2,1,0:T(8,128)S(1)} copy-done((f32[8,64,128]{2,1,0:T(8,128)S(1)}, f32[8,64,128]{2,1,0:T(8,128)}, u32[]{:S(2)}) %copy-start) | copy-done | bytes 262168
  1.0 0.0 copy-start.1
  1.0 0.9 %copy-done.1 = f32[8,64,128]{2,1,0:T(8,128)S(1)} copy-done((f32[8,64,128]{2,1,0:T(8,128)S(1)}, f32[8,64,128]{2,1,0:T(8,128)}, u32[]{:S(2)}) %copy-start.1) | copy-done | bytes 262168
  1.9 0.2 shard_map.28
  2.1 2.9 %collective-permute-start = (f32[6,64,128]{2,1,0:T(8,128)S(1)}, f32[6,64,128]{2,1,0:T(8,128)S(1)}, u32[]{:S(2)}, u32[]{:S(2)}) collective-permute-start(f32[6,64,128]{2,1,0:T(8,128)S(1)} %get-tuple-element.22), channel_id=1, source_target_pairs={{0,1},{1,2},{2,3},{3,4},{4,5},{5,6},{6,7},{7,8},{8,9},{9,10},{10,1... | collective-permute-start | bytes 589832 | tf_op jit(solution)/shard_map/ppermute | solution.py:397
  5.0 4.1 %collective-permute-start.1 = (f32[6,64,128]{2,1,0:T(8,128)S(1)}, f32[6,64,128]{2,1,0:T(8,128)S(1)}, u32[]{:S(2)}, u32[]{:S(2)}) collective-permute-start(f32[6,64,128]{2,1,0:T(8,128)S(1)} %get-tuple-element.23), channel_id=1, source_target_pairs={{1,0},{2,1},{3,2},{4,3},{5,4},{6,5},{7,6},{8,7},{9,8},{10,9},{11,1... | collective-permute-start | bytes 589832 | tf_op jit(solution)/shard_map/ppermute | solution.py:397
  9.2 1.9 %collective-permute-start.5 = (f32[12,64,128]{2,1,0:T(8,128)S(1)}, f32[12,64,128]{2,1,0:T(8,128)S(1)}, u32[]{:S(2)}, u32[]{:S(2)}) collective-permute-start(f32[12,64,128]{2,1,0:T(8,128)S(1)} %get-tuple-element.21.s), channel_id=1, source_target_pairs={{64,0},{128,64},{192,128},{256,192},{320,256},{384,320},{448,384},... | collective-permute-start | bytes 1179656 | tf_op jit(solution)/shard_map/ppermute | solution.py:403
  11.1 0.8 collective-permute-done.up
  11.8 1.4 %collective-permute-done.1.down = f32[6,64,128]{2,1,0:T(8,128)S(1)} collective-permute-done((f32[6,64,128]{2,1,0:T(8,128)S(1)}, f32[6,64,128]{2,1,0:T(8,128)S(1)}, u32[]{:S(2)}, u32[]{:S(2)}) %collective-permute-start.1) | collective-permute-done | bytes 196640 | tf_op jit(solution)/shard_map/ppermute | solution.py:397
  13.3 0.1 shard_map.29
  13.4 3.4 %collective-permute-start.2 = (f32[12,24,256]{2,1,0:T(8,128)S(1)}, f32[12,24,256]{2,1,0:T(8,128)S(1)}, u32[]{:S(2)}, u32[]{:S(2)}) collective-permute-start(f32[12,24,256]{2,1,0:T(8,128)S(1)} %get-tuple-element.25), channel_id=1, source_target_pairs={{0,16},{16,32},{32,48},{1,17},{17,33},{33,49},{2,18},{18,34},{34,5... | collective-permute-start | bytes 884744 | tf_op jit(solution)/shard_map/ppermute | solution.py:397
  16.8 1.3 %collective-permute-start.3 = (f32[12,24,256]{2,1,0:T(8,128)S(1)}, f32[12,24,256]{2,1,0:T(8,128)S(1)}, u32[]{:S(2)}, u32[]{:S(2)}) collective-permute-start(f32[12,24,256]{2,1,0:T(8,128)S(1)} %get-tuple-element.26), channel_id=1, source_target_pairs={{16,0},{32,16},{48,32},{17,1},{33,17},{49,33},{18,2},{34,18},{50,3... | collective-permute-start | bytes 884744 | tf_op jit(solution)/shard_map/ppermute | solution.py:397
  18.1 0.0 collective-permute-start.4
  18.2 2.9 %collective-permute-start.7 = (f32[12,64,128]{2,1,0:T(8,128)S(1)}, f32[12,64,128]{2,1,0:T(8,128)S(1)}, u32[]{:S(2)}, u32[]{:S(2)}) collective-permute-start(f32[12,64,128]{2,1,0:T(8,128)S(1)} %get-tuple-element.24.v), channel_id=1, source_target_pairs={{64,0},{128,64},{192,128},{256,192},{320,256},{384,320},{448,384},... | collective-permute-start | bytes 1179656 | tf_op jit(solution)/shard_map/ppermute | solution.py:403
  21.1 0.8 collective-permute-done.2.before
  21.9 0.0 collective-permute-start.6
  21.9 4.1 %collective-permute-done.3.after = f32[12,24,256]{2,1,0:T(8,128)S(1)} collective-permute-done((f32[12,24,256]{2,1,0:T(8,128)S(1)}, f32[12,24,256]{2,1,0:T(8,128)S(1)}, u32[]{:S(2)}, u32[]{:S(2)}) %collective-permute-start.3) | collective-permute-done | bytes 294944 | tf_op jit(solution)/shard_map/ppermute | solution.py:397
  26.0 0.1 shard_map.30
  26.1 0.0 collective-permute-start.8
  26.1 0.0 collective-permute-done.5.s_right
  26.1 2.9 %collective-permute-start.9 = (f32[6,64,256]{2,1,0:T(8,128)S(1)}, f32[6,64,256]{2,1,0:T(8,128)S(1)}, u32[]{:S(2)}, u32[]{:S(2)}) collective-permute-start(f32[6,64,256]{2,1,0:T(8,128)S(1)} %get-tuple-element.28), channel_id=1, source_target_pairs={{64,0},{128,64},{192,128},{256,192},{320,256},{384,320},{448,384},... | collective-permute-start | bytes 1179656 | tf_op jit(solution)/shard_map/ppermute | solution.py:403
  29.0 0.0 collective-permute-done.4.s_left
  29.0 0.0 collective-permute-done.7.v_right
  29.0 1.7 %collective-permute-done.6.v_left = f32[12,64,128]{2,1,0:T(8,128)S(1)} collective-permute-done((f32[12,64,128]{2,1,0:T(8,128)S(1)}, f32[12,64,128]{2,1,0:T(8,128)S(1)}, u32[]{:S(2)}, u32[]{:S(2)}) %collective-permute-start.6) | collective-permute-done | bytes 393248 | tf_op jit(solution)/shard_map/ppermute | solution.py:403
  30.8 4.2 %collective-permute-done.8.y_left = f32[6,64,256]{2,1,0:T(8,128)S(1)} collective-permute-done((f32[6,64,256]{2,1,0:T(8,128)S(1)}, f32[6,64,256]{2,1,0:T(8,128)S(1)}, u32[]{:S(2)}, u32[]{:S(2)}) %collective-permute-start.8) | collective-permute-done | bytes 393248 | tf_op jit(solution)/shard_map/ppermute | solution.py:403
  35.0 0.0 collective-permute-done.9.y_right
  35.0 3.4 %shard_map.31 = (f32[4,56,128]{2,1,0:T(8,128)S(1)}, f32[8,80,256]{2,1,0:T(8,128)S(1)}, f32[8,80,256]{2,1,0:T(8,128)S(1)}, f32[8,80,256]{2,1,0:T(8,128)S(1)}) custom-call(f32[12,64,128]{2,1,0:T(8,128)S(1)} %get-tuple-element.21.s, f32[12,64,128]{2,1,0:T(8,128)S(1)} %get-tuple-element.24.v, f32[12,24,256]{2,1,0:T(8,128)S(1)} %collective-permute-done.2.before, ...), custom_call_target="tpu_custom_call" | custom-call | tf_op jit(solution)/shard_map/pallas_call | solution.py:428
  38.4 0.1 broadcast_in_dim.6
  38.5 18.2 %all_to_all.10 = f32[8,4,56,128]{3,2,1,0:T(8,128)S(1)} all-to-all(f32[8,4,56,128]{3,2,1,0:T(8,128)S(1)} %broadcast_in_dim.6), channel_id=1, replica_groups=mesh['gx'=8,'gy'=4,'gz'=16] {'gx'}, dimensions={0} | all-to-all | bytes 1835008 | tf_op jit(solution)/shard_map/all_to_all | solution.py:408
  56.7 1.4 %shard_map.32 = (f32[8,16,128]{2,1,0:T(8,128)S(1)}, f32[8,56,128]{2,1,0:T(8,128)S(1)}, f32[8,56,128]{2,1,0:T(8,128)S(1)}, f32[8,56,128]{2,1,0:T(8,128)S(1)}) custom-call(f32[32,56,128]{2,1,0:T(8,128)S(1)} %bitcast.1), custom_call_target="tpu_custom_call" | custom-call | tf_op jit(solution)/shard_map/pallas_call | solution.py:437
  58.1 5.3 %collective-permute-start.11 = (f32[8,16,128]{2,1,0:T(8,128)S(1)}, f32[8,16,128]{2,1,0:T(8,128)S(1)}, u32[]{:S(2)}, u32[]{:S(2)}) collective-permute-start(f32[8,16,128]{2,1,0:T(8,128)S(1)} %get-tuple-element.30.own), channel_id=1, source_target_pairs={{1,0},{2,1},{3,2},{4,3},{5,4},{6,5},{7,6},{8,7},{9,8},{10,9},{11,1... | collective-permute-start | bytes 196616 | tf_op jit(solution)/shard_map/ppermute | solution.py:397
  63.4 1.9 %collective-permute-start.10 = (f32[8,16,128]{2,1,0:T(8,128)S(1)}, f32[8,16,128]{2,1,0:T(8,128)S(1)}, u32[]{:S(2)}, u32[]{:S(2)}) collective-permute-start(f32[8,16,128]{2,1,0:T(8,128)S(1)} %get-tuple-element.30.own), channel_id=1, source_target_pairs={{0,1},{1,2},{2,3},{3,4},{4,5},{5,6},{6,7},{7,8},{8,9},{9,10},{10,1... | collective-permute-start | bytes 196616 | tf_op jit(solution)/shard_map/ppermute | solution.py:397
  65.4 0.0 collective-permute-done.11.right
  65.4 5.4 %collective-permute-done.10.left = f32[8,16,128]{2,1,0:T(8,128)S(1)} collective-permute-done((f32[8,16,128]{2,1,0:T(8,128)S(1)}, f32[8,16,128]{2,1,0:T(8,128)S(1)}, u32[]{:S(2)}, u32[]{:S(2)}) %collective-permute-start.10) | collective-permute-done | bytes 65568 | tf_op jit(solution)/shard_map/ppermute | solution.py:397
  70.8 0.1 shard_map.33
  71.0 12.8 %all_to_all.11.b2 = f32[4,16,16,128]{3,2,1,0:T(8,128)S(1)} all-to-all(f32[4,16,16,128]{3,2,1,0:T(8,128)S(1)} %broadcast_in_dim.7), channel_id=1, replica_groups=mesh['gx'=8,'gy'=4,'gz'=16] {'gy'}, dimensions={0} | all-to-all | bytes 1048576 | tf_op jit(solution)/shard_map/all_to_all | solution.py:408
  83.8 5.9 %shard_map.34 = f32[8,64,128]{2,1,0:T(8,128)} custom-call(f32[4,16,16,128]{3,2,1,0:T(8,128)S(1)} %all_to_all.11.b2, f32[8,56,128]{2,1,0:T(8,128)S(1)} %get-tuple-element.31.black1, f32[8,56,128]{2,1,0:T(8,128)S(1)} %get-tuple-element.32.red_b1, f32[8,56,128]{2,1,0:T(8,128)S(1)} %get-tuple-element.33.black_b1, f32[8,80,256]{2,1,0:T(8,128)S(1)} %get-tuple-element.34.black0, ...), custom_call_target="tpu_custom_call" | custom-call | tf_op jit(solution)/shard_map/pallas_call | solution.py:448
  (1 shorter events, 0.0 us)
Async XLA Ops:
  0.0 0.9 %copy-start = (f32[8,64,128]{2,1,0:T(8,128)S(1)}, f32[8,64,128]{2,1,0:T(8,128)}, u32[]{:S(2)}) copy-start(f32[8,64,128]{2,1,0:T(8,128)} %start_hbm.1) | copy-start | bytes 786436
  1.0 0.9 %copy-start.1 = (f32[8,64,128]{2,1,0:T(8,128)S(1)}, f32[8,64,128]{2,1,0:T(8,128)}, u32[]{:S(2)}) copy-start(f32[8,64,128]{2,1,0:T(8,128)} %right_hbm.1) | copy-start | bytes 786436
  2.1 9.7 %collective-permute-start = (f32[6,64,128]{2,1,0:T(8,128)S(1)}, f32[6,64,128]{2,1,0:T(8,128)S(1)}, u32[]{:S(2)}, u32[]{:S(2)}) collective-permute-start(f32[6,64,128]{2,1,0:T(8,128)S(1)} %get-tuple-element.22), channel_id=1, source_target_pairs={{0,1},{1,2},{2,3},{3,4},{4,5},{5,6},{6,7},{7,8},{8,9},{9,10},{10,1... | collective-permute-start | bytes 589832 | tf_op jit(solution)/shard_map/ppermute | solution.py:397
  5.0 8.3 %collective-permute-start.1 = (f32[6,64,128]{2,1,0:T(8,128)S(1)}, f32[6,64,128]{2,1,0:T(8,128)S(1)}, u32[]{:S(2)}, u32[]{:S(2)}) collective-permute-start(f32[6,64,128]{2,1,0:T(8,128)S(1)} %get-tuple-element.23), channel_id=1, source_target_pairs={{1,0},{2,1},{3,2},{4,3},{5,4},{6,5},{7,6},{8,7},{9,8},{10,9},{11,1... | collective-permute-start | bytes 589832 | tf_op jit(solution)/shard_map/ppermute | solution.py:397
  9.2 16.9 %collective-permute-start.5 = (f32[12,64,128]{2,1,0:T(8,128)S(1)}, f32[12,64,128]{2,1,0:T(8,128)S(1)}, u32[]{:S(2)}, u32[]{:S(2)}) collective-permute-start(f32[12,64,128]{2,1,0:T(8,128)S(1)} %get-tuple-element.21.s), channel_id=1, source_target_pairs={{64,0},{128,64},{192,128},{256,192},{320,256},{384,320},{448,384},... | collective-permute-start | bytes 1179656 | tf_op jit(solution)/shard_map/ppermute | solution.py:403
  13.4 8.5 %collective-permute-start.2 = (f32[12,24,256]{2,1,0:T(8,128)S(1)}, f32[12,24,256]{2,1,0:T(8,128)S(1)}, u32[]{:S(2)}, u32[]{:S(2)}) collective-permute-start(f32[12,24,256]{2,1,0:T(8,128)S(1)} %get-tuple-element.25), channel_id=1, source_target_pairs={{0,16},{16,32},{32,48},{1,17},{17,33},{33,49},{2,18},{18,34},{34,5... | collective-permute-start | bytes 884744 | tf_op jit(solution)/shard_map/ppermute | solution.py:397
  16.8 9.2 %collective-permute-start.3 = (f32[12,24,256]{2,1,0:T(8,128)S(1)}, f32[12,24,256]{2,1,0:T(8,128)S(1)}, u32[]{:S(2)}, u32[]{:S(2)}) collective-permute-start(f32[12,24,256]{2,1,0:T(8,128)S(1)} %get-tuple-element.26), channel_id=1, source_target_pairs={{16,0},{32,16},{48,32},{17,1},{33,17},{49,33},{18,2},{34,18},{50,3... | collective-permute-start | bytes 884744 | tf_op jit(solution)/shard_map/ppermute | solution.py:397
  18.1 10.9 %collective-permute-start.4 = (f32[12,64,128]{2,1,0:T(8,128)S(1)}, f32[12,64,128]{2,1,0:T(8,128)S(1)}, u32[]{:S(2)}, u32[]{:S(2)}) collective-permute-start(f32[12,64,128]{2,1,0:T(8,128)S(1)} %get-tuple-element.21.s), channel_id=1, source_target_pairs={{0,64},{64,128},{128,192},{192,256},{256,320},{320,384},{384,448},... | collective-permute-start | bytes 1179656 | tf_op jit(solution)/shard_map/ppermute | solution.py:403
  18.2 10.9 %collective-permute-start.7 = (f32[12,64,128]{2,1,0:T(8,128)S(1)}, f32[12,64,128]{2,1,0:T(8,128)S(1)}, u32[]{:S(2)}, u32[]{:S(2)}) collective-permute-start(f32[12,64,128]{2,1,0:T(8,128)S(1)} %get-tuple-element.24.v), channel_id=1, source_target_pairs={{64,0},{128,64},{192,128},{256,192},{320,256},{384,320},{448,384},... | collective-permute-start | bytes 1179656 | tf_op jit(solution)/shard_map/ppermute | solution.py:403
  21.9 8.9 %collective-permute-start.6 = (f32[12,64,128]{2,1,0:T(8,128)S(1)}, f32[12,64,128]{2,1,0:T(8,128)S(1)}, u32[]{:S(2)}, u32[]{:S(2)}) collective-permute-start(f32[12,64,128]{2,1,0:T(8,128)S(1)} %get-tuple-element.24.v), channel_id=1, source_target_pairs={{0,64},{64,128},{128,192},{192,256},{256,320},{320,384},{384,448},... | collective-permute-start | bytes 1179656 | tf_op jit(solution)/shard_map/ppermute | solution.py:403
  26.1 8.9 %collective-permute-start.8 = (f32[6,64,256]{2,1,0:T(8,128)S(1)}, f32[6,64,256]{2,1,0:T(8,128)S(1)}, u32[]{:S(2)}, u32[]{:S(2)}) collective-permute-start(f32[6,64,256]{2,1,0:T(8,128)S(1)} %get-tuple-element.27), channel_id=1, source_target_pairs={{0,64},{64,128},{128,192},{192,256},{256,320},{320,384},{384,448},... | collective-permute-start | bytes 1179656 | tf_op jit(solution)/shard_map/ppermute | solution.py:403
  26.1 8.9 %collective-permute-start.9 = (f32[6,64,256]{2,1,0:T(8,128)S(1)}, f32[6,64,256]{2,1,0:T(8,128)S(1)}, u32[]{:S(2)}, u32[]{:S(2)}) collective-permute-start(f32[6,64,256]{2,1,0:T(8,128)S(1)} %get-tuple-element.28), channel_id=1, source_target_pairs={{64,0},{128,64},{192,128},{256,192},{320,256},{384,320},{448,384},... | collective-permute-start | bytes 1179656 | tf_op jit(solution)/shard_map/ppermute | solution.py:403
  58.1 7.3 %collective-permute-start.11 = (f32[8,16,128]{2,1,0:T(8,128)S(1)}, f32[8,16,128]{2,1,0:T(8,128)S(1)}, u32[]{:S(2)}, u32[]{:S(2)}) collective-permute-start(f32[8,16,128]{2,1,0:T(8,128)S(1)} %get-tuple-element.30.own), channel_id=1, source_target_pairs={{1,0},{2,1},{3,2},{4,3},{5,4},{6,5},{7,6},{8,7},{9,8},{10,9},{11,1... | collective-permute-start | bytes 196616 | tf_op jit(solution)/shard_map/ppermute | solution.py:397
  63.4 7.4 %collective-permute-start.10 = (f32[8,16,128]{2,1,0:T(8,128)S(1)}, f32[8,16,128]{2,1,0:T(8,128)S(1)}, u32[]{:S(2)}, u32[]{:S(2)}) collective-permute-start(f32[8,16,128]{2,1,0:T(8,128)S(1)} %get-tuple-element.30.own), channel_id=1, source_target_pairs={{0,1},{1,2},{2,3},{3,4},{4,5},{5,6},{6,7},{7,8},{8,9},{9,10},{10,1... | collective-permute-start | bytes 196616 | tf_op jit(solution)/shard_map/ppermute | solution.py:397

commit v3 on v2

--- a/solution.py
+++ b/solution.py
@@ -13,6 +13,7 @@
 EY = 24
 ROWS0 = 64 + 2 * EY
 ROWS1 = ROWS0 // 2
+SENT1 = ROWS1 - 8
 PAD = 8
 UP0 = EY - 8
 VMEM_LIMIT = 40 * 1024 * 1024
@@ -118,16 +119,17 @@
         down[p] = jnp.where(low, a, b)
 
 
-def widen_kernel(s, up, down, v, first, last):
+def widen_kernel(s, up, down, sv, first, last):
     low = lane_of((64, 128)) < 64
     for p in range(6):
-        v[p] = jnp.where(low, down[p], up[p])
-        v[p + 6] = pltpu.roll(jnp.where(low, up[p], down[p]), 64, 1)
+        sv[p + 12] = jnp.where(low, down[p], up[p])
+        sv[p + 18] = pltpu.roll(jnp.where(low, up[p], down[p]), 64, 1)
     for p in range(12):
+        sv[p] = s[p]
         first[p, :, :128] = s[p, :EY]
-        first[p, :, 128:] = v[p, :EY]
+        first[p, :, 128:] = sv[p + 12, :EY]
         last[p, :, :128] = s[p, 64 - EY :]
-        last[p, :, 128:] = v[p, 64 - EY :]
+        last[p, :, 128:] = sv[p + 12, 64 - EY :]
 
 
 def strips_kernel(before, after, up, down):
@@ -142,8 +144,8 @@
 
 
 def fine_down_kernel(
-    n, s, v, before, after, s_left, s_right, v_left, v_right, y_left, y_right,
-    coarse, black_out, red_b_out, black_b_out, red, black, rb, bb, weight, pairs,
+    n, s, before, after, s_left, s_right, y_left, y_right,
+    coarse, sent, black_out, red_b_out, black_b_out, red, black, rb, bb, weight, pairs,
 ):
     gx, gy, gz = (lax.axis_index(a) for a in ("gx", "gy", "gz"))
     inner = domain((ROWS0, 256), 64 * gy - EY, 64 * n[1], 128 * gz, 128 * n[2], 192)
@@ -166,9 +168,9 @@
 
         for p in range(4):
             j = 4 * a + p
-            for base, centre, strip, there in ((4, s, v, None), (0, s_left, v_left, has_left), (8, s_right, v_right, has_right)):
-                put(base + p, mid, centre[j], (there, slice(0, 128)))
-                put(base + p, mid, strip[j], (there, slice(128, 256)))
+            for base, whole, there in ((4, s, None), (0, s_left, has_left), (8, s_right, has_right)):
+                put(base + p, mid, whole[j], (there, slice(0, 128)))
+                put(base + p, mid, whole[j + 12], (there, slice(128, 256)))
             put(4 + p, top, before[j], (None, None))
             put(4 + p, end, after[j], (None, None))
         for q in range(2):
@@ -202,24 +204,39 @@
     result = dot(jnp.concatenate(rows, axis=0), table(256, 128, lambda k, c: (k >> 1) == c, 0.5))
     for p in range(4):
         coarse[p] = result[p * ROWS1 : (p + 1) * ROWS1]
+        sent[p] = coarse[p, 4 : 4 + SENT1]
     for p in range(8):
         black_out[p] = black[p + 3, PAD + UP0 : PAD + UP0 + 80]
         red_b_out[p] = rb[p + 2, UP0 : UP0 + 80]
         black_b_out[p] = bb[p + 2, UP0 : UP0 + 80]
 
 
-def middle_down_kernel(n, b1, coarse, black_out, red_b_out, black_b_out, red, black, rb, bb, weight, pairs):
+def middle_down_kernel(
+    n, own, same, other, coarse, black_out, red_b_out, black_b_out, red, black, rb, bb, weight, pairs
+):
     gx, gy, gz = (lax.axis_index(a) for a in ("gx", "gy", "gz"))
     count = 2 * n[0]
+    core = gx % 2
     even = even_mask((ROWS1, 128))
+    even_sent = even_mask((SENT1, 128))
     weight[...] = domain((ROWS1, 128), 32 * gy - EY // 2, 32 * n[1], 64 * gz, 64 * n[2], 96)
     clear_pads(red, black)
+    zero4 = jnp.zeros((4, 128), F32)
     for i in range(count):
-        a, b = b1[2 * i], b1[2 * i + 1]
-        r = jnp.where(even, a, b)
-        rb[i] = r
-        bb[i] = jnp.where(even, b, a)
-        red[i + 1, PAD : PAD + ROWS1] = r * weight[...]
+        block, q = i // 2, 2 * (i % 2)
+        mine = core == block % 2
+        a = jnp.where(mine, same[block // 2, q], other[block // 2, q])
+        b = jnp.where(mine, same[block // 2, q + 1], other[block // 2, q + 1])
+        for ref, v in ((rb, jnp.where(even_sent, a, b)), (bb, jnp.where(even_sent, b, a))):
+            ref[i, :4] = zero4
+            ref[i, 4 : 4 + SENT1] = v
+            ref[i, 4 + SENT1 :] = zero4
+    for h in range(2):
+        a, b = own[2 * h], own[2 * h + 1]
+        rb[2 * gx + h] = jnp.where(even, a, b)
+        bb[2 * gx + h] = jnp.where(even, b, a)
+    for i in range(count):
+        red[i + 1, PAD : PAD + ROWS1] = rb[i] * weight[...]
 
     def weights(i, r, step):
         return weight[r : r + step]
@@ -239,65 +256,102 @@
     for i in every:
         pairs[i] = residual_sum(red, black, rb, bb, i, top, 40, even40)
     sums = [pairs[i, pl.ds(4, 16, stride=2), :] + pairs[i, pl.ds(5, 16, stride=2), :] for i in every]
+    to2 = lambda k: jnp.where(k < 96, (k >> 1) + 16, (k >> 1) - 48)
     low = jnp.concatenate(sums[: n[0]], axis=0)
     high = jnp.concatenate(sums[n[0] :], axis=0)
-    result = dot(jnp.concatenate([low, high], axis=1), table(256, 128, lambda k, c: (k >> 1) == c, 0.5))
+    take = table(256, 128, lambda k, c: to2(k & 127) + (k & 128) // 2 == c, 0.5)
+    result = dot(jnp.concatenate([low, high], axis=1), take)
     for i in range(n[0]):
         coarse[i] = result[16 * i : 16 * i + 16]
 
 
-def widen_coarse_kernel(n, own, left, right, wide):
-    lanes = lane_of((16, 128))
-    for i in range(n[0]):
-        w, a, b = own[i], left[i], right[i]
-        a32, a96, b32, b96 = pltpu.roll(a, 32, 1), pltpu.roll(a, 96, 1), pltpu.roll(b, 32, 1), pltpu.roll(b, 96, 1)
-        for k, x, y, z0, z1 in ((i, w, b32, a32, a96), (i + n[0], pltpu.roll(w, 64, 1), b96, a96, a32)):
-            wide[k] = jnp.where(lanes < 32, x, jnp.where(lanes < 80, y, jnp.where(lanes < 96, z0, z1)))
+def wrap_pairs(ref, rows):
+    last = ref.shape[0] - 2
+    low = lane_of((rows, 128)) < 64
+    ref[0, PAD : PAD + rows] = jnp.where(low, 0.0, pltpu.roll(ref[last, PAD : PAD + rows], 64, 1))
+    ref[last + 1, PAD : PAD + rows] = jnp.where(low, pltpu.roll(ref[1, PAD : PAD + rows], 64, 1), 0.0)
+
+
+def domain2(n, gz, rows):
+    y = lane_of((rows, 128))
+    z = (y & 63) - 16 + 32 * gz
+    return jnp.where((z >= 0) & (z < 32 * n[2]), F32(SIXTH), F32(0.0))
+
+
+def third_place(n, i):
+    packed = n[0] // 2
+    arrays = max(1, packed // 2)
+    p = i % packed
+    return p % arrays, 64 * (i // packed) + 32 * (p // arrays)
+
+
+def coarse_down_kernel(n, b2, coarse, black_out, rb, bb, red, black, weight, pairs):
+    gz = lax.axis_index("gz")
+    rows, packed = 16 * n[1], n[0] // 2
+    weight[...] = domain2(n, gz, rows)
+    clear_pads(red, black)
+    even16 = even_mask((16, 128))
+    for i in range(packed):
+        for g in range(n[1]):
+            a, b = b2[g, 2 * i], b2[g, 2 * i + 1]
+            at = 16 * g
+            r = jnp.where(even16, a, b)
+            rb[i, at : at + 16] = r
+            bb[i, at : at + 16] = jnp.where(even16, b, a)
+            red[i + 1, PAD + at : PAD + at + 16] = r * weight[at : at + 16]
+
+    def weights(i, r, step):
+        return weight[r : r + step]
+
+    every = range(packed)
+    wrap_pairs(red, rows)
+    half(black, red, bb, weights, False, every, rows, rows)
+    wrap_pairs(black, rows)
+    half(red, black, rb, weights, True, every, rows, rows)
+    wrap_pairs(red, rows)
+    half(black, red, bb, weights, False, every, rows, rows)
+    wrap_pairs(black, rows)
+    even = even_mask((rows, 128))
+    for i in every:
+        pairs[i] = residual_sum(red, black, rb, bb, i, 0, rows, even)
+        black_out[i] = black[i + 1, PAD : PAD + rows]
+    rows3 = rows // 2
+    sums = [pairs[i, pl.ds(0, rows3, stride=2), :] + pairs[i, pl.ds(1, rows3, stride=2), :] for i in every]
+    take = table(128, 128, lambda k, c: ((k & 63) >> 1) + (k & 64) == c, 0.5)
+    result = dot(jnp.concatenate(sums, axis=0), take)
+    arrays = coarse.shape[0]
+    for r in range(arrays):
+        total = result[r * rows3 : (r + 1) * rows3]
+        if packed > arrays:
+            total = total + pltpu.roll(result[(r + arrays) * rows3 : (r + arrays + 1) * rows3], 32, 1)
+        coarse[r] = total
 
 
 def up_kernel(
-    n, b2, black1, red_b1, black_b1, black0, red_b0, black_b0, out,
-    rb2, bb2, red2, black2, weight2, pairs2,
+    n, b3, b3_left, b3_right, start2, rb2, bb2, black1, red_b1, black_b1, black0, red_b0, black_b0, out,
+    red2, black2, weight2,
     rb3, bb3, red3, black3, weight3, add2,
     add1, red1, bl1, weight1,
     add0, red0, bl0, weight0,
 ):
     gx, gy, gz = (lax.axis_index(a) for a in ("gx", "gy", "gz"))
     rows2, rows3 = 16 * n[1], 8 * n[1]
-    pairs_2, pairs_3 = n[0], n[0] // 2
-
-    weight2[...] = domain((rows2, 128), 0, rows2, 32 * gz, 32 * n[2], 80)
-    clear_pads(red2, black2)
-    even16 = even_mask((16, 128))
-    for i in range(pairs_2):
-        for g in range(n[1]):
-            a, b = b2[g, 2 * i], b2[g, 2 * i + 1]
-            at = 16 * g
-            r = jnp.where(even16, a, b)
-            rb2[i, at : at + 16] = r
-            bb2[i, at : at + 16] = jnp.where(even16, b, a)
-            red2[i + 1, PAD + at : PAD + at + 16] = r * weight2[at : at + 16]
-
-    def weights2(i, r, step):
-        return weight2[r : r + step]
-
-    every2 = range(pairs_2)
-    half(black2, red2, bb2, weights2, False, every2, rows2, rows2)
-    half(red2, black2, rb2, weights2, True, every2, rows2, rows2)
-    half(black2, red2, bb2, weights2, False, every2, rows2, rows2)
-    even2 = even_mask((rows2, 128))
-    for i in every2:
-        pairs2[i] = residual_sum(red2, black2, rb2, bb2, i, 0, rows2, even2)
-    sums = [pairs2[i, pl.ds(0, rows3, stride=2), :] + pairs2[i, pl.ds(1, rows3, stride=2), :] for i in every2]
-    to3 = lambda k, c: jnp.where(k < 80, k >> 1, (k >> 1) + 64) == c
-    b3 = dot(jnp.concatenate(sums, axis=0), table(128, 128, to3, 0.5))
-
-    even3 = even_mask((rows3, 128))
-    weight3[...] = domain((rows3, 128), 0, rows3, 16 * gz, 16 * n[2], 64, (40, 104))
+    packed, pairs_3 = n[0] // 2, n[0] // 2
+
+    shape3 = (rows3, 128)
+    even3 = even_mask(shape3)
+    lane3 = lane_of(shape3)
+    z3 = lane3 - 24 + 16 * gz
+    weight3[...] = jnp.where((z3 >= 0) & (z3 < 16 * n[2]) & (lane3 < 64), F32(SIXTH), F32(0.0))
     clear_pads(red3, black3)
+
+    def plane3(i):
+        at, lane = third_place(n, i)
+        own, left, right = (pltpu.roll(ref[at], (to - lane) % 128, 1) if (to - lane) % 128 else ref[at] for ref, to in ((b3, 16), (b3_left, 0), (b3_right, 32)))
+        return jnp.where(lane3 < 24, left, jnp.where(lane3 < 40, own, right))
+
     for i in range(pairs_3):
-        a = b3[2 * i * rows3 : (2 * i + 1) * rows3]
-        b = b3[(2 * i + 1) * rows3 : (2 * i + 2) * rows3]
+        a, b = plane3(2 * i), plane3(2 * i + 1)
         r = jnp.where(even3, a, b)
         rb3[i] = r
         bb3[i] = jnp.where(even3, b, a)
@@ -319,24 +373,41 @@
     for i in every3:
         r, b = red3[i + 1, PAD : PAD + rows3], black3[i + 1, PAD : PAD + rows3]
         planes += [jnp.where(even3, r, b), jnp.where(even3, b, r)]
-    wide = dot(jnp.concatenate(planes, axis=0), table(128, 128, lambda k, c: to3(c, k)))
+
+    halves = [jnp.concatenate(planes[:packed], axis=0), jnp.concatenate(planes[packed:], axis=0)]
+    spread = table(256, 128, lambda k, c: ((c & 63) >> 1) + 16 + 2 * (c & 64) == k)
+    wide = dot(jnp.concatenate(halves, axis=1), spread)
+    weight2[...] = domain2(n, gz, rows2)
+    clear_pads(red2, black2)
+    every2 = range(packed)
     for i in every2:
         w = wide[i * rows3 : (i + 1) * rows3]
         add2[i, pl.ds(0, rows3, stride=2), :] = w
         add2[i, pl.ds(1, rows3, stride=2), :] = w
-        black2[i + 1, PAD : PAD + rows2] = black2[i + 1, PAD : PAD + rows2] + add2[i]
+        black2[i + 1, PAD : PAD + rows2] = start2[i] + add2[i]
+
+    def weights2(i, r, step):
+        return weight2[r : r + step]
+
     for _ in range(2):
+        wrap_pairs(black2, rows2)
         half(red2, black2, rb2, weights2, True, every2, rows2, rows2)
+        wrap_pairs(red2, rows2)
         half(black2, red2, bb2, weights2, False, every2, rows2, rows2)
 
     even32 = even_mask((32, 128))
     top = pl.multiple_of(16 * gy, 8)
     planes = []
+    second = lane_of((32, 128)) >= 64
     for i in range(8):
-        q = jnp.clip(gx - 1 + (i + 1) // 2, 0, n[0] + 1)
-        r, b = red2[q, pl.ds(top, 32), :], black2[q, pl.ds(top, 32), :]
-        planes.append(jnp.where(even32, r, b) if i % 2 == 1 else jnp.where(even32, b, r))
-    to2 = lambda k, c: jnp.where(c < 96, c >> 1, (c >> 1) + 64) == k
+        q = gx - 2 + (i + 1) // 2
+        there = (q >= 0) & (q < n[0])
+        upper = q >= packed
+        at = jnp.clip(jnp.where(upper, q - packed, q), 0, packed - 1) + 1
+        r, b = red2[at, pl.ds(top, 32), :], black2[at, pl.ds(top, 32), :]
+        plane = jnp.where(even32, r, b) if i % 2 == 1 else jnp.where(even32, b, r)
+        planes.append(jnp.where(there & (second == upper), plane, 0.0))
+    to2 = lambda k, c: jnp.where(c < 96, (c >> 1) + 16, (c >> 1) - 48) == (k & 63)
     wide = dot(jnp.concatenate(planes, axis=0), table(128, 128, to2))
     inner = domain((ROWS1, 128), 32 * gy - EY // 2, 32 * n[1], 64 * gz, 64 * n[2], 96)
     clear_pads(red1, bl1)
@@ -403,58 +474,64 @@
     return lax.ppermute(up_value, axis, up), lax.ppermute(down_value, axis, [(b, a) for a, b in up])
 
 
-def gathered(value, axis):
-    copies = jnp.broadcast_to(value, (lax.axis_size(axis), *value.shape))
-    return lax.all_to_all(copies, axis, split_axis=0, concat_axis=0, tiled=True)
+def gathered(value, axis, groups=None):
+    size = lax.axis_size(axis) if groups is None else len(groups[0])
+    copies = jnp.broadcast_to(value, (size, *value.shape))
+    return lax.all_to_all(copies, axis, split_axis=0, concat_axis=0, axis_index_groups=groups, tiled=True)
 
 
 def local(right_side, start):
     n = tuple(lax.axis_size(a) for a in ("gx", "gy", "gz"))
-    block = (12, 64, 128)
     s, up, down = call(
         pack_kernel,
-        [block, (6, 64, 128), (6, 64, 128)],
+        [(12, 64, 128), (6, 64, 128), (6, 64, 128)],
         [(8, 64, 128), (8, 64, 128), pltpu.SemaphoreType.DMA, pltpu.SemaphoreType.DMA],
         [pl.BlockSpec(memory_space=pltpu.HBM)] * 2,
     )(start, right_side)
-    s_left, s_right = from_both_round(s, s, "gx")
     up, down = from_both(up, down, "gz")
-    v, first, last = call(widen_kernel, [block, (12, EY, 256), (12, EY, 256)])(s, up, down)
-    v_left, v_right = from_both_round(v, v, "gx")
+    sv, first, last = call(widen_kernel, [(24, 64, 128), (12, EY, 256), (12, EY, 256)])(s, up, down)
+    s_left, s_right = from_both_round(sv, sv, "gx")
     before, after = from_both(last, first, "gy")
     up, down = call(strips_kernel, [(6, 64, 256)] * 2)(before, after)
     y_left, y_right = from_both_round(up, down, "gx")
     up0 = (8, 80, 256)
-    b1, black0, red_b0, black_b0 = call(
+    b1, sent, black0, red_b0, black_b0 = call(
         functools.partial(fine_down_kernel, n),
-        [(4, ROWS1, 128), up0, up0, up0],
+        [(4, ROWS1, 128), (4, SENT1, 128), up0, up0, up0],
         [(14, ROWS0 + 2 * PAD, 256)] * 2 + [(12, ROWS0, 256)] * 2 + [(3, ROWS0, 256), (8, ROWS0, 128)],
-    )(s, v, before, after, s_left, s_right, v_left, v_right, y_left, y_right)
-    b1 = gathered(b1, "gx").reshape(4 * n[0], ROWS1, 128)
+    )(sv, before, after, s_left, s_right, y_left, y_right)
+    groups = [[2 * chip + core for chip in range(n[0] // 2)] for core in range(2)]
+    same = gathered(sent[None], "gx", groups)
+    other = lax.ppermute(same, "gx", [(i, i ^ 1) for i in range(n[0])])
     all1 = (2 * n[0], ROWS1, 128)
     colour1 = (2 * n[0] + 2, ROWS1 + 2 * PAD, 128)
     window1 = (8, ROWS1, 128)
+    blocks = (n[0] // 2, 4, SENT1, 128)
     b2, black1, red_b1, black_b1 = call(
         functools.partial(middle_down_kernel, n),
         [(n[0], 16, 128), window1, window1, window1],
         [colour1, colour1, all1, all1, (ROWS1, 128), (2 * n[0], 40, 128)],
-    )(b1)
-    left, right = from_both(b2, b2, "gz")
-    (b2,) = call(functools.partial(widen_coarse_kernel, n), [(2 * n[0], 16, 128)])(b2, left, right)
-    b2 = gathered(b2, "gy").reshape(n[1], 2 * n[0], 16, 128)
+    )(b1, same.reshape(blocks), other.reshape(blocks))
+    b2 = gathered(b2, "gy").reshape(n[1], n[0], 16, 128)
     rows2, rows3 = 16 * n[1], 8 * n[1]
-    p2, p3 = n[0], n[0] // 2
-    colour2, colour3 = (p2 + 2, rows2 + 2 * PAD, 128), (p3 + 2, rows3 + 2 * PAD, 128)
+    packed = n[0] // 2
+    all2, colour2, colour3 = (packed, rows2, 128), (packed + 2, rows2 + 2 * PAD, 128), (packed + 2, rows3 + 2 * PAD, 128)
+    b3, black2, red_b2, black_b2 = call(
+        functools.partial(coarse_down_kernel, n),
+        [(max(1, packed // 2), rows3, 128), all2, all2, all2],
+        [colour2, colour2, (rows2, 128), all2],
+    )(b2)
+    left, right = from_both(b3, b3, "gz")
     (out,) = call(
         functools.partial(up_kernel, n),
         [(8, 64, 128)],
         [
-            (p2, rows2, 128), (p2, rows2, 128), colour2, colour2, (rows2, 128), (p2, rows2, 128),
-            (p3, rows3, 128), (p3, rows3, 128), colour3, colour3, (rows3, 128), (p2, rows2, 128),
+            colour2, colour2, (rows2, 128),
+            (packed, rows3, 128), (packed, rows3, 128), colour3, colour3, (rows3, 128), all2,
             window1, (10, ROWS1 + 2 * PAD, 128), (10, ROWS1 + 2 * PAD, 128), window1,
             (16, 80, 128), (10, 80 + 2 * PAD, 256), (10, 80 + 2 * PAD, 256), (3, 80, 256),
         ],
-    )(b2, black1, red_b1, black_b1, black0, red_b0, black_b0)
+    )(b3, left, right, black2, red_b2, black_b2, black1, red_b1, black_b1, black0, red_b0, black_b0)
     return out
 
 

time: 90.1 us -> 87.2 us (0.968)
  the two profiles are of different devices: /device:TPU:384 before, /device:TPU:256 now
where the time goes in v3:
time: 87.2 us; the launch traced here: 86.8 us
  waiting for transfers between devices  25.9 us (30%)
  starting transfers between devices  25.3 us (29%)
  blocking collectives  22.7 us (26%)
  Pallas kernels  10.9 us (12%)
  local copies, waits for them, and re-layouts  1.95 us (2%)
    all_to_all x2, blocking collectives, gathered(): lax.all_to_all(copies, axis, split_axis=0, concat_axis=0, axis_index_grou...  22.7 us
    ppermute x3, waiting for transfers between devices, from_both(): lax.ppermute(up_value, axis, up)  13.3 us
    ppermute x3, starting transfers between devices, from_both(): lax.ppermute(down_value, axis, [(b, a) for a, b in up])  10.8 us
    ppermute x3, starting transfers between devices, from_both(): lax.ppermute(up_value, axis, up)  8.25 us
    ppermute x3, waiting for transfers between devices, from_both(): lax.ppermute(down_value, axis, [(b, a) for a, b in up])  5.58 us
    ppermute x2, waiting for transfers between devices, from_both_round(): lax.ppermute(up_value, axis, up)  5.46 us
    pallas_call x1, Pallas kernels, local(): call(functools.partial(up_kernel, n), [(8, 64, 128)], [colour2, colour2,...  4.83 us
    ppermute x2, starting transfers between devices, from_both_round(): lax.ppermute(down_value, axis, [(b, a) for a, b in up])  4.22 us
  transfers between devices with their start and end apart: 11, of which 7 were waited for; matrix products, arithmetic and copies ran while one was open for 0% of the time, Pallas kernels for 0%

profile of v3, /device:TPU:256, one launch (start us, length us, event | category | flops | bytes accessed | tf_op | source)
XLA Modules:
  0.0 86.8 jit_solution(8277649677846057545)
XLA Ops:
  0.0 0.0 copy-start
  0.0 0.9 %copy-done = f32[8,64,128]{2,1,0:T(8,128)S(1)} copy-done((f32[8,64,128]{2,1,0:T(8,128)S(1)}, f32[8,64,128]{2,1,0:T(8,128)}, u32[]{:S(2)}) %copy-start) | copy-done | bytes 262168
  1.0 0.0 copy-start.1
  1.0 0.9 %copy-done.1 = f32[8,64,128]{2,1,0:T(8,128)S(1)} copy-done((f32[8,64,128]{2,1,0:T(8,128)S(1)}, f32[8,64,128]{2,1,0:T(8,128)}, u32[]{:S(2)}) %copy-start.1) | copy-done | bytes 262168
  1.9 0.2 shard_map.28
  2.1 2.9 %collective-permute-start = (f32[6,64,128]{2,1,0:T(8,128)S(1)}, f32[6,64,128]{2,1,0:T(8,128)S(1)}, u32[]{:S(2)}, u32[]{:S(2)}) collective-permute-start(f32[6,64,128]{2,1,0:T(8,128)S(1)} %get-tuple-element.27), channel_id=1, source_target_pairs={{0,1},{1,2},{2,3},{3,4},{4,5},{5,6},{6,7},{7,8},{8,9},{9,10},{10,1... | collective-permute-start | bytes 589832 | tf_op jit(solution)/shard_map/ppermute | solution.py:468
  5.0 4.1 %collective-permute-start.1 = (f32[6,64,128]{2,1,0:T(8,128)S(1)}, f32[6,64,128]{2,1,0:T(8,128)S(1)}, u32[]{:S(2)}, u32[]{:S(2)}) collective-permute-start(f32[6,64,128]{2,1,0:T(8,128)S(1)} %get-tuple-element.28), channel_id=1, source_target_pairs={{1,0},{2,1},{3,2},{4,3},{5,4},{6,5},{7,6},{8,7},{9,8},{10,9},{11,1... | collective-permute-start | bytes 589832 | tf_op jit(solution)/shard_map/ppermute | solution.py:468
  9.2 2.7 %collective-permute-done.up = f32[6,64,128]{2,1,0:T(8,128)S(1)} collective-permute-done((f32[6,64,128]{2,1,0:T(8,128)S(1)}, f32[6,64,128]{2,1,0:T(8,128)S(1)}, u32[]{:S(2)}, u32[]{:S(2)}) %collective-permute-start) | collective-permute-done | bytes 196640 | tf_op jit(solution)/shard_map/ppermute | solution.py:468
  11.8 1.4 %collective-permute-done.1.down = f32[6,64,128]{2,1,0:T(8,128)S(1)} collective-permute-done((f32[6,64,128]{2,1,0:T(8,128)S(1)}, f32[6,64,128]{2,1,0:T(8,128)S(1)}, u32[]{:S(2)}, u32[]{:S(2)}) %collective-permute-start.1) | collective-permute-done | bytes 196640 | tf_op jit(solution)/shard_map/ppermute | solution.py:468
  13.3 0.1 shard_map.29
  13.4 1.3 %collective-permute-start.5 = (f32[24,64,128]{2,1,0:T(8,128)S(1)}, f32[24,64,128]{2,1,0:T(8,128)S(1)}, u32[]{:S(2)}, u32[]{:S(2)}) collective-permute-start(f32[24,64,128]{2,1,0:T(8,128)S(1)} %get-tuple-element.29.s), channel_id=1, source_target_pairs={{64,0},{128,64},{192,128},{256,192},{320,256},{384,320},{448,384},... | collective-permute-start | bytes 2359304 | tf_op jit(solution)/shard_map/ppermute | solution.py:474
  14.7 0.0 collective-permute-start.4
  14.7 3.4 %collective-permute-start.2 = (f32[12,24,256]{2,1,0:T(8,128)S(1)}, f32[12,24,256]{2,1,0:T(8,128)S(1)}, u32[]{:S(2)}, u32[]{:S(2)}) collective-permute-start(f32[12,24,256]{2,1,0:T(8,128)S(1)} %get-tuple-element.30), channel_id=1, source_target_pairs={{0,16},{16,32},{32,48},{1,17},{17,33},{33,49},{2,18},{18,34},{34,5... | collective-permute-start | bytes 884744 | tf_op jit(solution)/shard_map/ppermute | solution.py:468
  18.1 1.3 %collective-permute-start.3 = (f32[12,24,256]{2,1,0:T(8,128)S(1)}, f32[12,24,256]{2,1,0:T(8,128)S(1)}, u32[]{:S(2)}, u32[]{:S(2)}) collective-permute-start(f32[12,24,256]{2,1,0:T(8,128)S(1)} %get-tuple-element.31), channel_id=1, source_target_pairs={{16,0},{32,16},{48,32},{17,1},{33,17},{49,33},{18,2},{34,18},{50,3... | collective-permute-start | bytes 884744 | tf_op jit(solution)/shard_map/ppermute | solution.py:468
  19.4 5.5 %collective-permute-done.2.before = f32[12,24,256]{2,1,0:T(8,128)S(1)} collective-permute-done((f32[12,24,256]{2,1,0:T(8,128)S(1)}, f32[12,24,256]{2,1,0:T(8,128)S(1)}, u32[]{:S(2)}, u32[]{:S(2)}) %collective-permute-start.2) | collective-permute-done | bytes 294944 | tf_op jit(solution)/shard_map/ppermute | solution.py:468
  25.0 4.1 %collective-permute-done.3.after = f32[12,24,256]{2,1,0:T(8,128)S(1)} collective-permute-done((f32[12,24,256]{2,1,0:T(8,128)S(1)}, f32[12,24,256]{2,1,0:T(8,128)S(1)}, u32[]{:S(2)}, u32[]{:S(2)}) %collective-permute-start.3) | collective-permute-done | bytes 294944 | tf_op jit(solution)/shard_map/ppermute | solution.py:468
  29.1 0.1 shard_map.30
  29.1 0.0 collective-permute-start.6
  29.2 2.9 %collective-permute-start.7 = (f32[6,64,256]{2,1,0:T(8,128)S(1)}, f32[6,64,256]{2,1,0:T(8,128)S(1)}, u32[]{:S(2)}, u32[]{:S(2)}) collective-permute-start(f32[6,64,256]{2,1,0:T(8,128)S(1)} %get-tuple-element.33), channel_id=1, source_target_pairs={{64,0},{128,64},{192,128},{256,192},{320,256},{384,320},{448,384},... | collective-permute-start | bytes 1179656 | tf_op jit(solution)/shard_map/ppermute | solution.py:474
  32.1 5.5 %collective-permute-done.6.y_left = f32[6,64,256]{2,1,0:T(8,128)S(1)} collective-permute-done((f32[6,64,256]{2,1,0:T(8,128)S(1)}, f32[6,64,256]{2,1,0:T(8,128)S(1)}, u32[]{:S(2)}, u32[]{:S(2)}) %collective-permute-start.6) | collective-permute-done | bytes 393248 | tf_op jit(solution)/shard_map/ppermute | solution.py:474
  37.6 0.0 collective-permute-done.7.y_right
  37.6 0.0 collective-permute-done.5.s_right
  37.6 0.0 collective-permute-done.4.s_left
  37.6 3.4 %shard_map.31 = (f32[4,56,128]{2,1,0:T(8,128)S(1)}, f32[4,48,128]{2,1,0:T(8,128)S(1)}, f32[8,80,256]{2,1,0:T(8,128)S(1)}, f32[8,80,256]{2,1,0:T(8,128)S(1)}, f32[8,80,256]{2,1,0:T(8,128)S(1)}) custom-call(f32[24,64,128]{2,1,0:T(8,128)S(1)} %get-tuple-element.29.s, f32[12,24,256]{2,1,0:T(8,128)S(1)} %collective-permute-done.2.before, ...), custom_call_target="tpu_custom_call" | custom-call | tf_op jit(solution)/shard_map/pallas_call | solution.py:498
  41.1 11.9 %all_to_all.10 = f32[4,1,4,48,128]{4,3,2,1,0:T(8,128)S(1)} all-to-all(f32[4,1,4,48,128]{4,3,2,1,0:T(8,128)S(1)} %broadcast_in_dim.7), channel_id=1, replica_groups={{0,128,256,384},{64,192,320,448},{1,129,257,385},{65,193,321,449},{2,13..., dimensions={0} | all-to-all | bytes 786432 | tf_op jit(solution)/shard_map/all_to_all | solution.py:480
  53.0 2.0 %collective-permute-start.8 = (f32[4,1,4,48,128]{4,3,2,0,1:T(8,128)S(1)}, f32[4,1,4,48,128]{4,3,2,0,1:T(8,128)S(1)}, u32[]{:S(2)}, u32[]{:S(2)}) collective-permute-start(f32[4,1,4,48,128]{4,3,2,0,1:T(8,128)S(1)} %bitcast.3), channel_id=1, source_target_pairs={{0,64},{64,0},{128,192},{192,128},{256,320},{320,256},{384,448},{4... | collective-permute-start | bytes 1179656 | tf_op jit(solution)/shard_map/ppermute | solution.py:505
  55.0 1.6 %collective-permute-done.8 = f32[4,1,4,48,128]{4,3,2,0,1:T(8,128)S(1)} collective-permute-done((f32[4,1,4,48,128]{4,3,2,0,1:T(8,128)S(1)}, f32[4,1,4,48,128]{4,3,2,0,1:T(8,128)S(1)}, u32[]{:S(2)}, u32[]{:S(2)}) %collective-permute-start.8) | collective-permute-done | bytes 393248 | tf_op jit(solution)/shard_map/ppermute | solution.py:505
  56.6 1.5 %shard_map.32 = (f32[8,16,128]{2,1,0:T(8,128)S(1)}, f32[8,56,128]{2,1,0:T(8,128)S(1)}, f32[8,56,128]{2,1,0:T(8,128)S(1)}, f32[8,56,128]{2,1,0:T(8,128)S(1)}) custom-call(f32[4,56,128]{2,1,0:T(8,128)S(1)} %get-tuple-element.34.own, f32[4,4,48,128]{3,2,1,0:T(8,128)S(1)} %bitcast.4, f32[4,4,48,128]{3,2,1,0:T(8,128)S(1)} %bitcast.5), custom_call_target="tpu_custom_call" | custom-call | tf_op jit(solution)/shard_map/pallas_call | solution.py:510
  58.1 10.8 %all_to_all.11.b2 = f32[4,8,16,128]{3,2,1,0:T(8,128)S(1)} all-to-all(f32[4,8,16,128]{3,2,1,0:T(8,128)S(1)} %broadcast_in_dim.8), channel_id=1, replica_groups=mesh['gx'=8,'gy'=4,'gz'=16] {'gy'}, dimensions={0} | all-to-all | bytes 524288 | tf_op jit(solution)/shard_map/all_to_all | solution.py:480
  68.9 0.8 shard_map.33
  69.6 5.3 %collective-permute-start.10 = (f32[2,32,128]{2,1,0:T(8,128)S(1)}, f32[2,32,128]{2,1,0:T(8,128)S(1)}, u32[]{:S(2)}, u32[]{:S(2)}) collective-permute-start(f32[2,32,128]{2,1,0:T(8,128)S(1)} %get-tuple-element.37.b3), channel_id=1, source_target_pairs={{1,0},{2,1},{3,2},{4,3},{5,4},{6,5},{7,6},{8,7},{9,8},{10,9},{11,1... | collective-permute-start | bytes 98312 | tf_op jit(solution)/shard_map/ppermute | solution.py:468
  75.0 1.9 %collective-permute-start.9 = (f32[2,32,128]{2,1,0:T(8,128)S(1)}, f32[2,32,128]{2,1,0:T(8,128)S(1)}, u32[]{:S(2)}, u32[]{:S(2)}) collective-permute-start(f32[2,32,128]{2,1,0:T(8,128)S(1)} %get-tuple-element.37.b3), channel_id=1, source_target_pairs={{0,1},{1,2},{2,3},{3,4},{4,5},{5,6},{6,7},{7,8},{8,9},{9,10},{10,1... | collective-permute-start | bytes 98312 | tf_op jit(solution)/shard_map/ppermute | solution.py:468
  76.9 0.0 collective-permute-done.10.b3_right
  76.9 5.1 %collective-permute-done.9.b3_left = f32[2,32,128]{2,1,0:T(8,128)S(1)} collective-permute-done((f32[2,32,128]{2,1,0:T(8,128)S(1)}, f32[2,32,128]{2,1,0:T(8,128)S(1)}, u32[]{:S(2)}, u32[]{:S(2)}) %collective-permute-start.9) | collective-permute-done | bytes 32800 | tf_op jit(solution)/shard_map/ppermute | solution.py:468
  82.0 4.8 %shard_map.34 = f32[8,64,128]{2,1,0:T(8,128)} custom-call(f32[2,32,128]{2,1,0:T(8,128)S(1)} %get-tuple-element.37.b3, f32[2,32,128]{2,1,0:T(8,128)S(1)} %collective-permute-done.9.b3_left, f32[2,32,128]{2,1,0:T(8,128)S(1)} %collective-permute-done.10.b3_right, f32[4,64,128]{2,1,0:T(8,128)S(1)} %get-tuple-element.38.start2, ...), custom_call_target="tpu_custom_call" | custom-call | tf_op jit(solution)/shard_map/pallas_call | solution.py:525
  (2 shorter events, 0.0 us)
Async XLA Ops:
  0.0 0.9 %copy-start = (f32[8,64,128]{2,1,0:T(8,128)S(1)}, f32[8,64,128]{2,1,0:T(8,128)}, u32[]{:S(2)}) copy-start(f32[8,64,128]{2,1,0:T(8,128)} %start_hbm.1) | copy-start | bytes 786436
  1.0 0.9 %copy-start.1 = (f32[8,64,128]{2,1,0:T(8,128)S(1)}, f32[8,64,128]{2,1,0:T(8,128)}, u32[]{:S(2)}) copy-start(f32[8,64,128]{2,1,0:T(8,128)} %right_hbm.1) | copy-start | bytes 786436
  2.1 9.7 %collective-permute-start = (f32[6,64,128]{2,1,0:T(8,128)S(1)}, f32[6,64,128]{2,1,0:T(8,128)S(1)}, u32[]{:S(2)}, u32[]{:S(2)}) collective-permute-start(f32[6,64,128]{2,1,0:T(8,128)S(1)} %get-tuple-element.27), channel_id=1, source_target_pairs={{0,1},{1,2},{2,3},{3,4},{4,5},{5,6},{6,7},{7,8},{8,9},{9,10},{10,1... | collective-permute-start | bytes 589832 | tf_op jit(solution)/shard_map/ppermute | solution.py:468
  5.0 8.3 %collective-permute-start.1 = (f32[6,64,128]{2,1,0:T(8,128)S(1)}, f32[6,64,128]{2,1,0:T(8,128)S(1)}, u32[]{:S(2)}, u32[]{:S(2)}) collective-permute-start(f32[6,64,128]{2,1,0:T(8,128)S(1)} %get-tuple-element.28), channel_id=1, source_target_pairs={{1,0},{2,1},{3,2},{4,3},{5,4},{6,5},{7,6},{8,7},{9,8},{10,9},{11,1... | collective-permute-start | bytes 589832 | tf_op jit(solution)/shard_map/ppermute | solution.py:468
  13.4 24.2 %collective-permute-start.5 = (f32[24,64,128]{2,1,0:T(8,128)S(1)}, f32[24,64,128]{2,1,0:T(8,128)S(1)}, u32[]{:S(2)}, u32[]{:S(2)}) collective-permute-start(f32[24,64,128]{2,1,0:T(8,128)S(1)} %get-tuple-element.29.s), channel_id=1, source_target_pairs={{64,0},{128,64},{192,128},{256,192},{320,256},{384,320},{448,384},... | collective-permute-start | bytes 2359304 | tf_op jit(solution)/shard_map/ppermute | solution.py:474
  14.7 22.9 %collective-permute-start.4 = (f32[24,64,128]{2,1,0:T(8,128)S(1)}, f32[24,64,128]{2,1,0:T(8,128)S(1)}, u32[]{:S(2)}, u32[]{:S(2)}) collective-permute-start(f32[24,64,128]{2,1,0:T(8,128)S(1)} %get-tuple-element.29.s), channel_id=1, source_target_pairs={{0,64},{64,128},{128,192},{192,256},{256,320},{320,384},{384,448},... | collective-permute-start | bytes 2359304 | tf_op jit(solution)/shard_map/ppermute | solution.py:474
  14.7 10.3 %collective-permute-start.2 = (f32[12,24,256]{2,1,0:T(8,128)S(1)}, f32[12,24,256]{2,1,0:T(8,128)S(1)}, u32[]{:S(2)}, u32[]{:S(2)}) collective-permute-start(f32[12,24,256]{2,1,0:T(8,128)S(1)} %get-tuple-element.30), channel_id=1, source_target_pairs={{0,16},{16,32},{32,48},{1,17},{17,33},{33,49},{2,18},{18,34},{34,5... | collective-permute-start | bytes 884744 | tf_op jit(solution)/shard_map/ppermute | solution.py:468
  18.1 11.0 %collective-permute-start.3 = (f32[12,24,256]{2,1,0:T(8,128)S(1)}, f32[12,24,256]{2,1,0:T(8,128)S(1)}, u32[]{:S(2)}, u32[]{:S(2)}) collective-permute-start(f32[12,24,256]{2,1,0:T(8,128)S(1)} %get-tuple-element.31), channel_id=1, source_target_pairs={{16,0},{32,16},{48,32},{17,1},{33,17},{49,33},{18,2},{34,18},{50,3... | collective-permute-start | bytes 884744 | tf_op jit(solution)/shard_map/ppermute | solution.py:468
  29.1 8.4 %collective-permute-start.6 = (f32[6,64,256]{2,1,0:T(8,128)S(1)}, f32[6,64,256]{2,1,0:T(8,128)S(1)}, u32[]{:S(2)}, u32[]{:S(2)}) collective-permute-start(f32[6,64,256]{2,1,0:T(8,128)S(1)} %get-tuple-element.32), channel_id=1, source_target_pairs={{0,64},{64,128},{128,192},{192,256},{256,320},{320,384},{384,448},... | collective-permute-start | bytes 1179656 | tf_op jit(solution)/shard_map/ppermute | solution.py:474
  29.2 8.4 %collective-permute-start.7 = (f32[6,64,256]{2,1,0:T(8,128)S(1)}, f32[6,64,256]{2,1,0:T(8,128)S(1)}, u32[]{:S(2)}, u32[]{:S(2)}) collective-permute-start(f32[6,64,256]{2,1,0:T(8,128)S(1)} %get-tuple-element.33), channel_id=1, source_target_pairs={{64,0},{128,64},{192,128},{256,192},{320,256},{384,320},{448,384},... | collective-permute-start | bytes 1179656 | tf_op jit(solution)/shard_map/ppermute | solution.py:474
  53.0 3.6 %collective-permute-start.8 = (f32[4,1,4,48,128]{4,3,2,0,1:T(8,128)S(1)}, f32[4,1,4,48,128]{4,3,2,0,1:T(8,128)S(1)}, u32[]{:S(2)}, u32[]{:S(2)}) collective-permute-start(f32[4,1,4,48,128]{4,3,2,0,1:T(8,128)S(1)} %bitcast.3), channel_id=1, source_target_pairs={{0,64},{64,0},{128,192},{192,128},{256,320},{320,256},{384,448},{4... | collective-permute-start | bytes 1179656 | tf_op jit(solution)/shard_map/ppermute | solution.py:505
  69.6 7.3 %collective-permute-start.10 = (f32[2,32,128]{2,1,0:T(8,128)S(1)}, f32[2,32,128]{2,1,0:T(8,128)S(1)}, u32[]{:S(2)}, u32[]{:S(2)}) collective-permute-start(f32[2,32,128]{2,1,0:T(8,128)S(1)} %get-tuple-element.37.b3), channel_id=1, source_target_pairs={{1,0},{2,1},{3,2},{4,3},{5,4},{6,5},{7,6},{8,7},{9,8},{10,9},{11,1... | collective-permute-start | bytes 98312 | tf_op jit(solution)/shard_map/ppermute | solution.py:468
  75.0 7.0 %collective-permute-start.9 = (f32[2,32,128]{2,1,0:T(8,128)S(1)}, f32[2,32,128]{2,1,0:T(8,128)S(1)}, u32[]{:S(2)}, u32[]{:S(2)}) collective-permute-start(f32[2,32,128]{2,1,0:T(8,128)S(1)} %get-tuple-element.37.b3), channel_id=1, source_target_pairs={{0,1},{1,2},{2,3},{3,4},{4,5},{5,6},{6,7},{7,8},{8,9},{9,10},{10,1... | collective-permute-start | bytes 98312 | tf_op jit(solution)/shard_map/ppermute | solution.py:468

commit v4 on v3

--- a/solution.py
+++ b/solution.py
@@ -13,7 +13,8 @@
 EY = 24
 ROWS0 = 64 + 2 * EY
 ROWS1 = ROWS0 // 2
-SENT1 = ROWS1 - 8
+SENT1 = 50
+SENT1_AT = 3
 PAD = 8
 UP0 = EY - 8
 VMEM_LIMIT = 40 * 1024 * 1024
@@ -119,32 +120,83 @@
         down[p] = jnp.where(low, a, b)
 
 
-def widen_kernel(s, up, down, sv, first, last):
+def pack16(planes, first=0):
+    lanes = lane_of(planes[0].shape)
+    total = jnp.zeros(planes[0].shape, F32)
+    for k, plane in enumerate(planes):
+        at = 16 * (k + first)
+        total = jnp.where((lanes >= at) & (lanes < at + 16), pltpu.roll(plane, (8 + at) % 128, 1), total)
+    return total
+
+
+def unpack16(packed, k):
+    lanes = lane_of(packed.shape)
+    shift = (-8 - 16 * k) % 128
+    plane = pltpu.roll(packed, shift, 1) if shift else packed
+    return jnp.where((lanes < 8) | (lanes >= 120), plane, 0.0)
+
+
+UP_NEAR, UP_FAR = (1, 2, 3, 6, 7, 10, 11), (0, 4, 5, 8, 9)
+DOWN_NEAR, DOWN_FAR = (0, 1, 2, 4, 5, 8, 9), (3, 6, 7, 10, 11)
+NEAR, FAR = len(UP_NEAR), len(UP_FAR)
+CROSS_Y = 12 * 24 + 12 * 16 + 2 * 8
+STRIP_AT = 48 * NEAR
+FAR_AT = STRIP_AT + 32 * NEAR
+PACKED_AT = FAR_AT + 16 * FAR
+CROSS_X = PACKED_AT + 2 * 16
+
+
+def widen_kernel(s, up, down, v, v_up, v_down, first, last):
     low = lane_of((64, 128)) < 64
     for p in range(6):
-        sv[p + 12] = jnp.where(low, down[p], up[p])
-        sv[p + 18] = pltpu.roll(jnp.where(low, up[p], down[p]), 64, 1)
+        v[p] = jnp.where(low, down[p], up[p])
+        v[p + 6] = pltpu.roll(jnp.where(low, up[p], down[p]), 64, 1)
     for p in range(12):
-        sv[p] = s[p]
-        first[p, :, :128] = s[p, :EY]
-        first[p, :, 128:] = sv[p + 12, :EY]
-        last[p, :, :128] = s[p, 64 - EY :]
-        last[p, :, 128:] = sv[p + 12, 64 - EY :]
-
-
-def strips_kernel(before, after, up, down):
-    for a in range(3):
-        for q in range(2):
-            for ref, near, far in ((up, 2 + q, q), (down, q, 2 + q)):
-                j = 2 * a + q
-                ref[j, :EY] = before[4 * a + near]
-                ref[j, EY : 2 * EY] = after[4 * a + near]
-                ref[j, 48:56] = before[4 * a + far, EY - 8 :]
-                ref[j, 56:64] = after[4 * a + far, :8]
+        first[24 * p : 24 * p + 24] = s[p, :24]
+        last[24 * p : 24 * p + 24] = s[p, 40:]
+        at = 288 + 16 * p
+        first[at : at + 16] = v[p, :16]
+        last[at : at + 16] = v[p, 48:]
+    for t in range(2):
+        at = 480 + 8 * t
+        first[at : at + 8] = pack16([v[6 * t + k, 16:24] for k in range(6)])
+        last[at : at + 8] = pack16([v[6 * t + k, 40:48] for k in range(6)])
+    for ref, near, far in ((v_up, UP_NEAR, UP_FAR), (v_down, DOWN_NEAR, DOWN_FAR)):
+        for k, p in enumerate(near):
+            ref[k] = v[p]
+        ref[NEAR] = pack16([v[p] for p in far])
+
+
+def strips_kernel(before, after, *rest):
+    lanes = lane_of((8, 128))
+    for ref, near, far in ((rest[-2], UP_NEAR, UP_FAR), (rest[-1], DOWN_NEAR, DOWN_FAR)):
+        outer = [jnp.zeros((8, 128), F32), jnp.zeros((8, 128), F32)]
+        for k, p in enumerate(near):
+            ref[48 * k : 48 * k + 24] = before[24 * p : 24 * p + 24]
+            ref[48 * k + 24 : 48 * k + 48] = after[24 * p : 24 * p + 24]
+            at, inner = STRIP_AT + 32 * k, 288 + 16 * p
+            ref[at : at + 16] = before[inner : inner + 16]
+            ref[at + 16 : at + 32] = after[inner : inner + 16]
+            at, shift = 480 + 8 * (p // 6), 16 * (k - p % 6) % 128
+            for h, strip in enumerate((before, after)):
+                plane = strip[at : at + 8]
+                plane = pltpu.roll(plane, shift, 1) if shift else plane
+                outer[h] = jnp.where((lanes >= 16 * k) & (lanes < 16 * k + 16), plane, outer[h])
+        edges = [[], []]
+        for k, p in enumerate(far):
+            at, inner = FAR_AT + 16 * k, 288 + 16 * p
+            ref[at : at + 8] = before[24 * p + 16 : 24 * p + 24]
+            ref[at + 8 : at + 16] = after[24 * p : 24 * p + 8]
+            edges[0].append(before[inner + 8 : inner + 16])
+            edges[1].append(after[inner : inner + 8])
+        for h in range(2):
+            at = PACKED_AT + 8 * h
+            ref[at : at + 8] = outer[h]
+            ref[at + 16 : at + 24] = pack16(edges[h])
 
 
 def fine_down_kernel(
-    n, s, before, after, s_left, s_right, y_left, y_right,
+    n, s, v, before, after, s_left, s_right, v_left, v_right, y_left, y_right,
     coarse, sent, black_out, red_b_out, black_b_out, red, black, rb, bb, weight, pairs,
 ):
     gx, gy, gz = (lax.axis_index(a) for a in ("gx", "gy", "gz"))
@@ -154,35 +206,57 @@
     weight[1] = inner
     weight[2] = jnp.where(has_right, inner, 0.0)
     clear_pads(black, red)
-    zero8 = jnp.zeros((8, 256), F32)
+    block, strip = slice(0, 128), slice(128, 256)
+    zero8 = jnp.zeros((8, 128), F32)
     for a, ref in enumerate((black, rb, bb)):
         off, top = (1, PAD) if a == 0 else (0, 0)
-        mid, end = top + EY, top + EY + 64
-
-        def put(i, lo, value, keep, ref=ref, off=off, a=a):
-            hi = lo + value.shape[0]
-            lanes = slice(0, 256) if value.shape[1] == 256 else keep[1]
-            if a == 0 and keep[0] is not None:
-                value = jnp.where(keep[0], value, 0.0)
-            ref[i + off, lo:hi, lanes] = value
+
+        def put(i, lo, lanes, value, there=None, ref=ref, off=off, top=top, a=a):
+            if a == 0 and there is not None:
+                value = jnp.where(there, value, 0.0)
+            ref[i + off, top + lo : top + lo + value.shape[0], lanes] = value
 
         for p in range(4):
-            j = 4 * a + p
-            for base, whole, there in ((4, s, None), (0, s_left, has_left), (8, s_right, has_right)):
-                put(base + p, mid, whole[j], (there, slice(0, 128)))
-                put(base + p, mid, whole[j + 12], (there, slice(128, 256)))
-            put(4 + p, top, before[j], (None, None))
-            put(4 + p, end, after[j], (None, None))
-        for q in range(2):
-            j = 2 * a + q
-            for base, y, near, far, there in ((0, y_left, 2 + q, q, has_left), (8, y_right, q, 2 + q, has_right)):
-                put(base + near, top, y[j, :EY], (there, None))
-                put(base + near, end, y[j, EY : 2 * EY], (there, None))
-                for k in range(2):
-                    put(base + far, top + 8 * k, zero8, (None, None))
-                    put(base + far, end + 8 + 8 * k, zero8, (None, None))
-                put(base + far, mid - 8, y[j, 48:56], (there, None))
-                put(base + far, end, y[j, 56:64], (there, None))
+            j, i = 4 * a + p, 4 + p
+            put(i, EY, block, s[j])
+            put(i, EY, strip, v[j])
+            put(p, EY, block, s_left[j], has_left)
+            put(8 + p, EY, block, s_right[j], has_right)
+            put(i, 0, block, before[24 * j : 24 * j + 24])
+            put(i, EY + 64, block, after[24 * j : 24 * j + 24])
+            at = 288 + 16 * j
+            put(i, 8, strip, before[at : at + 16])
+            put(i, EY + 64, strip, after[at : at + 16])
+            at = 480 + 8 * (j // 6)
+            put(i, 0, strip, unpack16(before[at : at + 8], j % 6))
+            put(i, EY + 80, strip, unpack16(after[at : at + 8], j % 6))
+        sides = ((0, UP_NEAR, UP_FAR, v_left, y_left, has_left), (8, DOWN_NEAR, DOWN_FAR, v_right, y_right, has_right))
+        for base, near, far, strips, y, there in sides:
+            for k, p in enumerate(near):
+                if p // 4 != a:
+                    continue
+                i = base + p % 4
+                put(i, EY, strip, strips[k], there)
+                put(i, 0, block, y[48 * k : 48 * k + 24], there)
+                put(i, EY + 64, block, y[48 * k + 24 : 48 * k + 48], there)
+                at = STRIP_AT + 32 * k
+                put(i, 8, strip, y[at : at + 16], there)
+                put(i, EY + 64, strip, y[at + 16 : at + 32], there)
+                put(i, 0, strip, unpack16(y[PACKED_AT : PACKED_AT + 8], k), there)
+                put(i, EY + 80, strip, unpack16(y[PACKED_AT + 8 : PACKED_AT + 16], k), there)
+            for k, p in enumerate(far):
+                if p // 4 != a:
+                    continue
+                i = base + p % 4
+                put(i, EY, strip, unpack16(strips[NEAR], k), there)
+                at = FAR_AT + 16 * k
+                put(i, 16, block, y[at : at + 8], there)
+                put(i, EY + 64, block, y[at + 8 : at + 16], there)
+                put(i, 16, strip, unpack16(y[PACKED_AT + 16 : PACKED_AT + 24], k), there)
+                put(i, EY + 64, strip, unpack16(y[PACKED_AT + 24 : PACKED_AT + 32], k), there)
+                for lanes in (block, strip):
+                    for lo in (0, 8, EY + 72, EY + 80):
+                        put(i, lo, lanes, zero8)
 
     def weights(i, r, step):
         return weight[i // 4, r : r + step]
@@ -204,7 +278,7 @@
     result = dot(jnp.concatenate(rows, axis=0), table(256, 128, lambda k, c: (k >> 1) == c, 0.5))
     for p in range(4):
         coarse[p] = result[p * ROWS1 : (p + 1) * ROWS1]
-        sent[p] = coarse[p, 4 : 4 + SENT1]
+        sent[SENT1 * p : SENT1 * p + SENT1] = coarse[p, SENT1_AT : SENT1_AT + SENT1]
     for p in range(8):
         black_out[p] = black[p + 3, PAD + UP0 : PAD + UP0 + 80]
         red_b_out[p] = rb[p + 2, UP0 : UP0 + 80]
@@ -218,19 +292,18 @@
     count = 2 * n[0]
     core = gx % 2
     even = even_mask((ROWS1, 128))
-    even_sent = even_mask((SENT1, 128))
+    even_sent = even_mask((SENT1, 128)) ^ (SENT1_AT % 2 == 1)
     weight[...] = domain((ROWS1, 128), 32 * gy - EY // 2, 32 * n[1], 64 * gz, 64 * n[2], 96)
     clear_pads(red, black)
-    zero4 = jnp.zeros((4, 128), F32)
+    zero = jnp.zeros((SENT1_AT, 128), F32)
     for i in range(count):
-        block, q = i // 2, 2 * (i % 2)
+        block, q = i // 2, 2 * SENT1 * (i % 2)
         mine = core == block % 2
-        a = jnp.where(mine, same[block // 2, q], other[block // 2, q])
-        b = jnp.where(mine, same[block // 2, q + 1], other[block // 2, q + 1])
+        a, b = (jnp.where(mine, same[block // 2, at : at + SENT1], other[block // 2, at : at + SENT1]) for at in (q, q + SENT1))
         for ref, v in ((rb, jnp.where(even_sent, a, b)), (bb, jnp.where(even_sent, b, a))):
-            ref[i, :4] = zero4
-            ref[i, 4 : 4 + SENT1] = v
-            ref[i, 4 + SENT1 :] = zero4
+            ref[i, :SENT1_AT] = zero
+            ref[i, SENT1_AT : SENT1_AT + SENT1] = v
+            ref[i, SENT1_AT + SENT1 :] = zero
     for h in range(2):
         a, b = own[2 * h], own[2 * h + 1]
         rb[2 * gx + h] = jnp.where(even, a, b)
@@ -489,24 +562,27 @@
         [pl.BlockSpec(memory_space=pltpu.HBM)] * 2,
     )(start, right_side)
     up, down = from_both(up, down, "gz")
-    sv, first, last = call(widen_kernel, [(24, 64, 128), (12, EY, 256), (12, EY, 256)])(s, up, down)
-    s_left, s_right = from_both_round(sv, sv, "gx")
+    s_left, s_right = from_both_round(s, s, "gx")
+    v, v_up, v_down, first, last = call(
+        widen_kernel, [(12, 64, 128), (NEAR + 1, 64, 128), (NEAR + 1, 64, 128), (CROSS_Y, 128), (CROSS_Y, 128)]
+    )(s, up, down)
+    v_left, v_right = from_both_round(v_up, v_down, "gx")
     before, after = from_both(last, first, "gy")
-    up, down = call(strips_kernel, [(6, 64, 256)] * 2)(before, after)
+    up, down = call(strips_kernel, [(CROSS_X, 128)] * 2)(before, after, s_left, s_right, v_left, v_right)
     y_left, y_right = from_both_round(up, down, "gx")
     up0 = (8, 80, 256)
     b1, sent, black0, red_b0, black_b0 = call(
         functools.partial(fine_down_kernel, n),
-        [(4, ROWS1, 128), (4, SENT1, 128), up0, up0, up0],
+        [(4, ROWS1, 128), (4 * SENT1, 128), up0, up0, up0],
         [(14, ROWS0 + 2 * PAD, 256)] * 2 + [(12, ROWS0, 256)] * 2 + [(3, ROWS0, 256), (8, ROWS0, 128)],
-    )(sv, before, after, s_left, s_right, y_left, y_right)
+    )(s, v, before, after, s_left, s_right, v_left, v_right, y_left, y_right)
     groups = [[2 * chip + core for chip in range(n[0] // 2)] for core in range(2)]
     same = gathered(sent[None], "gx", groups)
     other = lax.ppermute(same, "gx", [(i, i ^ 1) for i in range(n[0])])
     all1 = (2 * n[0], ROWS1, 128)
     colour1 = (2 * n[0] + 2, ROWS1 + 2 * PAD, 128)
     window1 = (8, ROWS1, 128)
-    blocks = (n[0] // 2, 4, SENT1, 128)
+    blocks = (n[0] // 2, 4 * SENT1, 128)
     b2, black1, red_b1, black_b1 = call(
         functools.partial(middle_down_kernel, n),
         [(n[0], 16, 128), window1, window1, window1],

time: 87.2 us -> 88.2 us (1.011)
  the two profiles are of different devices: /device:TPU:256 before, /device:TPU:128 now
where the time goes in v4:
time: 88.2 us; the launch traced here: 87.8 us
  starting transfers between devices  29 us (33%)
  waiting for transfers between devices  22.5 us (26%)
  blocking collectives  22.3 us (25%)
  Pallas kernels  11.9 us (13%)
  local copies, waits for them, and re-layouts  1.95 us (2%)
    all_to_all x2, blocking collectives, gathered(): lax.all_to_all(copies, axis, split_axis=0, concat_axis=0, axis_index_grou...  22.3 us
    ppermute x3, waiting for transfers between devices, from_both(): lax.ppermute(up_value, axis, up)  9.21 us
    ppermute x3, starting transfers between devices, from_both(): lax.ppermute(up_value, axis, up)  9.13 us
    ppermute x3, starting transfers between devices, from_both(): lax.ppermute(down_value, axis, [(b, a) for a, b in up])  8.96 us
    ppermute x3, starting transfers between devices, from_both_round(): lax.ppermute(down_value, axis, [(b, a) for a, b in up])  8.35 us
    ppermute x3, waiting for transfers between devices, from_both(): lax.ppermute(down_value, axis, [(b, a) for a, b in up])  7.04 us
    ppermute x3, waiting for transfers between devices, from_both_round(): lax.ppermute(up_value, axis, up)  4.93 us
    pallas_call x1, Pallas kernels, local(): call(functools.partial(up_kernel, n), [(8, 64, 128)], [colour2, colour2,...  4.87 us
  transfers between devices with their start and end apart: 13, of which 7 were waited for; matrix products, arithmetic and copies ran while one was open for 0% of the time, Pallas kernels for 0%

profile of v4, /device:TPU:128, one launch (start us, length us, event | category | flops | bytes accessed | tf_op | source)
XLA Modules:
  0.0 87.8 jit_solution(14352200393027730204)
XLA Ops:
  0.0 0.0 copy-start
  0.0 0.9 %copy-done = f32[8,64,128]{2,1,0:T(8,128)S(1)} copy-done((f32[8,64,128]{2,1,0:T(8,128)S(1)}, f32[8,64,128]{2,1,0:T(8,128)}, u32[]{:S(2)}) %copy-start) | copy-done | bytes 262168
  1.0 0.0 copy-start.1
  1.0 0.9 %copy-done.1 = f32[8,64,128]{2,1,0:T(8,128)S(1)} copy-done((f32[8,64,128]{2,1,0:T(8,128)S(1)}, f32[8,64,128]{2,1,0:T(8,128)}, u32[]{:S(2)}) %copy-start.1) | copy-done | bytes 262168
  1.9 0.2 shard_map.28
  2.1 2.5 %collective-permute-start.5 = (f32[12,64,128]{2,1,0:T(8,128)S(1)}, f32[12,64,128]{2,1,0:T(8,128)S(1)}, u32[]{:S(2)}, u32[]{:S(2)}) collective-permute-start(f32[12,64,128]{2,1,0:T(8,128)S(1)} %get-tuple-element.28.s), channel_id=1, source_target_pairs={{64,0},{128,64},{192,128},{256,192},{320,256},{384,320},{448,384},... | collective-permute-start | bytes 1179656 | tf_op jit(solution)/shard_map/ppermute | solution.py:547
  4.6 3.8 %collective-permute-start = (f32[6,64,128]{2,1,0:T(8,128)S(1)}, f32[6,64,128]{2,1,0:T(8,128)S(1)}, u32[]{:S(2)}, u32[]{:S(2)}) collective-permute-start(f32[6,64,128]{2,1,0:T(8,128)S(1)} %get-tuple-element.29), channel_id=1, source_target_pairs={{0,1},{1,2},{2,3},{3,4},{4,5},{5,6},{6,7},{7,8},{8,9},{9,10},{10,1... | collective-permute-start | bytes 589832 | tf_op jit(solution)/shard_map/ppermute | solution.py:541
  8.4 3.2 %collective-permute-start.1 = (f32[6,64,128]{2,1,0:T(8,128)S(1)}, f32[6,64,128]{2,1,0:T(8,128)S(1)}, u32[]{:S(2)}, u32[]{:S(2)}) collective-permute-start(f32[6,64,128]{2,1,0:T(8,128)S(1)} %get-tuple-element.30), channel_id=1, source_target_pairs={{1,0},{2,1},{3,2},{4,3},{5,4},{6,5},{7,6},{8,7},{9,8},{10,9},{11,1... | collective-permute-start | bytes 589832 | tf_op jit(solution)/shard_map/ppermute | solution.py:541
  11.6 0.0 collective-permute-start.4
  11.6 1.7 %collective-permute-done.up = f32[6,64,128]{2,1,0:T(8,128)S(1)} collective-permute-done((f32[6,64,128]{2,1,0:T(8,128)S(1)}, f32[6,64,128]{2,1,0:T(8,128)S(1)}, u32[]{:S(2)}, u32[]{:S(2)}) %collective-permute-start) | collective-permute-done | bytes 196640 | tf_op jit(solution)/shard_map/ppermute | solution.py:541
  13.3 2.6 %collective-permute-done.1.down = f32[6,64,128]{2,1,0:T(8,128)S(1)} collective-permute-done((f32[6,64,128]{2,1,0:T(8,128)S(1)}, f32[6,64,128]{2,1,0:T(8,128)S(1)}, u32[]{:S(2)}, u32[]{:S(2)}) %collective-permute-start.1) | collective-permute-done | bytes 196640 | tf_op jit(solution)/shard_map/ppermute | solution.py:541
  15.9 0.3 shard_map.29
  16.2 0.0 collective-permute-start.6
  16.3 2.9 %collective-permute-start.7 = (f32[8,64,128]{2,1,0:T(8,128)S(1)}, f32[8,64,128]{2,1,0:T(8,128)S(1)}, u32[]{:S(2)}, u32[]{:S(2)}) collective-permute-start(f32[8,64,128]{2,1,0:T(8,128)S(1)} %get-tuple-element.35), channel_id=1, source_target_pairs={{64,0},{128,64},{192,128},{256,192},{320,256},{384,320},{448,384},... | collective-permute-start | bytes 786440 | tf_op jit(solution)/shard_map/ppermute | solution.py:547
  19.2 3.4 %collective-permute-start.2 = (f32[496,128]{1,0:T(8,128)S(1)}, f32[496,128]{1,0:T(8,128)S(1)}, u32[]{:S(2)}, u32[]{:S(2)}) collective-permute-start(f32[496,128]{1,0:T(8,128)S(1)} %get-tuple-element.32), channel_id=1, source_target_pairs={{0,16},{16,32},{32,48},{1,17},{17,33},{33,49},{2,18},{18,34},{34,5... | collective-permute-start | bytes 761864 | tf_op jit(solution)/shard_map/ppermute | solution.py:541
  22.6 0.0 collective-permute-done.5.rest_1_.s_right
  22.6 1.3 %collective-permute-start.3 = (f32[496,128]{1,0:T(8,128)S(1)}, f32[496,128]{1,0:T(8,128)S(1)}, u32[]{:S(2)}, u32[]{:S(2)}) collective-permute-start(f32[496,128]{1,0:T(8,128)S(1)} %get-tuple-element.33), channel_id=1, source_target_pairs={{16,0},{32,16},{48,32},{17,1},{33,17},{49,33},{18,2},{34,18},{50,3... | collective-permute-start | bytes 761864 | tf_op jit(solution)/shard_map/ppermute | solution.py:541
  23.9 0.0 collective-permute-done.4.rest_0_.s_left
  23.9 2.4 %collective-permute-done.2.before = f32[496,128]{1,0:T(8,128)S(1)} collective-permute-done((f32[496,128]{1,0:T(8,128)S(1)}, f32[496,128]{1,0:T(8,128)S(1)}, u32[]{:S(2)}, u32[]{:S(2)}) %collective-permute-start.2) | collective-permute-done | bytes 253984 | tf_op jit(solution)/shard_map/ppermute | solution.py:541
  26.4 4.4 %collective-permute-done.3.after = f32[496,128]{1,0:T(8,128)S(1)} collective-permute-done((f32[496,128]{1,0:T(8,128)S(1)}, f32[496,128]{1,0:T(8,128)S(1)}, u32[]{:S(2)}, u32[]{:S(2)}) %collective-permute-start.3) | collective-permute-done | bytes 253984 | tf_op jit(solution)/shard_map/ppermute | solution.py:541
  30.8 0.0 collective-permute-done.6.rest_2_.v_left
  30.8 0.0 collective-permute-done.7.rest_3_.v_right
  30.8 0.1 shard_map.30
  30.9 0.0 collective-permute-start.8
  30.9 2.9 %collective-permute-start.9 = (f32[672,128]{1,0:T(8,128)S(1)}, f32[672,128]{1,0:T(8,128)S(1)}, u32[]{:S(2)}, u32[]{:S(2)}) collective-permute-start(f32[672,128]{1,0:T(8,128)S(1)} %get-tuple-element.37), channel_id=1, source_target_pairs={{64,0},{128,64},{192,128},{256,192},{320,256},{384,320},{448,384},... | collective-permute-start | bytes 1032200 | tf_op jit(solution)/shard_map/ppermute | solution.py:547
  33.9 4.9 %collective-permute-done.8.y_left = f32[672,128]{1,0:T(8,128)S(1)} collective-permute-done((f32[672,128]{1,0:T(8,128)S(1)}, f32[672,128]{1,0:T(8,128)S(1)}, u32[]{:S(2)}, u32[]{:S(2)}) %collective-permute-start.8) | collective-permute-done | bytes 344096 | tf_op jit(solution)/shard_map/ppermute | solution.py:547
  38.8 0.0 collective-permute-done.9.y_right
  38.8 4.2 %shard_map.31 = (f32[4,56,128]{2,1,0:T(8,128)S(1)}, f32[200,128]{1,0:T(8,128)S(1)}, f32[8,80,256]{2,1,0:T(8,128)S(1)}, f32[8,80,256]{2,1,0:T(8,128)S(1)}, f32[8,80,256]{2,1,0:T(8,128)S(1)}) custom-call(f32[12,64,128]{2,1,0:T(8,128)S(1)} %get-tuple-element.28.s, f32[12,64,128]{2,1,0:T(8,128)S(1)} %get-tuple-element.31.v, ...), custom_call_target="tpu_custom_call" | custom-call | tf_op jit(solution)/shard_map/pallas_call | solution.py:574
  43.1 11.3 %all_to_all.10 = f32[4,1,200,128]{3,2,1,0:T(8,128)S(1)} all-to-all(f32[4,1,200,128]{3,2,1,0:T(8,128)S(1)} %broadcast_in_dim.7), channel_id=1, replica_groups={{0,128,256,384},{64,192,320,448},{1,129,257,385},{65,193,321,449},{2,13..., dimensions={0} | all-to-all | bytes 819200 | tf_op jit(solution)/shard_map/all_to_all | solution.py:553
  54.3 2.5 %collective-permute-start.10 = (f32[4,1,200,128]{3,2,0,1:T(8,128)S(1)}, f32[4,1,200,128]{3,2,0,1:T(8,128)S(1)}, u32[]{:S(2)}, u32[]{:S(2)}) collective-permute-start(f32[4,1,200,128]{3,2,0,1:T(8,128)S(1)} %bitcast.3), channel_id=1, source_target_pairs={{0,64},{64,0},{128,192},{192,128},{256,320},{320,256},{384,448},{4... | collective-permute-start | bytes 1228808 | tf_op jit(solution)/shard_map/ppermute | solution.py:581
  56.8 1.4 %collective-permute-done.10 = f32[4,1,200,128]{3,2,0,1:T(8,128)S(1)} collective-permute-done((f32[4,1,200,128]{3,2,0,1:T(8,128)S(1)}, f32[4,1,200,128]{3,2,0,1:T(8,128)S(1)}, u32[]{:S(2)}, u32[]{:S(2)}) %collective-permute-start.10) | collective-permute-done | bytes 409632 | tf_op jit(solution)/shard_map/ppermute | solution.py:581
  58.2 1.5 %shard_map.32 = (f32[8,16,128]{2,1,0:T(8,128)S(1)}, f32[8,56,128]{2,1,0:T(8,128)S(1)}, f32[8,56,128]{2,1,0:T(8,128)S(1)}, f32[8,56,128]{2,1,0:T(8,128)S(1)}) custom-call(f32[4,56,128]{2,1,0:T(8,128)S(1)} %get-tuple-element.38.own, f32[4,200,128]{2,1,0:T(8,128)S(1)} %bitcast.4, f32[4,200,128]{2,1,0:T(8,128)S(1)} %bitcast.5), custom_call_target="tpu_custom_call" | custom-call | tf_op jit(solution)/shard_map/pallas_call | solution.py:586
  59.7 11.0 %all_to_all.11.b2 = f32[4,8,16,128]{3,2,1,0:T(8,128)S(1)} all-to-all(f32[4,8,16,128]{3,2,1,0:T(8,128)S(1)} %broadcast_in_dim.8), channel_id=1, replica_groups=mesh['gx'=8,'gy'=4,'gz'=16] {'gy'}, dimensions={0} | all-to-all | bytes 524288 | tf_op jit(solution)/shard_map/all_to_all | solution.py:553
  70.7 0.8 shard_map.33
  71.5 4.4 %collective-permute-start.12 = (f32[2,32,128]{2,1,0:T(8,128)S(1)}, f32[2,32,128]{2,1,0:T(8,128)S(1)}, u32[]{:S(2)}, u32[]{:S(2)}) collective-permute-start(f32[2,32,128]{2,1,0:T(8,128)S(1)} %get-tuple-element.41.b3), channel_id=1, source_target_pairs={{1,0},{2,1},{3,2},{4,3},{5,4},{6,5},{7,6},{8,7},{9,8},{10,9},{11,1... | collective-permute-start | bytes 98312 | tf_op jit(solution)/shard_map/ppermute | solution.py:541
  75.9 1.9 %collective-permute-start.11 = (f32[2,32,128]{2,1,0:T(8,128)S(1)}, f32[2,32,128]{2,1,0:T(8,128)S(1)}, u32[]{:S(2)}, u32[]{:S(2)}) collective-permute-start(f32[2,32,128]{2,1,0:T(8,128)S(1)} %get-tuple-element.41.b3), channel_id=1, source_target_pairs={{0,1},{1,2},{2,3},{3,4},{4,5},{5,6},{6,7},{7,8},{8,9},{9,10},{10,1... | collective-permute-start | bytes 98312 | tf_op jit(solution)/shard_map/ppermute | solution.py:541
  77.8 0.0 collective-permute-done.12.b3_right
  77.9 5.1 %collective-permute-done.11.b3_left = f32[2,32,128]{2,1,0:T(8,128)S(1)} collective-permute-done((f32[2,32,128]{2,1,0:T(8,128)S(1)}, f32[2,32,128]{2,1,0:T(8,128)S(1)}, u32[]{:S(2)}, u32[]{:S(2)}) %collective-permute-start.11) | collective-permute-done | bytes 32800 | tf_op jit(solution)/shard_map/ppermute | solution.py:541
  82.9 4.9 %shard_map.34 = f32[8,64,128]{2,1,0:T(8,128)} custom-call(f32[2,32,128]{2,1,0:T(8,128)S(1)} %get-tuple-element.41.b3, f32[2,32,128]{2,1,0:T(8,128)S(1)} %collective-permute-done.11.b3_left, f32[2,32,128]{2,1,0:T(8,128)S(1)} %collective-permute-done.12.b3_right, f32[4,64,128]{2,1,0:T(8,128)S(1)} %get-tuple-element.42.start2, ...), custom_call_target="tpu_custom_call" | custom-call | tf_op jit(solution)/shard_map/pallas_call | solution.py:601
  (2 shorter events, 0.0 us)
Async XLA Ops:
  0.0 0.9 %copy-start = (f32[8,64,128]{2,1,0:T(8,128)S(1)}, f32[8,64,128]{2,1,0:T(8,128)}, u32[]{:S(2)}) copy-start(f32[8,64,128]{2,1,0:T(8,128)} %start_hbm.1) | copy-start | bytes 786436
  1.0 0.9 %copy-start.1 = (f32[8,64,128]{2,1,0:T(8,128)S(1)}, f32[8,64,128]{2,1,0:T(8,128)}, u32[]{:S(2)}) copy-start(f32[8,64,128]{2,1,0:T(8,128)} %right_hbm.1) | copy-start | bytes 786436
  2.1 20.5 %collective-permute-start.5 = (f32[12,64,128]{2,1,0:T(8,128)S(1)}, f32[12,64,128]{2,1,0:T(8,128)S(1)}, u32[]{:S(2)}, u32[]{:S(2)}) collective-permute-start(f32[12,64,128]{2,1,0:T(8,128)S(1)} %get-tuple-element.28.s), channel_id=1, source_target_pairs={{64,0},{128,64},{192,128},{256,192},{320,256},{384,320},{448,384},... | collective-permute-start | bytes 1179656 | tf_op jit(solution)/shard_map/ppermute | solution.py:547
  4.6 8.8 %collective-permute-start = (f32[6,64,128]{2,1,0:T(8,128)S(1)}, f32[6,64,128]{2,1,0:T(8,128)S(1)}, u32[]{:S(2)}, u32[]{:S(2)}) collective-permute-start(f32[6,64,128]{2,1,0:T(8,128)S(1)} %get-tuple-element.29), channel_id=1, source_target_pairs={{0,1},{1,2},{2,3},{3,4},{4,5},{5,6},{6,7},{7,8},{8,9},{9,10},{10,1... | collective-permute-start | bytes 589832 | tf_op jit(solution)/shard_map/ppermute | solution.py:541
  8.4 7.6 %collective-permute-start.1 = (f32[6,64,128]{2,1,0:T(8,128)S(1)}, f32[6,64,128]{2,1,0:T(8,128)S(1)}, u32[]{:S(2)}, u32[]{:S(2)}) collective-permute-start(f32[6,64,128]{2,1,0:T(8,128)S(1)} %get-tuple-element.30), channel_id=1, source_target_pairs={{1,0},{2,1},{3,2},{4,3},{5,4},{6,5},{7,6},{8,7},{9,8},{10,9},{11,1... | collective-permute-start | bytes 589832 | tf_op jit(solution)/shard_map/ppermute | solution.py:541
  11.6 12.3 %collective-permute-start.4 = (f32[12,64,128]{2,1,0:T(8,128)S(1)}, f32[12,64,128]{2,1,0:T(8,128)S(1)}, u32[]{:S(2)}, u32[]{:S(2)}) collective-permute-start(f32[12,64,128]{2,1,0:T(8,128)S(1)} %get-tuple-element.28.s), channel_id=1, source_target_pairs={{0,64},{64,128},{128,192},{192,256},{256,320},{320,384},{384,448},... | collective-permute-start | bytes 1179656 | tf_op jit(solution)/shard_map/ppermute | solution.py:547
  16.2 14.6 %collective-permute-start.6 = (f32[8,64,128]{2,1,0:T(8,128)S(1)}, f32[8,64,128]{2,1,0:T(8,128)S(1)}, u32[]{:S(2)}, u32[]{:S(2)}) collective-permute-start(f32[8,64,128]{2,1,0:T(8,128)S(1)} %get-tuple-element.34), channel_id=1, source_target_pairs={{0,64},{64,128},{128,192},{192,256},{256,320},{320,384},{384,448},... | collective-permute-start | bytes 786440 | tf_op jit(solution)/shard_map/ppermute | solution.py:547
  16.3 14.5 %collective-permute-start.7 = (f32[8,64,128]{2,1,0:T(8,128)S(1)}, f32[8,64,128]{2,1,0:T(8,128)S(1)}, u32[]{:S(2)}, u32[]{:S(2)}) collective-permute-start(f32[8,64,128]{2,1,0:T(8,128)S(1)} %get-tuple-element.35), channel_id=1, source_target_pairs={{64,0},{128,64},{192,128},{256,192},{320,256},{384,320},{448,384},... | collective-permute-start | bytes 786440 | tf_op jit(solution)/shard_map/ppermute | solution.py:547
  19.2 7.2 %collective-permute-start.2 = (f32[496,128]{1,0:T(8,128)S(1)}, f32[496,128]{1,0:T(8,128)S(1)}, u32[]{:S(2)}, u32[]{:S(2)}) collective-permute-start(f32[496,128]{1,0:T(8,128)S(1)} %get-tuple-element.32), channel_id=1, source_target_pairs={{0,16},{16,32},{32,48},{1,17},{17,33},{33,49},{2,18},{18,34},{34,5... | collective-permute-start | bytes 761864 | tf_op jit(solution)/shard_map/ppermute | solution.py:541
  22.6 8.2 %collective-permute-start.3 = (f32[496,128]{1,0:T(8,128)S(1)}, f32[496,128]{1,0:T(8,128)S(1)}, u32[]{:S(2)}, u32[]{:S(2)}) collective-permute-start(f32[496,128]{1,0:T(8,128)S(1)} %get-tuple-element.33), channel_id=1, source_target_pairs={{16,0},{32,16},{48,32},{17,1},{33,17},{49,33},{18,2},{34,18},{50,3... | collective-permute-start | bytes 761864 | tf_op jit(solution)/shard_map/ppermute | solution.py:541
  30.9 7.9 %collective-permute-start.8 = (f32[672,128]{1,0:T(8,128)S(1)}, f32[672,128]{1,0:T(8,128)S(1)}, u32[]{:S(2)}, u32[]{:S(2)}) collective-permute-start(f32[672,128]{1,0:T(8,128)S(1)} %get-tuple-element.36), channel_id=1, source_target_pairs={{0,64},{64,128},{128,192},{192,256},{256,320},{320,384},{384,448},... | collective-permute-start | bytes 1032200 | tf_op jit(solution)/shard_map/ppermute | solution.py:547
  30.9 7.9 %collective-permute-start.9 = (f32[672,128]{1,0:T(8,128)S(1)}, f32[672,128]{1,0:T(8,128)S(1)}, u32[]{:S(2)}, u32[]{:S(2)}) collective-permute-start(f32[672,128]{1,0:T(8,128)S(1)} %get-tuple-element.37), channel_id=1, source_target_pairs={{64,0},{128,64},{192,128},{256,192},{320,256},{384,320},{448,384},... | collective-permute-start | bytes 1032200 | tf_op jit(solution)/shard_map/ppermute | solution.py:547
  54.3 3.8 %collective-permute-start.10 = (f32[4,1,200,128]{3,2,0,1:T(8,128)S(1)}, f32[4,1,200,128]{3,2,0,1:T(8,128)S(1)}, u32[]{:S(2)}, u32[]{:S(2)}) collective-permute-start(f32[4,1,200,128]{3,2,0,1:T(8,128)S(1)} %bitcast.3), channel_id=1, source_target_pairs={{0,64},{64,0},{128,192},{192,128},{256,320},{320,256},{384,448},{4... | collective-permute-start | bytes 1228808 | tf_op jit(solution)/shard_map/ppermute | solution.py:581
  71.5 6.4 %collective-permute-start.12 = (f32[2,32,128]{2,1,0:T(8,128)S(1)}, f32[2,32,128]{2,1,0:T(8,128)S(1)}, u32[]{:S(2)}, u32[]{:S(2)}) collective-permute-start(f32[2,32,128]{2,1,0:T(8,128)S(1)} %get-tuple-element.41.b3), channel_id=1, source_target_pairs={{1,0},{2,1},{3,2},{4,3},{5,4},{6,5},{7,6},{8,7},{9,8},{10,9},{11,1... | collective-permute-start | bytes 98312 | tf_op jit(solution)/shard_map/ppermute | solution.py:541
  75.9 7.0 %collective-permute-start.11 = (f32[2,32,128]{2,1,0:T(8,128)S(1)}, f32[2,32,128]{2,1,0:T(8,128)S(1)}, u32[]{:S(2)}, u32[]{:S(2)}) collective-permute-start(f32[2,32,128]{2,1,0:T(8,128)S(1)} %get-tuple-element.41.b3), channel_id=1, source_target_pairs={{0,1},{1,2},{2,3},{3,4},{4,5},{5,6},{6,7},{7,8},{8,9},{9,10},{10,1... | collective-permute-start | bytes 98312 | tf_op jit(solution)/shard_map/ppermute | solution.py:541

commit v5 on v4

--- a/solution.py
+++ b/solution.py
@@ -143,10 +143,11 @@
 STRIP_AT = 48 * NEAR
 FAR_AT = STRIP_AT + 32 * NEAR
 PACKED_AT = FAR_AT + 16 * FAR
-CROSS_X = PACKED_AT + 2 * 16
-
-
-def widen_kernel(s, up, down, v, v_up, v_down, first, last):
+WHOLE_AT = PACKED_AT + 2 * 16
+CROSS_X = WHOLE_AT + 64 * (NEAR + 1)
+
+
+def widen_kernel(s, up, down, v, first, last):
     low = lane_of((64, 128)) < 64
     for p in range(6):
         v[p] = jnp.where(low, down[p], up[p])
@@ -161,17 +162,14 @@
         at = 480 + 8 * t
         first[at : at + 8] = pack16([v[6 * t + k, 16:24] for k in range(6)])
         last[at : at + 8] = pack16([v[6 * t + k, 40:48] for k in range(6)])
-    for ref, near, far in ((v_up, UP_NEAR, UP_FAR), (v_down, DOWN_NEAR, DOWN_FAR)):
-        for k, p in enumerate(near):
-            ref[k] = v[p]
-        ref[NEAR] = pack16([v[p] for p in far])
-
-
-def strips_kernel(before, after, *rest):
+
+
+def strips_kernel(v, before, after, *rest):
     lanes = lane_of((8, 128))
     for ref, near, far in ((rest[-2], UP_NEAR, UP_FAR), (rest[-1], DOWN_NEAR, DOWN_FAR)):
         outer = [jnp.zeros((8, 128), F32), jnp.zeros((8, 128), F32)]
         for k, p in enumerate(near):
+            ref[WHOLE_AT + 64 * k : WHOLE_AT + 64 * k + 64] = v[p]
             ref[48 * k : 48 * k + 24] = before[24 * p : 24 * p + 24]
             ref[48 * k + 24 : 48 * k + 48] = after[24 * p : 24 * p + 24]
             at, inner = STRIP_AT + 32 * k, 288 + 16 * p
@@ -182,6 +180,7 @@
                 plane = strip[at : at + 8]
                 plane = pltpu.roll(plane, shift, 1) if shift else plane
                 outer[h] = jnp.where((lanes >= 16 * k) & (lanes < 16 * k + 16), plane, outer[h])
+        ref[WHOLE_AT + 64 * NEAR :] = pack16([v[p] for p in far])
         edges = [[], []]
         for k, p in enumerate(far):
             at, inner = FAR_AT + 16 * k, 288 + 16 * p
@@ -196,7 +195,7 @@
 
 
 def fine_down_kernel(
-    n, s, v, before, after, s_left, s_right, v_left, v_right, y_left, y_right,
+    n, s, v, before, after, s_left, s_right, y_left, y_right,
     coarse, sent, black_out, red_b_out, black_b_out, red, black, rb, bb, weight, pairs,
 ):
     gx, gy, gz = (lax.axis_index(a) for a in ("gx", "gy", "gz"))
@@ -230,13 +229,13 @@
             at = 480 + 8 * (j // 6)
             put(i, 0, strip, unpack16(before[at : at + 8], j % 6))
             put(i, EY + 80, strip, unpack16(after[at : at + 8], j % 6))
-        sides = ((0, UP_NEAR, UP_FAR, v_left, y_left, has_left), (8, DOWN_NEAR, DOWN_FAR, v_right, y_right, has_right))
-        for base, near, far, strips, y, there in sides:
+        sides = ((0, UP_NEAR, UP_FAR, y_left, has_left), (8, DOWN_NEAR, DOWN_FAR, y_right, has_right))
+        for base, near, far, y, there in sides:
             for k, p in enumerate(near):
                 if p // 4 != a:
                     continue
                 i = base + p % 4
-                put(i, EY, strip, strips[k], there)
+                put(i, EY, strip, y[WHOLE_AT + 64 * k : WHOLE_AT + 64 * k + 64], there)
                 put(i, 0, block, y[48 * k : 48 * k + 24], there)
                 put(i, EY + 64, block, y[48 * k + 24 : 48 * k + 48], there)
                 at = STRIP_AT + 32 * k
@@ -248,7 +247,7 @@
                 if p // 4 != a:
                     continue
                 i = base + p % 4
-                put(i, EY, strip, unpack16(strips[NEAR], k), there)
+                put(i, EY, strip, unpack16(y[WHOLE_AT + 64 * NEAR :], k), there)
                 at = FAR_AT + 16 * k
                 put(i, 16, block, y[at : at + 8], there)
                 put(i, EY + 64, block, y[at + 8 : at + 16], there)
@@ -563,19 +562,16 @@
     )(start, right_side)
     up, down = from_both(up, down, "gz")
     s_left, s_right = from_both_round(s, s, "gx")
-    v, v_up, v_down, first, last = call(
-        widen_kernel, [(12, 64, 128), (NEAR + 1, 64, 128), (NEAR + 1, 64, 128), (CROSS_Y, 128), (CROSS_Y, 128)]
-    )(s, up, down)
-    v_left, v_right = from_both_round(v_up, v_down, "gx")
+    v, first, last = call(widen_kernel, [(12, 64, 128), (CROSS_Y, 128), (CROSS_Y, 128)])(s, up, down)
     before, after = from_both(last, first, "gy")
-    up, down = call(strips_kernel, [(CROSS_X, 128)] * 2)(before, after, s_left, s_right, v_left, v_right)
+    up, down = call(strips_kernel, [(CROSS_X, 128)] * 2)(v, before, after, s_left, s_right)
     y_left, y_right = from_both_round(up, down, "gx")
     up0 = (8, 80, 256)
     b1, sent, black0, red_b0, black_b0 = call(
         functools.partial(fine_down_kernel, n),
         [(4, ROWS1, 128), (4 * SENT1, 128), up0, up0, up0],
         [(14, ROWS0 + 2 * PAD, 256)] * 2 + [(12, ROWS0, 256)] * 2 + [(3, ROWS0, 256), (8, ROWS0, 128)],
-    )(s, v, before, after, s_left, s_right, v_left, v_right, y_left, y_right)
+    )(s, v, before, after, s_left, s_right, y_left, y_right)
     groups = [[2 * chip + core for chip in range(n[0] // 2)] for core in range(2)]
     same = gathered(sent[None], "gx", groups)
     other = lax.ppermute(same, "gx", [(i, i ^ 1) for i in range(n[0])])

time: 88.2 us -> 87.2 us (0.989)
  the two profiles are of different devices: /device:TPU:128 before, /device:TPU:256 now
where the time goes in v5:
time: 87.2 us; the launch traced here: 86.8 us
  starting transfers between devices  25.9 us (30%)
  waiting for transfers between devices  23.6 us (27%)
  blocking collectives  23.3 us (27%)
  Pallas kernels  11.9 us (14%)
  local copies, waits for them, and re-layouts  1.95 us (2%)
    all_to_all x2, blocking collectives, gathered(): lax.all_to_all(copies, axis, split_axis=0, concat_axis=0, axis_index_grou...  23.3 us
    ppermute x3, starting transfers between devices, from_both(): lax.ppermute(down_value, axis, [(b, a) for a, b in up])  10.8 us
    ppermute x2, waiting for transfers between devices, from_both_round(): lax.ppermute(up_value, axis, up)  9.05 us
    ppermute x3, starting transfers between devices, from_both(): lax.ppermute(up_value, axis, up)  8.26 us
    ppermute x3, waiting for transfers between devices, from_both(): lax.ppermute(up_value, axis, up)  7.39 us
    ppermute x3, waiting for transfers between devices, from_both(): lax.ppermute(down_value, axis, [(b, a) for a, b in up])  5.57 us
    pallas_call x1, Pallas kernels, local(): call(functools.partial(up_kernel, n), [(8, 64, 128)], [colour2, colour2,...  4.87 us
    ppermute x2, starting transfers between devices, from_both_round(): lax.ppermute(down_value, axis, [(b, a) for a, b in up])  4.85 us
  transfers between devices with their start and end apart: 11, of which 8 were waited for; matrix products, arithmetic and copies ran while one was open for 0% of the time, Pallas kernels for 0%

profile of v5, /device:TPU:256, one launch (start us, length us, event | category | flops | bytes accessed | tf_op | source)
XLA Modules:
  0.0 86.8 jit_solution(1669157960287065438)
XLA Ops:
  0.0 0.0 copy-start
  0.0 0.9 %copy-done = f32[8,64,128]{2,1,0:T(8,128)S(1)} copy-done((f32[8,64,128]{2,1,0:T(8,128)S(1)}, f32[8,64,128]{2,1,0:T(8,128)}, u32[]{:S(2)}) %copy-start) | copy-done | bytes 262168
  1.0 0.0 copy-start.1
  1.0 0.9 %copy-done.1 = f32[8,64,128]{2,1,0:T(8,128)S(1)} copy-done((f32[8,64,128]{2,1,0:T(8,128)S(1)}, f32[8,64,128]{2,1,0:T(8,128)}, u32[]{:S(2)}) %copy-start.1) | copy-done | bytes 262168
  1.9 0.2 shard_map.28
  2.1 2.9 %collective-permute-start = (f32[6,64,128]{2,1,0:T(8,128)S(1)}, f32[6,64,128]{2,1,0:T(8,128)S(1)}, u32[]{:S(2)}, u32[]{:S(2)}) collective-permute-start(f32[6,64,128]{2,1,0:T(8,128)S(1)} %get-tuple-element.27), channel_id=1, source_target_pairs={{0,1},{1,2},{2,3},{3,4},{4,5},{5,6},{6,7},{7,8},{8,9},{9,10},{10,1... | collective-permute-start | bytes 589832 | tf_op jit(solution)/shard_map/ppermute | solution.py:540
  5.0 4.1 %collective-permute-start.1 = (f32[6,64,128]{2,1,0:T(8,128)S(1)}, f32[6,64,128]{2,1,0:T(8,128)S(1)}, u32[]{:S(2)}, u32[]{:S(2)}) collective-permute-start(f32[6,64,128]{2,1,0:T(8,128)S(1)} %get-tuple-element.28), channel_id=1, source_target_pairs={{1,0},{2,1},{3,2},{4,3},{5,4},{6,5},{7,6},{8,7},{9,8},{10,9},{11,1... | collective-permute-start | bytes 589832 | tf_op jit(solution)/shard_map/ppermute | solution.py:540
  9.2 1.9 %collective-permute-start.5 = (f32[12,64,128]{2,1,0:T(8,128)S(1)}, f32[12,64,128]{2,1,0:T(8,128)S(1)}, u32[]{:S(2)}, u32[]{:S(2)}) collective-permute-start(f32[12,64,128]{2,1,0:T(8,128)S(1)} %get-tuple-element.26.s), channel_id=1, source_target_pairs={{64,0},{128,64},{192,128},{256,192},{320,256},{384,320},{448,384},... | collective-permute-start | bytes 1179656 | tf_op jit(solution)/shard_map/ppermute | solution.py:546
  11.1 0.0 collective-permute-start.4
  11.1 0.8 collective-permute-done.up
  11.8 1.4 %collective-permute-done.1.down = f32[6,64,128]{2,1,0:T(8,128)S(1)} collective-permute-done((f32[6,64,128]{2,1,0:T(8,128)S(1)}, f32[6,64,128]{2,1,0:T(8,128)S(1)}, u32[]{:S(2)}, u32[]{:S(2)}) %collective-permute-start.1) | collective-permute-done | bytes 196640 | tf_op jit(solution)/shard_map/ppermute | solution.py:540
  13.3 0.2 shard_map.29
  13.4 3.4 %collective-permute-start.2 = (f32[496,128]{1,0:T(8,128)S(1)}, f32[496,128]{1,0:T(8,128)S(1)}, u32[]{:S(2)}, u32[]{:S(2)}) collective-permute-start(f32[496,128]{1,0:T(8,128)S(1)} %get-tuple-element.30), channel_id=1, source_target_pairs={{0,16},{16,32},{32,48},{1,17},{17,33},{33,49},{2,18},{18,34},{34,5... | collective-permute-start | bytes 761864 | tf_op jit(solution)/shard_map/ppermute | solution.py:540
  16.9 1.3 %collective-permute-start.3 = (f32[496,128]{1,0:T(8,128)S(1)}, f32[496,128]{1,0:T(8,128)S(1)}, u32[]{:S(2)}, u32[]{:S(2)}) collective-permute-start(f32[496,128]{1,0:T(8,128)S(1)} %get-tuple-element.31), channel_id=1, source_target_pairs={{16,0},{32,16},{48,32},{17,1},{33,17},{49,33},{18,2},{34,18},{50,3... | collective-permute-start | bytes 761864 | tf_op jit(solution)/shard_map/ppermute | solution.py:540
  18.2 0.0 collective-permute-done.5.rest_1_.s_right
  18.2 1.3 %collective-permute-done.4.rest_0_.s_left = f32[12,64,128]{2,1,0:T(8,128)S(1)} collective-permute-done((f32[12,64,128]{2,1,0:T(8,128)S(1)}, f32[12,64,128]{2,1,0:T(8,128)S(1)}, u32[]{:S(2)}, u32[]{:S(2)}) %collective-permute-start.4) | collective-permute-done | bytes 393248 | tf_op jit(solution)/shard_map/ppermute | solution.py:546
  19.5 1.5 %collective-permute-done.2.before = f32[496,128]{1,0:T(8,128)S(1)} collective-permute-done((f32[496,128]{1,0:T(8,128)S(1)}, f32[496,128]{1,0:T(8,128)S(1)}, u32[]{:S(2)}, u32[]{:S(2)}) %collective-permute-start.2) | collective-permute-done | bytes 253984 | tf_op jit(solution)/shard_map/ppermute | solution.py:540
  21.0 4.1 %collective-permute-done.3.after = f32[496,128]{1,0:T(8,128)S(1)} collective-permute-done((f32[496,128]{1,0:T(8,128)S(1)}, f32[496,128]{1,0:T(8,128)S(1)}, u32[]{:S(2)}, u32[]{:S(2)}) %collective-permute-start.3) | collective-permute-done | bytes 253984 | tf_op jit(solution)/shard_map/ppermute | solution.py:540
  25.2 0.2 shard_map.30
  25.4 0.0 collective-permute-start.6
  25.4 2.9 %collective-permute-start.7 = (f32[1184,128]{1,0:T(8,128)S(1)}, f32[1184,128]{1,0:T(8,128)S(1)}, u32[]{:S(2)}, u32[]{:S(2)}) collective-permute-start(f32[1184,128]{1,0:T(8,128)S(1)} %get-tuple-element.33), channel_id=1, source_target_pairs={{64,0},{128,64},{192,128},{256,192},{320,256},{384,320},{448,384},... | collective-permute-start | bytes 1818632 | tf_op jit(solution)/shard_map/ppermute | solution.py:546
  28.3 7.7 %collective-permute-done.6.y_left = f32[1184,128]{1,0:T(8,128)S(1)} collective-permute-done((f32[1184,128]{1,0:T(8,128)S(1)}, f32[1184,128]{1,0:T(8,128)S(1)}, u32[]{:S(2)}, u32[]{:S(2)}) %collective-permute-start.6) | collective-permute-done | bytes 606240 | tf_op jit(solution)/shard_map/ppermute | solution.py:546
  36.1 0.0 collective-permute-done.7.y_right
  36.1 4.2 %shard_map.31 = (f32[4,56,128]{2,1,0:T(8,128)S(1)}, f32[200,128]{1,0:T(8,128)S(1)}, f32[8,80,256]{2,1,0:T(8,128)S(1)}, f32[8,80,256]{2,1,0:T(8,128)S(1)}, f32[8,80,256]{2,1,0:T(8,128)S(1)}) custom-call(f32[12,64,128]{2,1,0:T(8,128)S(1)} %get-tuple-element.26.s, f32[12,64,128]{2,1,0:T(8,128)S(1)} %get-tuple-element.29.v, ...), custom_call_target="tpu_custom_call" | custom-call | tf_op jit(solution)/shard_map/pallas_call | solution.py:570
  40.3 12.6 %all_to_all.10 = f32[4,1,200,128]{3,2,1,0:T(8,128)S(1)} all-to-all(f32[4,1,200,128]{3,2,1,0:T(8,128)S(1)} %broadcast_in_dim.7), channel_id=1, replica_groups={{0,128,256,384},{64,192,320,448},{1,129,257,385},{65,193,321,449},{2,13..., dimensions={0} | all-to-all | bytes 819200 | tf_op jit(solution)/shard_map/all_to_all | solution.py:552
  52.9 2.0 %collective-permute-start.8 = (f32[4,1,200,128]{3,2,0,1:T(8,128)S(1)}, f32[4,1,200,128]{3,2,0,1:T(8,128)S(1)}, u32[]{:S(2)}, u32[]{:S(2)}) collective-permute-start(f32[4,1,200,128]{3,2,0,1:T(8,128)S(1)} %bitcast.3), channel_id=1, source_target_pairs={{0,64},{64,0},{128,192},{192,128},{256,320},{320,256},{384,448},{4... | collective-permute-start | bytes 1228808 | tf_op jit(solution)/shard_map/ppermute | solution.py:577
  54.9 1.6 %collective-permute-done.8 = f32[4,1,200,128]{3,2,0,1:T(8,128)S(1)} collective-permute-done((f32[4,1,200,128]{3,2,0,1:T(8,128)S(1)}, f32[4,1,200,128]{3,2,0,1:T(8,128)S(1)}, u32[]{:S(2)}, u32[]{:S(2)}) %collective-permute-start.8) | collective-permute-done | bytes 409632 | tf_op jit(solution)/shard_map/ppermute | solution.py:577
  56.5 1.5 %shard_map.32 = (f32[8,16,128]{2,1,0:T(8,128)S(1)}, f32[8,56,128]{2,1,0:T(8,128)S(1)}, f32[8,56,128]{2,1,0:T(8,128)S(1)}, f32[8,56,128]{2,1,0:T(8,128)S(1)}) custom-call(f32[4,56,128]{2,1,0:T(8,128)S(1)} %get-tuple-element.34.own, f32[4,200,128]{2,1,0:T(8,128)S(1)} %bitcast.4, f32[4,200,128]{2,1,0:T(8,128)S(1)} %bitcast.5), custom_call_target="tpu_custom_call" | custom-call | tf_op jit(solution)/shard_map/pallas_call | solution.py:582
  58.1 10.8 %all_to_all.11.b2 = f32[4,8,16,128]{3,2,1,0:T(8,128)S(1)} all-to-all(f32[4,8,16,128]{3,2,1,0:T(8,128)S(1)} %broadcast_in_dim.8), channel_id=1, replica_groups=mesh['gx'=8,'gy'=4,'gz'=16] {'gy'}, dimensions={0} | all-to-all | bytes 524288 | tf_op jit(solution)/shard_map/all_to_all | solution.py:552
  68.8 0.8 shard_map.33
  69.6 5.3 %collective-permute-start.10 = (f32[2,32,128]{2,1,0:T(8,128)S(1)}, f32[2,32,128]{2,1,0:T(8,128)S(1)}, u32[]{:S(2)}, u32[]{:S(2)}) collective-permute-start(f32[2,32,128]{2,1,0:T(8,128)S(1)} %get-tuple-element.37.b3), channel_id=1, source_target_pairs={{1,0},{2,1},{3,2},{4,3},{5,4},{6,5},{7,6},{8,7},{9,8},{10,9},{11,1... | collective-permute-start | bytes 98312 | tf_op jit(solution)/shard_map/ppermute | solution.py:540
  74.9 1.9 %collective-permute-start.9 = (f32[2,32,128]{2,1,0:T(8,128)S(1)}, f32[2,32,128]{2,1,0:T(8,128)S(1)}, u32[]{:S(2)}, u32[]{:S(2)}) collective-permute-start(f32[2,32,128]{2,1,0:T(8,128)S(1)} %get-tuple-element.37.b3), channel_id=1, source_target_pairs={{0,1},{1,2},{2,3},{3,4},{4,5},{5,6},{6,7},{7,8},{8,9},{9,10},{10,1... | collective-permute-start | bytes 98312 | tf_op jit(solution)/shard_map/ppermute | solution.py:540
  76.9 0.0 collective-permute-done.10.b3_right
  76.9 5.1 %collective-permute-done.9.b3_left = f32[2,32,128]{2,1,0:T(8,128)S(1)} collective-permute-done((f32[2,32,128]{2,1,0:T(8,128)S(1)}, f32[2,32,128]{2,1,0:T(8,128)S(1)}, u32[]{:S(2)}, u32[]{:S(2)}) %collective-permute-start.9) | collective-permute-done | bytes 32800 | tf_op jit(solution)/shard_map/ppermute | solution.py:540
  82.0 4.9 %shard_map.34 = f32[8,64,128]{2,1,0:T(8,128)} custom-call(f32[2,32,128]{2,1,0:T(8,128)S(1)} %get-tuple-element.37.b3, f32[2,32,128]{2,1,0:T(8,128)S(1)} %collective-permute-done.9.b3_left, f32[2,32,128]{2,1,0:T(8,128)S(1)} %collective-permute-done.10.b3_right, f32[4,64,128]{2,1,0:T(8,128)S(1)} %get-tuple-element.38.start2, ...), custom_call_target="tpu_custom_call" | custom-call | tf_op jit(solution)/shard_map/pallas_call | solution.py:597
  (2 shorter events, 0.0 us)
Async XLA Ops:
  0.0 0.9 %copy-start = (f32[8,64,128]{2,1,0:T(8,128)S(1)}, f32[8,64,128]{2,1,0:T(8,128)}, u32[]{:S(2)}) copy-start(f32[8,64,128]{2,1,0:T(8,128)} %start_hbm.1) | copy-start | bytes 786436
  1.0 0.9 %copy-start.1 = (f32[8,64,128]{2,1,0:T(8,128)S(1)}, f32[8,64,128]{2,1,0:T(8,128)}, u32[]{:S(2)}) copy-start(f32[8,64,128]{2,1,0:T(8,128)} %right_hbm.1) | copy-start | bytes 786436
  2.1 9.7 %collective-permute-start = (f32[6,64,128]{2,1,0:T(8,128)S(1)}, f32[6,64,128]{2,1,0:T(8,128)S(1)}, u32[]{:S(2)}, u32[]{:S(2)}) collective-permute-start(f32[6,64,128]{2,1,0:T(8,128)S(1)} %get-tuple-element.27), channel_id=1, source_target_pairs={{0,1},{1,2},{2,3},{3,4},{4,5},{5,6},{6,7},{7,8},{8,9},{9,10},{10,1... | collective-permute-start | bytes 589832 | tf_op jit(solution)/shard_map/ppermute | solution.py:540
  5.0 8.3 %collective-permute-start.1 = (f32[6,64,128]{2,1,0:T(8,128)S(1)}, f32[6,64,128]{2,1,0:T(8,128)S(1)}, u32[]{:S(2)}, u32[]{:S(2)}) collective-permute-start(f32[6,64,128]{2,1,0:T(8,128)S(1)} %get-tuple-element.28), channel_id=1, source_target_pairs={{1,0},{2,1},{3,2},{4,3},{5,4},{6,5},{7,6},{8,7},{9,8},{10,9},{11,1... | collective-permute-start | bytes 589832 | tf_op jit(solution)/shard_map/ppermute | solution.py:540
  9.2 9.0 %collective-permute-start.5 = (f32[12,64,128]{2,1,0:T(8,128)S(1)}, f32[12,64,128]{2,1,0:T(8,128)S(1)}, u32[]{:S(2)}, u32[]{:S(2)}) collective-permute-start(f32[12,64,128]{2,1,0:T(8,128)S(1)} %get-tuple-element.26.s), channel_id=1, source_target_pairs={{64,0},{128,64},{192,128},{256,192},{320,256},{384,320},{448,384},... | collective-permute-start | bytes 1179656 | tf_op jit(solution)/shard_map/ppermute | solution.py:546
  11.1 8.4 %collective-permute-start.4 = (f32[12,64,128]{2,1,0:T(8,128)S(1)}, f32[12,64,128]{2,1,0:T(8,128)S(1)}, u32[]{:S(2)}, u32[]{:S(2)}) collective-permute-start(f32[12,64,128]{2,1,0:T(8,128)S(1)} %get-tuple-element.26.s), channel_id=1, source_target_pairs={{0,64},{64,128},{128,192},{192,256},{256,320},{320,384},{384,448},... | collective-permute-start | bytes 1179656 | tf_op jit(solution)/shard_map/ppermute | solution.py:546
  13.4 7.6 %collective-permute-start.2 = (f32[496,128]{1,0:T(8,128)S(1)}, f32[496,128]{1,0:T(8,128)S(1)}, u32[]{:S(2)}, u32[]{:S(2)}) collective-permute-start(f32[496,128]{1,0:T(8,128)S(1)} %get-tuple-element.30), channel_id=1, source_target_pairs={{0,16},{16,32},{32,48},{1,17},{17,33},{33,49},{2,18},{18,34},{34,5... | collective-permute-start | bytes 761864 | tf_op jit(solution)/shard_map/ppermute | solution.py:540
  16.9 8.3 %collective-permute-start.3 = (f32[496,128]{1,0:T(8,128)S(1)}, f32[496,128]{1,0:T(8,128)S(1)}, u32[]{:S(2)}, u32[]{:S(2)}) collective-permute-start(f32[496,128]{1,0:T(8,128)S(1)} %get-tuple-element.31), channel_id=1, source_target_pairs={{16,0},{32,16},{48,32},{17,1},{33,17},{49,33},{18,2},{34,18},{50,3... | collective-permute-start | bytes 761864 | tf_op jit(solution)/shard_map/ppermute | solution.py:540
  25.4 10.7 %collective-permute-start.6 = (f32[1184,128]{1,0:T(8,128)S(1)}, f32[1184,128]{1,0:T(8,128)S(1)}, u32[]{:S(2)}, u32[]{:S(2)}) collective-permute-start(f32[1184,128]{1,0:T(8,128)S(1)} %get-tuple-element.32), channel_id=1, source_target_pairs={{0,64},{64,128},{128,192},{192,256},{256,320},{320,384},{384,448},... | collective-permute-start | bytes 1818632 | tf_op jit(solution)/shard_map/ppermute | solution.py:546
  25.4 10.7 %collective-permute-start.7 = (f32[1184,128]{1,0:T(8,128)S(1)}, f32[1184,128]{1,0:T(8,128)S(1)}, u32[]{:S(2)}, u32[]{:S(2)}) collective-permute-start(f32[1184,128]{1,0:T(8,128)S(1)} %get-tuple-element.33), channel_id=1, source_target_pairs={{64,0},{128,64},{192,128},{256,192},{320,256},{384,320},{448,384},... | collective-permute-start | bytes 1818632 | tf_op jit(solution)/shard_map/ppermute | solution.py:546
  52.9 3.6 %collective-permute-start.8 = (f32[4,1,200,128]{3,2,0,1:T(8,128)S(1)}, f32[4,1,200,128]{3,2,0,1:T(8,128)S(1)}, u32[]{:S(2)}, u32[]{:S(2)}) collective-permute-start(f32[4,1,200,128]{3,2,0,1:T(8,128)S(1)} %bitcast.3), channel_id=1, source_target_pairs={{0,64},{64,0},{128,192},{192,128},{256,320},{320,256},{384,448},{4... | collective-permute-start | bytes 1228808 | tf_op jit(solution)/shard_map/ppermute | solution.py:577
  69.6 7.3 %collective-permute-start.10 = (f32[2,32,128]{2,1,0:T(8,128)S(1)}, f32[2,32,128]{2,1,0:T(8,128)S(1)}, u32[]{:S(2)}, u32[]{:S(2)}) collective-permute-start(f32[2,32,128]{2,1,0:T(8,128)S(1)} %get-tuple-element.37.b3), channel_id=1, source_target_pairs={{1,0},{2,1},{3,2},{4,3},{5,4},{6,5},{7,6},{8,7},{9,8},{10,9},{11,1... | collective-permute-start | bytes 98312 | tf_op jit(solution)/shard_map/ppermute | solution.py:540
  74.9 7.0 %collective-permute-start.9 = (f32[2,32,128]{2,1,0:T(8,128)S(1)}, f32[2,32,128]{2,1,0:T(8,128)S(1)}, u32[]{:S(2)}, u32[]{:S(2)}) collective-permute-start(f32[2,32,128]{2,1,0:T(8,128)S(1)} %get-tuple-element.37.b3), channel_id=1, source_target_pairs={{0,1},{1,2},{2,3},{3,4},{4,5},{5,6},{6,7},{7,8},{8,9},{9,10},{10,1... | collective-permute-start | bytes 98312 | tf_op jit(solution)/shard_map/ppermute | solution.py:540

commit v6 on v4

--- a/solution.py
+++ b/solution.py
@@ -143,7 +143,8 @@
 STRIP_AT = 48 * NEAR
 FAR_AT = STRIP_AT + 32 * NEAR
 PACKED_AT = FAR_AT + 16 * FAR
-CROSS_X = PACKED_AT + 2 * 16
+WHOLE_AT = PACKED_AT + 2 * 16
+CROSS_X = WHOLE_AT + 64
 
 
 def widen_kernel(s, up, down, v, v_up, v_down, first, last):
@@ -161,13 +162,12 @@
         at = 480 + 8 * t
         first[at : at + 8] = pack16([v[6 * t + k, 16:24] for k in range(6)])
         last[at : at + 8] = pack16([v[6 * t + k, 40:48] for k in range(6)])
-    for ref, near, far in ((v_up, UP_NEAR, UP_FAR), (v_down, DOWN_NEAR, DOWN_FAR)):
+    for ref, near in ((v_up, UP_NEAR), (v_down, DOWN_NEAR)):
         for k, p in enumerate(near):
             ref[k] = v[p]
-        ref[NEAR] = pack16([v[p] for p in far])
-
-
-def strips_kernel(before, after, *rest):
+
+
+def strips_kernel(v, before, after, *rest):
     lanes = lane_of((8, 128))
     for ref, near, far in ((rest[-2], UP_NEAR, UP_FAR), (rest[-1], DOWN_NEAR, DOWN_FAR)):
         outer = [jnp.zeros((8, 128), F32), jnp.zeros((8, 128), F32)]
@@ -182,6 +182,7 @@
                 plane = strip[at : at + 8]
                 plane = pltpu.roll(plane, shift, 1) if shift else plane
                 outer[h] = jnp.where((lanes >= 16 * k) & (lanes < 16 * k + 16), plane, outer[h])
+        ref[WHOLE_AT:] = pack16([v[p] for p in far])
         edges = [[], []]
         for k, p in enumerate(far):
             at, inner = FAR_AT + 16 * k, 288 + 16 * p
@@ -248,7 +249,7 @@
                 if p // 4 != a:
                     continue
                 i = base + p % 4
-                put(i, EY, strip, unpack16(strips[NEAR], k), there)
+                put(i, EY, strip, unpack16(y[WHOLE_AT:], k), there)
                 at = FAR_AT + 16 * k
                 put(i, 16, block, y[at : at + 8], there)
                 put(i, EY + 64, block, y[at + 8 : at + 16], there)
@@ -563,12 +564,11 @@
     )(start, right_side)
     up, down = from_both(up, down, "gz")
     s_left, s_right = from_both_round(s, s, "gx")
-    v, v_up, v_down, first, last = call(
-        widen_kernel, [(12, 64, 128), (NEAR + 1, 64, 128), (NEAR + 1, 64, 128), (CROSS_Y, 128), (CROSS_Y, 128)]
-    )(s, up, down)
+    near = (NEAR, 64, 128)
+    v, v_up, v_down, first, last = call(widen_kernel, [(12, 64, 128), near, near, (CROSS_Y, 128), (CROSS_Y, 128)])(s, up, down)
     v_left, v_right = from_both_round(v_up, v_down, "gx")
     before, after = from_both(last, first, "gy")
-    up, down = call(strips_kernel, [(CROSS_X, 128)] * 2)(before, after, s_left, s_right, v_left, v_right)
+    up, down = call(strips_kernel, [(CROSS_X, 128)] * 2)(v, before, after, s_left, v_left, v_right)
     y_left, y_right = from_both_round(up, down, "gx")
     up0 = (8, 80, 256)
     b1, sent, black0, red_b0, black_b0 = call(

time: 88.2 us -> 85.4 us (0.968)
  the two profiles are of different devices: /device:TPU:128 before, /device:TPU:256 now
where the time goes in v6:
time: 85.4 us; the launch traced here: 85 us
  starting transfers between devices  27.2 us (32%)
  blocking collectives  23.9 us (28%)
  waiting for transfers between devices  19.9 us (23%)
  Pallas kernels  11.9 us (14%)
  local copies, waits for them, and re-layouts  1.95 us (2%)
    all_to_all x2, blocking collectives, gathered(): lax.all_to_all(copies, axis, split_axis=0, concat_axis=0, axis_index_grou...  23.9 us
    ppermute x3, starting transfers between devices, from_both(): lax.ppermute(down_value, axis, [(b, a) for a, b in up])  10.8 us
    ppermute x3, starting transfers between devices, from_both(): lax.ppermute(up_value, axis, up)  8.26 us
    ppermute x3, waiting for transfers between devices, from_both_round(): lax.ppermute(up_value, axis, up)  8.22 us
    ppermute x3, waiting for transfers between devices, from_both(): lax.ppermute(up_value, axis, up)  7.73 us
    ppermute x3, starting transfers between devices, from_both_round(): lax.ppermute(down_value, axis, [(b, a) for a, b in up])  5.93 us
    pallas_call x1, Pallas kernels, local(): call(functools.partial(up_kernel, n), [(8, 64, 128)], [colour2, colour2,...  4.87 us
    pallas_call x1, Pallas kernels, local(): call(functools.partial(fine_down_kernel, n), [(4, ROWS1, 128), (4 * SENT1...  4.23 us
  transfers between devices with their start and end apart: 13, of which 8 were waited for; matrix products, arithmetic and copies ran while one was open for 0% of the time, Pallas kernels for 0%

profile of v6, /device:TPU:256, one launch (start us, length us, event | category | flops | bytes accessed | tf_op | source)
XLA Modules:
  0.0 85.0 jit_solution(12541584348070962929)
XLA Ops:
  0.0 0.0 copy-start
  0.0 0.9 %copy-done = f32[8,64,128]{2,1,0:T(8,128)S(1)} copy-done((f32[8,64,128]{2,1,0:T(8,128)S(1)}, f32[8,64,128]{2,1,0:T(8,128)}, u32[]{:S(2)}) %copy-start) | copy-done | bytes 262168
  1.0 0.0 copy-start.1
  1.0 0.9 %copy-done.1 = f32[8,64,128]{2,1,0:T(8,128)S(1)} copy-done((f32[8,64,128]{2,1,0:T(8,128)S(1)}, f32[8,64,128]{2,1,0:T(8,128)}, u32[]{:S(2)}) %copy-start.1) | copy-done | bytes 262168
  1.9 0.2 shard_map.28
  2.1 2.9 %collective-permute-start = (f32[6,64,128]{2,1,0:T(8,128)S(1)}, f32[6,64,128]{2,1,0:T(8,128)S(1)}, u32[]{:S(2)}, u32[]{:S(2)}) collective-permute-start(f32[6,64,128]{2,1,0:T(8,128)S(1)} %get-tuple-element.29), channel_id=1, source_target_pairs={{0,1},{1,2},{2,3},{3,4},{4,5},{5,6},{6,7},{7,8},{8,9},{9,10},{10,1... | collective-permute-start | bytes 589832 | tf_op jit(solution)/shard_map/ppermute | solution.py:542
  5.0 4.1 %collective-permute-start.1 = (f32[6,64,128]{2,1,0:T(8,128)S(1)}, f32[6,64,128]{2,1,0:T(8,128)S(1)}, u32[]{:S(2)}, u32[]{:S(2)}) collective-permute-start(f32[6,64,128]{2,1,0:T(8,128)S(1)} %get-tuple-element.30), channel_id=1, source_target_pairs={{1,0},{2,1},{3,2},{4,3},{5,4},{6,5},{7,6},{8,7},{9,8},{10,9},{11,1... | collective-permute-start | bytes 589832 | tf_op jit(solution)/shard_map/ppermute | solution.py:542
  9.2 0.0 collective-permute-start.4
  9.2 2.7 %collective-permute-done.up = f32[6,64,128]{2,1,0:T(8,128)S(1)} collective-permute-done((f32[6,64,128]{2,1,0:T(8,128)S(1)}, f32[6,64,128]{2,1,0:T(8,128)S(1)}, u32[]{:S(2)}, u32[]{:S(2)}) %collective-permute-start) | collective-permute-done | bytes 196640 | tf_op jit(solution)/shard_map/ppermute | solution.py:542
  11.8 1.4 %collective-permute-done.1.down = f32[6,64,128]{2,1,0:T(8,128)S(1)} collective-permute-done((f32[6,64,128]{2,1,0:T(8,128)S(1)}, f32[6,64,128]{2,1,0:T(8,128)S(1)}, u32[]{:S(2)}, u32[]{:S(2)}) %collective-permute-start.1) | collective-permute-done | bytes 196640 | tf_op jit(solution)/shard_map/ppermute | solution.py:542
  13.3 0.2 shard_map.29
  13.5 3.4 %collective-permute-start.2 = (f32[496,128]{1,0:T(8,128)S(1)}, f32[496,128]{1,0:T(8,128)S(1)}, u32[]{:S(2)}, u32[]{:S(2)}) collective-permute-start(f32[496,128]{1,0:T(8,128)S(1)} %get-tuple-element.32), channel_id=1, source_target_pairs={{0,16},{16,32},{32,48},{1,17},{17,33},{33,49},{2,18},{18,34},{34,5... | collective-permute-start | bytes 761864 | tf_op jit(solution)/shard_map/ppermute | solution.py:542
  16.9 1.3 %collective-permute-start.3 = (f32[496,128]{1,0:T(8,128)S(1)}, f32[496,128]{1,0:T(8,128)S(1)}, u32[]{:S(2)}, u32[]{:S(2)}) collective-permute-start(f32[496,128]{1,0:T(8,128)S(1)} %get-tuple-element.33), channel_id=1, source_target_pairs={{16,0},{32,16},{48,32},{17,1},{33,17},{49,33},{18,2},{34,18},{50,3... | collective-permute-start | bytes 761864 | tf_op jit(solution)/shard_map/ppermute | solution.py:542
  18.2 0.0 collective-permute-start.6
  18.2 2.9 %collective-permute-start.7 = (f32[7,64,128]{2,1,0:T(8,128)S(1)}, f32[7,64,128]{2,1,0:T(8,128)S(1)}, u32[]{:S(2)}, u32[]{:S(2)}) collective-permute-start(f32[7,64,128]{2,1,0:T(8,128)S(1)} %get-tuple-element.35), channel_id=1, source_target_pairs={{64,0},{128,64},{192,128},{256,192},{320,256},{384,320},{448,384},... | collective-permute-start | bytes 688136 | tf_op jit(solution)/shard_map/ppermute | solution.py:548
  21.1 0.0 collective-permute-done.4.rest_0_.s_left
  21.1 0.2 collective-permute-start.5
  21.3 3.5 %collective-permute-done.6.rest_1_.v_left = f32[7,64,128]{2,1,0:T(8,128)S(1)} collective-permute-done((f32[7,64,128]{2,1,0:T(8,128)S(1)}, f32[7,64,128]{2,1,0:T(8,128)S(1)}, u32[]{:S(2)}, u32[]{:S(2)}) %collective-permute-start.6) | collective-permute-done | bytes 229408 | tf_op jit(solution)/shard_map/ppermute | solution.py:548
  24.8 0.0 collective-permute-done.7.rest_2_.v_right
  24.8 0.0 collective-permute-done.2.before
  24.9 0.3 collective-permute-done.3.after
  25.2 0.2 shard_map.30
  25.4 0.2 collective-permute-start.8
  25.5 2.8 %collective-permute-start.9 = (f32[736,128]{1,0:T(8,128)S(1)}, f32[736,128]{1,0:T(8,128)S(1)}, u32[]{:S(2)}, u32[]{:S(2)}) collective-permute-start(f32[736,128]{1,0:T(8,128)S(1)} %get-tuple-element.37), channel_id=1, source_target_pairs={{64,0},{128,64},{192,128},{256,192},{320,256},{384,320},{448,384},... | collective-permute-start | bytes 1130504 | tf_op jit(solution)/shard_map/ppermute | solution.py:548
  28.3 0.6 collective-permute-done.5.s_right
  28.9 4.7 %collective-permute-done.8.y_left = f32[736,128]{1,0:T(8,128)S(1)} collective-permute-done((f32[736,128]{1,0:T(8,128)S(1)}, f32[736,128]{1,0:T(8,128)S(1)}, u32[]{:S(2)}, u32[]{:S(2)}) %collective-permute-start.8) | collective-permute-done | bytes 376864 | tf_op jit(solution)/shard_map/ppermute | solution.py:548
  33.6 0.0 collective-permute-done.9.y_right
  33.6 4.2 %shard_map.31 = (f32[4,56,128]{2,1,0:T(8,128)S(1)}, f32[200,128]{1,0:T(8,128)S(1)}, f32[8,80,256]{2,1,0:T(8,128)S(1)}, f32[8,80,256]{2,1,0:T(8,128)S(1)}, f32[8,80,256]{2,1,0:T(8,128)S(1)}) custom-call(f32[12,64,128]{2,1,0:T(8,128)S(1)} %get-tuple-element.28.s, f32[12,64,128]{2,1,0:T(8,128)S(1)} %get-tuple-element.31.v, ...), custom_call_target="tpu_custom_call" | custom-call | tf_op jit(solution)/shard_map/pallas_call | solution.py:574
  37.9 12.6 %all_to_all.10 = f32[4,1,200,128]{3,2,1,0:T(8,128)S(1)} all-to-all(f32[4,1,200,128]{3,2,1,0:T(8,128)S(1)} %broadcast_in_dim.7), channel_id=1, replica_groups={{0,128,256,384},{64,192,320,448},{1,129,257,385},{65,193,321,449},{2,13..., dimensions={0} | all-to-all | bytes 819200 | tf_op jit(solution)/shard_map/all_to_all | solution.py:554
  50.5 2.0 %collective-permute-start.10 = (f32[4,1,200,128]{3,2,0,1:T(8,128)S(1)}, f32[4,1,200,128]{3,2,0,1:T(8,128)S(1)}, u32[]{:S(2)}, u32[]{:S(2)}) collective-permute-start(f32[4,1,200,128]{3,2,0,1:T(8,128)S(1)} %bitcast.3), channel_id=1, source_target_pairs={{0,64},{64,0},{128,192},{192,128},{256,320},{320,256},{384,448},{4... | collective-permute-start | bytes 1228808 | tf_op jit(solution)/shard_map/ppermute | solution.py:581
  52.5 1.6 %collective-permute-done.10 = f32[4,1,200,128]{3,2,0,1:T(8,128)S(1)} collective-permute-done((f32[4,1,200,128]{3,2,0,1:T(8,128)S(1)}, f32[4,1,200,128]{3,2,0,1:T(8,128)S(1)}, u32[]{:S(2)}, u32[]{:S(2)}) %collective-permute-start.10) | collective-permute-done | bytes 409632 | tf_op jit(solution)/shard_map/ppermute | solution.py:581
  54.1 1.5 %shard_map.32 = (f32[8,16,128]{2,1,0:T(8,128)S(1)}, f32[8,56,128]{2,1,0:T(8,128)S(1)}, f32[8,56,128]{2,1,0:T(8,128)S(1)}, f32[8,56,128]{2,1,0:T(8,128)S(1)}) custom-call(f32[4,56,128]{2,1,0:T(8,128)S(1)} %get-tuple-element.38.own, f32[4,200,128]{2,1,0:T(8,128)S(1)} %bitcast.4, f32[4,200,128]{2,1,0:T(8,128)S(1)} %bitcast.5), custom_call_target="tpu_custom_call" | custom-call | tf_op jit(solution)/shard_map/pallas_call | solution.py:586
  55.6 11.3 %all_to_all.11.b2 = f32[4,8,16,128]{3,2,1,0:T(8,128)S(1)} all-to-all(f32[4,8,16,128]{3,2,1,0:T(8,128)S(1)} %broadcast_in_dim.8), channel_id=1, replica_groups=mesh['gx'=8,'gy'=4,'gz'=16] {'gy'}, dimensions={0} | all-to-all | bytes 524288 | tf_op jit(solution)/shard_map/all_to_all | solution.py:554
  67.0 0.8 shard_map.33
  67.7 5.3 %collective-permute-start.12 = (f32[2,32,128]{2,1,0:T(8,128)S(1)}, f32[2,32,128]{2,1,0:T(8,128)S(1)}, u32[]{:S(2)}, u32[]{:S(2)}) collective-permute-start(f32[2,32,128]{2,1,0:T(8,128)S(1)} %get-tuple-element.41.b3), channel_id=1, source_target_pairs={{1,0},{2,1},{3,2},{4,3},{5,4},{6,5},{7,6},{8,7},{9,8},{10,9},{11,1... | collective-permute-start | bytes 98312 | tf_op jit(solution)/shard_map/ppermute | solution.py:542
  73.1 1.9 %collective-permute-start.11 = (f32[2,32,128]{2,1,0:T(8,128)S(1)}, f32[2,32,128]{2,1,0:T(8,128)S(1)}, u32[]{:S(2)}, u32[]{:S(2)}) collective-permute-start(f32[2,32,128]{2,1,0:T(8,128)S(1)} %get-tuple-element.41.b3), channel_id=1, source_target_pairs={{0,1},{1,2},{2,3},{3,4},{4,5},{5,6},{6,7},{7,8},{8,9},{9,10},{10,1... | collective-permute-start | bytes 98312 | tf_op jit(solution)/shard_map/ppermute | solution.py:542
  75.0 0.0 collective-permute-done.12.b3_right
  75.0 5.1 %collective-permute-done.11.b3_left = f32[2,32,128]{2,1,0:T(8,128)S(1)} collective-permute-done((f32[2,32,128]{2,1,0:T(8,128)S(1)}, f32[2,32,128]{2,1,0:T(8,128)S(1)}, u32[]{:S(2)}, u32[]{:S(2)}) %collective-permute-start.11) | collective-permute-done | bytes 32800 | tf_op jit(solution)/shard_map/ppermute | solution.py:542
  80.1 4.9 %shard_map.34 = f32[8,64,128]{2,1,0:T(8,128)} custom-call(f32[2,32,128]{2,1,0:T(8,128)S(1)} %get-tuple-element.41.b3, f32[2,32,128]{2,1,0:T(8,128)S(1)} %collective-permute-done.11.b3_left, f32[2,32,128]{2,1,0:T(8,128)S(1)} %collective-permute-done.12.b3_right, f32[4,64,128]{2,1,0:T(8,128)S(1)} %get-tuple-element.42.start2, ...), custom_call_target="tpu_custom_call" | custom-call | tf_op jit(solution)/shard_map/pallas_call | solution.py:601
  (2 shorter events, 0.0 us)
Async XLA Ops:
  0.0 0.9 %copy-start = (f32[8,64,128]{2,1,0:T(8,128)S(1)}, f32[8,64,128]{2,1,0:T(8,128)}, u32[]{:S(2)}) copy-start(f32[8,64,128]{2,1,0:T(8,128)} %start_hbm.1) | copy-start | bytes 786436
  1.0 0.9 %copy-start.1 = (f32[8,64,128]{2,1,0:T(8,128)S(1)}, f32[8,64,128]{2,1,0:T(8,128)}, u32[]{:S(2)}) copy-start(f32[8,64,128]{2,1,0:T(8,128)} %right_hbm.1) | copy-start | bytes 786436
  2.1 9.7 %collective-permute-start = (f32[6,64,128]{2,1,0:T(8,128)S(1)}, f32[6,64,128]{2,1,0:T(8,128)S(1)}, u32[]{:S(2)}, u32[]{:S(2)}) collective-permute-start(f32[6,64,128]{2,1,0:T(8,128)S(1)} %get-tuple-element.29), channel_id=1, source_target_pairs={{0,1},{1,2},{2,3},{3,4},{4,5},{5,6},{6,7},{7,8},{8,9},{9,10},{10,1... | collective-permute-start | bytes 589832 | tf_op jit(solution)/shard_map/ppermute | solution.py:542
  5.0 8.3 %collective-permute-start.1 = (f32[6,64,128]{2,1,0:T(8,128)S(1)}, f32[6,64,128]{2,1,0:T(8,128)S(1)}, u32[]{:S(2)}, u32[]{:S(2)}) collective-permute-start(f32[6,64,128]{2,1,0:T(8,128)S(1)} %get-tuple-element.30), channel_id=1, source_target_pairs={{1,0},{2,1},{3,2},{4,3},{5,4},{6,5},{7,6},{8,7},{9,8},{10,9},{11,1... | collective-permute-start | bytes 589832 | tf_op jit(solution)/shard_map/ppermute | solution.py:542
  9.2 12.0 %collective-permute-start.4 = (f32[12,64,128]{2,1,0:T(8,128)S(1)}, f32[12,64,128]{2,1,0:T(8,128)S(1)}, u32[]{:S(2)}, u32[]{:S(2)}) collective-permute-start(f32[12,64,128]{2,1,0:T(8,128)S(1)} %get-tuple-element.28.s), channel_id=1, source_target_pairs={{0,64},{64,128},{128,192},{192,256},{256,320},{320,384},{384,448},... | collective-permute-start | bytes 1179656 | tf_op jit(solution)/shard_map/ppermute | solution.py:548
  13.5 11.4 %collective-permute-start.2 = (f32[496,128]{1,0:T(8,128)S(1)}, f32[496,128]{1,0:T(8,128)S(1)}, u32[]{:S(2)}, u32[]{:S(2)}) collective-permute-start(f32[496,128]{1,0:T(8,128)S(1)} %get-tuple-element.32), channel_id=1, source_target_pairs={{0,16},{16,32},{32,48},{1,17},{17,33},{33,49},{2,18},{18,34},{34,5... | collective-permute-start | bytes 761864 | tf_op jit(solution)/shard_map/ppermute | solution.py:542
  16.9 8.3 %collective-permute-start.3 = (f32[496,128]{1,0:T(8,128)S(1)}, f32[496,128]{1,0:T(8,128)S(1)}, u32[]{:S(2)}, u32[]{:S(2)}) collective-permute-start(f32[496,128]{1,0:T(8,128)S(1)} %get-tuple-element.33), channel_id=1, source_target_pairs={{16,0},{32,16},{48,32},{17,1},{33,17},{49,33},{18,2},{34,18},{50,3... | collective-permute-start | bytes 761864 | tf_op jit(solution)/shard_map/ppermute | solution.py:542
  18.2 6.7 %collective-permute-start.6 = (f32[7,64,128]{2,1,0:T(8,128)S(1)}, f32[7,64,128]{2,1,0:T(8,128)S(1)}, u32[]{:S(2)}, u32[]{:S(2)}) collective-permute-start(f32[7,64,128]{2,1,0:T(8,128)S(1)} %get-tuple-element.34), channel_id=1, source_target_pairs={{0,64},{64,128},{128,192},{192,256},{256,320},{320,384},{384,448},... | collective-permute-start | bytes 688136 | tf_op jit(solution)/shard_map/ppermute | solution.py:548
  18.2 6.6 %collective-permute-start.7 = (f32[7,64,128]{2,1,0:T(8,128)S(1)}, f32[7,64,128]{2,1,0:T(8,128)S(1)}, u32[]{:S(2)}, u32[]{:S(2)}) collective-permute-start(f32[7,64,128]{2,1,0:T(8,128)S(1)} %get-tuple-element.35), channel_id=1, source_target_pairs={{64,0},{128,64},{192,128},{256,192},{320,256},{384,320},{448,384},... | collective-permute-start | bytes 688136 | tf_op jit(solution)/shard_map/ppermute | solution.py:548
  21.1 7.7 %collective-permute-start.5 = (f32[12,64,128]{2,1,0:T(8,128)S(1)}, f32[12,64,128]{2,1,0:T(8,128)S(1)}, u32[]{:S(2)}, u32[]{:S(2)}) collective-permute-start(f32[12,64,128]{2,1,0:T(8,128)S(1)} %get-tuple-element.28.s), channel_id=1, source_target_pairs={{64,0},{128,64},{192,128},{256,192},{320,256},{384,320},{448,384},... | collective-permute-start | bytes 1179656 | tf_op jit(solution)/shard_map/ppermute | solution.py:548
  25.4 8.2 %collective-permute-start.8 = (f32[736,128]{1,0:T(8,128)S(1)}, f32[736,128]{1,0:T(8,128)S(1)}, u32[]{:S(2)}, u32[]{:S(2)}) collective-permute-start(f32[736,128]{1,0:T(8,128)S(1)} %get-tuple-element.36), channel_id=1, source_target_pairs={{0,64},{64,128},{128,192},{192,256},{256,320},{320,384},{384,448},... | collective-permute-start | bytes 1130504 | tf_op jit(solution)/shard_map/ppermute | solution.py:548
  25.5 8.1 %collective-permute-start.9 = (f32[736,128]{1,0:T(8,128)S(1)}, f32[736,128]{1,0:T(8,128)S(1)}, u32[]{:S(2)}, u32[]{:S(2)}) collective-permute-start(f32[736,128]{1,0:T(8,128)S(1)} %get-tuple-element.37), channel_id=1, source_target_pairs={{64,0},{128,64},{192,128},{256,192},{320,256},{384,320},{448,384},... | collective-permute-start | bytes 1130504 | tf_op jit(solution)/shard_map/ppermute | solution.py:548
  50.5 3.6 %collective-permute-start.10 = (f32[4,1,200,128]{3,2,0,1:T(8,128)S(1)}, f32[4,1,200,128]{3,2,0,1:T(8,128)S(1)}, u32[]{:S(2)}, u32[]{:S(2)}) collective-permute-start(f32[4,1,200,128]{3,2,0,1:T(8,128)S(1)} %bitcast.3), channel_id=1, source_target_pairs={{0,64},{64,0},{128,192},{192,128},{256,320},{320,256},{384,448},{4... | collective-permute-start | bytes 1228808 | tf_op jit(solution)/shard_map/ppermute | solution.py:581
  67.7 7.3 %collective-permute-start.12 = (f32[2,32,128]{2,1,0:T(8,128)S(1)}, f32[2,32,128]{2,1,0:T(8,128)S(1)}, u32[]{:S(2)}, u32[]{:S(2)}) collective-permute-start(f32[2,32,128]{2,1,0:T(8,128)S(1)} %get-tuple-element.41.b3), channel_id=1, source_target_pairs={{1,0},{2,1},{3,2},{4,3},{5,4},{6,5},{7,6},{8,7},{9,8},{10,9},{11,1... | collective-permute-start | bytes 98312 | tf_op jit(solution)/shard_map/ppermute | solution.py:542
  73.1 7.0 %collective-permute-start.11 = (f32[2,32,128]{2,1,0:T(8,128)S(1)}, f32[2,32,128]{2,1,0:T(8,128)S(1)}, u32[]{:S(2)}, u32[]{:S(2)}) collective-permute-start(f32[2,32,128]{2,1,0:T(8,128)S(1)} %get-tuple-element.41.b3), channel_id=1, source_target_pairs={{0,1},{1,2},{2,3},{3,4},{4,5},{5,6},{6,7},{7,8},{8,9},{9,10},{10,1... | collective-permute-start | bytes 98312 | tf_op jit(solution)/shard_map/ppermute | solution.py:542

commit v7 on v6

--- a/solution.py
+++ b/solution.py
@@ -437,12 +437,9 @@
     every3 = range(pairs_3)
     half(black3, red3, bb3, weights3, False, every3, rows3, rows3)
 
-    def sweep3(_, carry):
+    for _ in range(7):
         half(red3, black3, rb3, weights3, True, every3, rows3, rows3)
         half(black3, red3, bb3, weights3, False, every3, rows3, rows3)
-        return carry
-
-    lax.fori_loop(0, 7, sweep3, 0)
     planes = []
     for i in every3:
         r, b = red3[i + 1, PAD : PAD + rows3], black3[i + 1, PAD : PAD + rows3]

time: 85.4 us -> 85.1 us (level)
  no operation moved by 1% of the time
where the time goes in v7:
time: 85.1 us; the launch traced here: 84.7 us
  starting transfers between devices  27.2 us (32%)
  blocking collectives  23.9 us (28%)
  waiting for transfers between devices  19.9 us (23%)
  Pallas kernels  11.7 us (14%)
  local copies, waits for them, and re-layouts  1.95 us (2%)
    all_to_all x2, blocking collectives, gathered(): lax.all_to_all(copies, axis, split_axis=0, concat_axis=0, axis_index_grou...  23.9 us
    ppermute x3, starting transfers between devices, from_both(): lax.ppermute(down_value, axis, [(b, a) for a, b in up])  10.8 us
    ppermute x3, starting transfers between devices, from_both(): lax.ppermute(up_value, axis, up)  8.26 us
    ppermute x3, waiting for transfers between devices, from_both_round(): lax.ppermute(up_value, axis, up)  8.22 us
    ppermute x3, waiting for transfers between devices, from_both(): lax.ppermute(up_value, axis, up)  7.73 us
    ppermute x3, starting transfers between devices, from_both_round(): lax.ppermute(down_value, axis, [(b, a) for a, b in up])  5.93 us
    pallas_call x1, Pallas kernels, local(): call(functools.partial(up_kernel, n), [(8, 64, 128)], [colour2, colour2,...  4.61 us
    pallas_call x1, Pallas kernels, local(): call(functools.partial(fine_down_kernel, n), [(4, ROWS1, 128), (4 * SENT1...  4.23 us
  transfers between devices with their start and end apart: 13, of which 8 were waited for; matrix products, arithmetic and copies ran while one was open for 0% of the time, Pallas kernels for 0%

profile of v7, /device:TPU:256, one launch (start us, length us, event | category | flops | bytes accessed | tf_op | source)
XLA Modules:
  0.0 84.7 jit_solution(732635242357101168)
XLA Ops:
  0.0 0.0 copy-start
  0.0 0.9 %copy-done = f32[8,64,128]{2,1,0:T(8,128)S(1)} copy-done((f32[8,64,128]{2,1,0:T(8,128)S(1)}, f32[8,64,128]{2,1,0:T(8,128)}, u32[]{:S(2)}) %copy-start) | copy-done | bytes 262168
  1.0 0.0 copy-start.1
  1.0 0.9 %copy-done.1 = f32[8,64,128]{2,1,0:T(8,128)S(1)} copy-done((f32[8,64,128]{2,1,0:T(8,128)S(1)}, f32[8,64,128]{2,1,0:T(8,128)}, u32[]{:S(2)}) %copy-start.1) | copy-done | bytes 262168
  1.9 0.2 shard_map.28
  2.1 2.9 %collective-permute-start = (f32[6,64,128]{2,1,0:T(8,128)S(1)}, f32[6,64,128]{2,1,0:T(8,128)S(1)}, u32[]{:S(2)}, u32[]{:S(2)}) collective-permute-start(f32[6,64,128]{2,1,0:T(8,128)S(1)} %get-tuple-element.29), channel_id=1, source_target_pairs={{0,1},{1,2},{2,3},{3,4},{4,5},{5,6},{6,7},{7,8},{8,9},{9,10},{10,1... | collective-permute-start | bytes 589832 | tf_op jit(solution)/shard_map/ppermute | solution.py:539
  5.0 4.1 %collective-permute-start.1 = (f32[6,64,128]{2,1,0:T(8,128)S(1)}, f32[6,64,128]{2,1,0:T(8,128)S(1)}, u32[]{:S(2)}, u32[]{:S(2)}) collective-permute-start(f32[6,64,128]{2,1,0:T(8,128)S(1)} %get-tuple-element.30), channel_id=1, source_target_pairs={{1,0},{2,1},{3,2},{4,3},{5,4},{6,5},{7,6},{8,7},{9,8},{10,9},{11,1... | collective-permute-start | bytes 589832 | tf_op jit(solution)/shard_map/ppermute | solution.py:539
  9.2 0.0 collective-permute-start.4
  9.2 2.7 %collective-permute-done.up = f32[6,64,128]{2,1,0:T(8,128)S(1)} collective-permute-done((f32[6,64,128]{2,1,0:T(8,128)S(1)}, f32[6,64,128]{2,1,0:T(8,128)S(1)}, u32[]{:S(2)}, u32[]{:S(2)}) %collective-permute-start) | collective-permute-done | bytes 196640 | tf_op jit(solution)/shard_map/ppermute | solution.py:539
  11.8 1.4 %collective-permute-done.1.down = f32[6,64,128]{2,1,0:T(8,128)S(1)} collective-permute-done((f32[6,64,128]{2,1,0:T(8,128)S(1)}, f32[6,64,128]{2,1,0:T(8,128)S(1)}, u32[]{:S(2)}, u32[]{:S(2)}) %collective-permute-start.1) | collective-permute-done | bytes 196640 | tf_op jit(solution)/shard_map/ppermute | solution.py:539
  13.3 0.2 shard_map.29
  13.5 3.4 %collective-permute-start.2 = (f32[496,128]{1,0:T(8,128)S(1)}, f32[496,128]{1,0:T(8,128)S(1)}, u32[]{:S(2)}, u32[]{:S(2)}) collective-permute-start(f32[496,128]{1,0:T(8,128)S(1)} %get-tuple-element.32), channel_id=1, source_target_pairs={{0,16},{16,32},{32,48},{1,17},{17,33},{33,49},{2,18},{18,34},{34,5... | collective-permute-start | bytes 761864 | tf_op jit(solution)/shard_map/ppermute | solution.py:539
  16.9 1.3 %collective-permute-start.3 = (f32[496,128]{1,0:T(8,128)S(1)}, f32[496,128]{1,0:T(8,128)S(1)}, u32[]{:S(2)}, u32[]{:S(2)}) collective-permute-start(f32[496,128]{1,0:T(8,128)S(1)} %get-tuple-element.33), channel_id=1, source_target_pairs={{16,0},{32,16},{48,32},{17,1},{33,17},{49,33},{18,2},{34,18},{50,3... | collective-permute-start | bytes 761864 | tf_op jit(solution)/shard_map/ppermute | solution.py:539
  18.2 0.0 collective-permute-start.6
  18.2 2.9 %collective-permute-start.7 = (f32[7,64,128]{2,1,0:T(8,128)S(1)}, f32[7,64,128]{2,1,0:T(8,128)S(1)}, u32[]{:S(2)}, u32[]{:S(2)}) collective-permute-start(f32[7,64,128]{2,1,0:T(8,128)S(1)} %get-tuple-element.35), channel_id=1, source_target_pairs={{64,0},{128,64},{192,128},{256,192},{320,256},{384,320},{448,384},... | collective-permute-start | bytes 688136 | tf_op jit(solution)/shard_map/ppermute | solution.py:545
  21.1 0.0 collective-permute-done.4.rest_0_.s_left
  21.1 0.2 collective-permute-start.5
  21.3 3.5 %collective-permute-done.6.rest_1_.v_left = f32[7,64,128]{2,1,0:T(8,128)S(1)} collective-permute-done((f32[7,64,128]{2,1,0:T(8,128)S(1)}, f32[7,64,128]{2,1,0:T(8,128)S(1)}, u32[]{:S(2)}, u32[]{:S(2)}) %collective-permute-start.6) | collective-permute-done | bytes 229408 | tf_op jit(solution)/shard_map/ppermute | solution.py:545
  24.8 0.0 collective-permute-done.7.rest_2_.v_right
  24.8 0.0 collective-permute-done.2.before
  24.9 0.3 collective-permute-done.3.after
  25.2 0.2 shard_map.30
  25.4 0.2 collective-permute-start.8
  25.5 2.8 %collective-permute-start.9 = (f32[736,128]{1,0:T(8,128)S(1)}, f32[736,128]{1,0:T(8,128)S(1)}, u32[]{:S(2)}, u32[]{:S(2)}) collective-permute-start(f32[736,128]{1,0:T(8,128)S(1)} %get-tuple-element.37), channel_id=1, source_target_pairs={{64,0},{128,64},{192,128},{256,192},{320,256},{384,320},{448,384},... | collective-permute-start | bytes 1130504 | tf_op jit(solution)/shard_map/ppermute | solution.py:545
  28.3 0.6 collective-permute-done.5.s_right
  28.9 4.7 %collective-permute-done.8.y_left = f32[736,128]{1,0:T(8,128)S(1)} collective-permute-done((f32[736,128]{1,0:T(8,128)S(1)}, f32[736,128]{1,0:T(8,128)S(1)}, u32[]{:S(2)}, u32[]{:S(2)}) %collective-permute-start.8) | collective-permute-done | bytes 376864 | tf_op jit(solution)/shard_map/ppermute | solution.py:545
  33.6 0.0 collective-permute-done.9.y_right
  33.6 4.2 %shard_map.31 = (f32[4,56,128]{2,1,0:T(8,128)S(1)}, f32[200,128]{1,0:T(8,128)S(1)}, f32[8,80,256]{2,1,0:T(8,128)S(1)}, f32[8,80,256]{2,1,0:T(8,128)S(1)}, f32[8,80,256]{2,1,0:T(8,128)S(1)}) custom-call(f32[12,64,128]{2,1,0:T(8,128)S(1)} %get-tuple-element.28.s, f32[12,64,128]{2,1,0:T(8,128)S(1)} %get-tuple-element.31.v, ...), custom_call_target="tpu_custom_call" | custom-call | tf_op jit(solution)/shard_map/pallas_call | solution.py:571
  37.9 12.6 %all_to_all.10 = f32[4,1,200,128]{3,2,1,0:T(8,128)S(1)} all-to-all(f32[4,1,200,128]{3,2,1,0:T(8,128)S(1)} %broadcast_in_dim.7), channel_id=1, replica_groups={{0,128,256,384},{64,192,320,448},{1,129,257,385},{65,193,321,449},{2,13..., dimensions={0} | all-to-all | bytes 819200 | tf_op jit(solution)/shard_map/all_to_all | solution.py:551
  50.5 2.0 %collective-permute-start.10 = (f32[4,1,200,128]{3,2,0,1:T(8,128)S(1)}, f32[4,1,200,128]{3,2,0,1:T(8,128)S(1)}, u32[]{:S(2)}, u32[]{:S(2)}) collective-permute-start(f32[4,1,200,128]{3,2,0,1:T(8,128)S(1)} %bitcast.3), channel_id=1, source_target_pairs={{0,64},{64,0},{128,192},{192,128},{256,320},{320,256},{384,448},{4... | collective-permute-start | bytes 1228808 | tf_op jit(solution)/shard_map/ppermute | solution.py:578
  52.5 1.6 %collective-permute-done.10 = f32[4,1,200,128]{3,2,0,1:T(8,128)S(1)} collective-permute-done((f32[4,1,200,128]{3,2,0,1:T(8,128)S(1)}, f32[4,1,200,128]{3,2,0,1:T(8,128)S(1)}, u32[]{:S(2)}, u32[]{:S(2)}) %collective-permute-start.10) | collective-permute-done | bytes 409632 | tf_op jit(solution)/shard_map/ppermute | solution.py:578
  54.1 1.5 %shard_map.32 = (f32[8,16,128]{2,1,0:T(8,128)S(1)}, f32[8,56,128]{2,1,0:T(8,128)S(1)}, f32[8,56,128]{2,1,0:T(8,128)S(1)}, f32[8,56,128]{2,1,0:T(8,128)S(1)}) custom-call(f32[4,56,128]{2,1,0:T(8,128)S(1)} %get-tuple-element.38.own, f32[4,200,128]{2,1,0:T(8,128)S(1)} %bitcast.4, f32[4,200,128]{2,1,0:T(8,128)S(1)} %bitcast.5), custom_call_target="tpu_custom_call" | custom-call | tf_op jit(solution)/shard_map/pallas_call | solution.py:583
  55.6 11.3 %all_to_all.11.b2 = f32[4,8,16,128]{3,2,1,0:T(8,128)S(1)} all-to-all(f32[4,8,16,128]{3,2,1,0:T(8,128)S(1)} %broadcast_in_dim.8), channel_id=1, replica_groups=mesh['gx'=8,'gy'=4,'gz'=16] {'gy'}, dimensions={0} | all-to-all | bytes 524288 | tf_op jit(solution)/shard_map/all_to_all | solution.py:551
  67.0 0.8 shard_map.33
  67.7 5.3 %collective-permute-start.12 = (f32[2,32,128]{2,1,0:T(8,128)S(1)}, f32[2,32,128]{2,1,0:T(8,128)S(1)}, u32[]{:S(2)}, u32[]{:S(2)}) collective-permute-start(f32[2,32,128]{2,1,0:T(8,128)S(1)} %get-tuple-element.41.b3), channel_id=1, source_target_pairs={{1,0},{2,1},{3,2},{4,3},{5,4},{6,5},{7,6},{8,7},{9,8},{10,9},{11,1... | collective-permute-start | bytes 98312 | tf_op jit(solution)/shard_map/ppermute | solution.py:539
  73.1 1.9 %collective-permute-start.11 = (f32[2,32,128]{2,1,0:T(8,128)S(1)}, f32[2,32,128]{2,1,0:T(8,128)S(1)}, u32[]{:S(2)}, u32[]{:S(2)}) collective-permute-start(f32[2,32,128]{2,1,0:T(8,128)S(1)} %get-tuple-element.41.b3), channel_id=1, source_target_pairs={{0,1},{1,2},{2,3},{3,4},{4,5},{5,6},{6,7},{7,8},{8,9},{9,10},{10,1... | collective-permute-start | bytes 98312 | tf_op jit(solution)/shard_map/ppermute | solution.py:539
  75.0 0.0 collective-permute-done.12.b3_right
  75.0 5.1 %collective-permute-done.11.b3_left = f32[2,32,128]{2,1,0:T(8,128)S(1)} collective-permute-done((f32[2,32,128]{2,1,0:T(8,128)S(1)}, f32[2,32,128]{2,1,0:T(8,128)S(1)}, u32[]{:S(2)}, u32[]{:S(2)}) %collective-permute-start.11) | collective-permute-done | bytes 32800 | tf_op jit(solution)/shard_map/ppermute | solution.py:539
  80.1 4.6 %shard_map.34 = f32[8,64,128]{2,1,0:T(8,128)} custom-call(f32[2,32,128]{2,1,0:T(8,128)S(1)} %get-tuple-element.41.b3, f32[2,32,128]{2,1,0:T(8,128)S(1)} %collective-permute-done.11.b3_left, f32[2,32,128]{2,1,0:T(8,128)S(1)} %collective-permute-done.12.b3_right, f32[4,64,128]{2,1,0:T(8,128)S(1)} %get-tuple-element.42.start2, ...), custom_call_target="tpu_custom_call" | custom-call | tf_op jit(solution)/shard_map/pallas_call | solution.py:598
  (2 shorter events, 0.0 us)
Async XLA Ops:
  0.0 0.9 %copy-start = (f32[8,64,128]{2,1,0:T(8,128)S(1)}, f32[8,64,128]{2,1,0:T(8,128)}, u32[]{:S(2)}) copy-start(f32[8,64,128]{2,1,0:T(8,128)} %start_hbm.1) | copy-start | bytes 786436
  1.0 0.9 %copy-start.1 = (f32[8,64,128]{2,1,0:T(8,128)S(1)}, f32[8,64,128]{2,1,0:T(8,128)}, u32[]{:S(2)}) copy-start(f32[8,64,128]{2,1,0:T(8,128)} %right_hbm.1) | copy-start | bytes 786436
  2.1 9.7 %collective-permute-start = (f32[6,64,128]{2,1,0:T(8,128)S(1)}, f32[6,64,128]{2,1,0:T(8,128)S(1)}, u32[]{:S(2)}, u32[]{:S(2)}) collective-permute-start(f32[6,64,128]{2,1,0:T(8,128)S(1)} %get-tuple-element.29), channel_id=1, source_target_pairs={{0,1},{1,2},{2,3},{3,4},{4,5},{5,6},{6,7},{7,8},{8,9},{9,10},{10,1... | collective-permute-start | bytes 589832 | tf_op jit(solution)/shard_map/ppermute | solution.py:539
  5.0 8.3 %collective-permute-start.1 = (f32[6,64,128]{2,1,0:T(8,128)S(1)}, f32[6,64,128]{2,1,0:T(8,128)S(1)}, u32[]{:S(2)}, u32[]{:S(2)}) collective-permute-start(f32[6,64,128]{2,1,0:T(8,128)S(1)} %get-tuple-element.30), channel_id=1, source_target_pairs={{1,0},{2,1},{3,2},{4,3},{5,4},{6,5},{7,6},{8,7},{9,8},{10,9},{11,1... | collective-permute-start | bytes 589832 | tf_op jit(solution)/shard_map/ppermute | solution.py:539
  9.2 12.0 %collective-permute-start.4 = (f32[12,64,128]{2,1,0:T(8,128)S(1)}, f32[12,64,128]{2,1,0:T(8,128)S(1)}, u32[]{:S(2)}, u32[]{:S(2)}) collective-permute-start(f32[12,64,128]{2,1,0:T(8,128)S(1)} %get-tuple-element.28.s), channel_id=1, source_target_pairs={{0,64},{64,128},{128,192},{192,256},{256,320},{320,384},{384,448},... | collective-permute-start | bytes 1179656 | tf_op jit(solution)/shard_map/ppermute | solution.py:545
  13.5 11.4 %collective-permute-start.2 = (f32[496,128]{1,0:T(8,128)S(1)}, f32[496,128]{1,0:T(8,128)S(1)}, u32[]{:S(2)}, u32[]{:S(2)}) collective-permute-start(f32[496,128]{1,0:T(8,128)S(1)} %get-tuple-element.32), channel_id=1, source_target_pairs={{0,16},{16,32},{32,48},{1,17},{17,33},{33,49},{2,18},{18,34},{34,5... | collective-permute-start | bytes 761864 | tf_op jit(solution)/shard_map/ppermute | solution.py:539
  16.9 8.3 %collective-permute-start.3 = (f32[496,128]{1,0:T(8,128)S(1)}, f32[496,128]{1,0:T(8,128)S(1)}, u32[]{:S(2)}, u32[]{:S(2)}) collective-permute-start(f32[496,128]{1,0:T(8,128)S(1)} %get-tuple-element.33), channel_id=1, source_target_pairs={{16,0},{32,16},{48,32},{17,1},{33,17},{49,33},{18,2},{34,18},{50,3... | collective-permute-start | bytes 761864 | tf_op jit(solution)/shard_map/ppermute | solution.py:539
  18.2 6.7 %collective-permute-start.6 = (f32[7,64,128]{2,1,0:T(8,128)S(1)}, f32[7,64,128]{2,1,0:T(8,128)S(1)}, u32[]{:S(2)}, u32[]{:S(2)}) collective-permute-start(f32[7,64,128]{2,1,0:T(8,128)S(1)} %get-tuple-element.34), channel_id=1, source_target_pairs={{0,64},{64,128},{128,192},{192,256},{256,320},{320,384},{384,448},... | collective-permute-start | bytes 688136 | tf_op jit(solution)/shard_map/ppermute | solution.py:545
  18.2 6.6 %collective-permute-start.7 = (f32[7,64,128]{2,1,0:T(8,128)S(1)}, f32[7,64,128]{2,1,0:T(8,128)S(1)}, u32[]{:S(2)}, u32[]{:S(2)}) collective-permute-start(f32[7,64,128]{2,1,0:T(8,128)S(1)} %get-tuple-element.35), channel_id=1, source_target_pairs={{64,0},{128,64},{192,128},{256,192},{320,256},{384,320},{448,384},... | collective-permute-start | bytes 688136 | tf_op jit(solution)/shard_map/ppermute | solution.py:545
  21.1 7.7 %collective-permute-start.5 = (f32[12,64,128]{2,1,0:T(8,128)S(1)}, f32[12,64,128]{2,1,0:T(8,128)S(1)}, u32[]{:S(2)}, u32[]{:S(2)}) collective-permute-start(f32[12,64,128]{2,1,0:T(8,128)S(1)} %get-tuple-element.28.s), channel_id=1, source_target_pairs={{64,0},{128,64},{192,128},{256,192},{320,256},{384,320},{448,384},... | collective-permute-start | bytes 1179656 | tf_op jit(solution)/shard_map/ppermute | solution.py:545
  25.4 8.2 %collective-permute-start.8 = (f32[736,128]{1,0:T(8,128)S(1)}, f32[736,128]{1,0:T(8,128)S(1)}, u32[]{:S(2)}, u32[]{:S(2)}) collective-permute-start(f32[736,128]{1,0:T(8,128)S(1)} %get-tuple-element.36), channel_id=1, source_target_pairs={{0,64},{64,128},{128,192},{192,256},{256,320},{320,384},{384,448},... | collective-permute-start | bytes 1130504 | tf_op jit(solution)/shard_map/ppermute | solution.py:545
  25.5 8.1 %collective-permute-start.9 = (f32[736,128]{1,0:T(8,128)S(1)}, f32[736,128]{1,0:T(8,128)S(1)}, u32[]{:S(2)}, u32[]{:S(2)}) collective-permute-start(f32[736,128]{1,0:T(8,128)S(1)} %get-tuple-element.37), channel_id=1, source_target_pairs={{64,0},{128,64},{192,128},{256,192},{320,256},{384,320},{448,384},... | collective-permute-start | bytes 1130504 | tf_op jit(solution)/shard_map/ppermute | solution.py:545
  50.5 3.6 %collective-permute-start.10 = (f32[4,1,200,128]{3,2,0,1:T(8,128)S(1)}, f32[4,1,200,128]{3,2,0,1:T(8,128)S(1)}, u32[]{:S(2)}, u32[]{:S(2)}) collective-permute-start(f32[4,1,200,128]{3,2,0,1:T(8,128)S(1)} %bitcast.3), channel_id=1, source_target_pairs={{0,64},{64,0},{128,192},{192,128},{256,320},{320,256},{384,448},{4... | collective-permute-start | bytes 1228808 | tf_op jit(solution)/shard_map/ppermute | solution.py:578
  67.7 7.3 %collective-permute-start.12 = (f32[2,32,128]{2,1,0:T(8,128)S(1)}, f32[2,32,128]{2,1,0:T(8,128)S(1)}, u32[]{:S(2)}, u32[]{:S(2)}) collective-permute-start(f32[2,32,128]{2,1,0:T(8,128)S(1)} %get-tuple-element.41.b3), channel_id=1, source_target_pairs={{1,0},{2,1},{3,2},{4,3},{5,4},{6,5},{7,6},{8,7},{9,8},{10,9},{11,1... | collective-permute-start | bytes 98312 | tf_op jit(solution)/shard_map/ppermute | solution.py:539
  73.1 7.0 %collective-permute-start.11 = (f32[2,32,128]{2,1,0:T(8,128)S(1)}, f32[2,32,128]{2,1,0:T(8,128)S(1)}, u32[]{:S(2)}, u32[]{:S(2)}) collective-permute-start(f32[2,32,128]{2,1,0:T(8,128)S(1)} %get-tuple-element.41.b3), channel_id=1, source_target_pairs={{0,1},{1,2},{2,3},{3,4},{4,5},{5,6},{6,7},{7,8},{8,9},{9,10},{10,1... | collective-permute-start | bytes 98312 | tf_op jit(solution)/shard_map/ppermute | solution.py:539

commit v8 on v7

--- a/solution.py
+++ b/solution.py
@@ -565,7 +565,7 @@
     v, v_up, v_down, first, last = call(widen_kernel, [(12, 64, 128), near, near, (CROSS_Y, 128), (CROSS_Y, 128)])(s, up, down)
     v_left, v_right = from_both_round(v_up, v_down, "gx")
     before, after = from_both(last, first, "gy")
-    up, down = call(strips_kernel, [(CROSS_X, 128)] * 2)(v, before, after, s_left, v_left, v_right)
+    up, down = call(strips_kernel, [(CROSS_X, 128)] * 2)(v, before, after, s_left, s_right, v_left, v_right)
     y_left, y_right = from_both_round(up, down, "gx")
     up0 = (8, 80, 256)
     b1, sent, black0, red_b0, black_b0 = call(

time: 85.1 us -> 86.5 us (1.016)
  starting transfers between devices: 27.2 us -> 29.5 us
    ppermute x3, starting transfers between devices: 5.93 us -> 8.35 us  [from_both_round(): lax.ppermute(down_value, axis, [(b, a) for a, b in up])]
    ppermute x3, waiting for transfers between devices: 7.73 us -> 6.76 us  [from_both(): lax.ppermute(up_value, axis, up)]
  transfers between devices with their start and end apart: 13 -> 13, of which waited for: 8 -> 7; matrix products, arithmetic and copies ran while one was open for 0% -> 0% of each run, Pallas kernels for 0% -> 0%
where the time goes in v8:
time: 86.5 us; the launch traced here: 86.2 us
  starting transfers between devices  29.5 us (34%)
  blocking collectives  23.7 us (27%)
  waiting for transfers between devices  19.2 us (22%)
  Pallas kernels  11.6 us (13%)
  local copies, waits for them, and re-layouts  1.95 us (2%)
    all_to_all x2, blocking collectives, gathered(): lax.all_to_all(copies, axis, split_axis=0, concat_axis=0, axis_index_grou...  23.7 us
    ppermute x3, starting transfers between devices, from_both(): lax.ppermute(down_value, axis, [(b, a) for a, b in up])  10.8 us
    ppermute x3, waiting for transfers between devices, from_both_round(): lax.ppermute(up_value, axis, up)  8.97 us
    ppermute x3, starting transfers between devices, from_both_round(): lax.ppermute(down_value, axis, [(b, a) for a, b in up])  8.35 us
    ppermute x3, starting transfers between devices, from_both(): lax.ppermute(up_value, axis, up)  8.25 us
    ppermute x3, waiting for transfers between devices, from_both(): lax.ppermute(up_value, axis, up)  6.76 us
    pallas_call x1, Pallas kernels, local(): call(functools.partial(up_kernel, n), [(8, 64, 128)], [colour2, colour2,...  4.61 us
    pallas_call x1, Pallas kernels, local(): call(functools.partial(fine_down_kernel, n), [(4, ROWS1, 128), (4 * SENT1...  4.21 us
  transfers between devices with their start and end apart: 13, of which 7 were waited for; matrix products, arithmetic and copies ran while one was open for 0% of the time, Pallas kernels for 0%

profile of v8, /device:TPU:256, one launch (start us, length us, event | category | flops | bytes accessed | tf_op | source)
XLA Modules:
  0.0 86.2 jit_solution(3497795016410614232)
XLA Ops:
  0.0 0.0 copy-start
  0.0 0.9 %copy-done = f32[8,64,128]{2,1,0:T(8,128)S(1)} copy-done((f32[8,64,128]{2,1,0:T(8,128)S(1)}, f32[8,64,128]{2,1,0:T(8,128)}, u32[]{:S(2)}) %copy-start) | copy-done | bytes 262168
  1.0 0.0 copy-start.1
  1.0 0.9 %copy-done.1 = f32[8,64,128]{2,1,0:T(8,128)S(1)} copy-done((f32[8,64,128]{2,1,0:T(8,128)S(1)}, f32[8,64,128]{2,1,0:T(8,128)}, u32[]{:S(2)}) %copy-start.1) | copy-done | bytes 262168
  1.9 0.2 shard_map.28
  2.1 2.5 %collective-permute-start.5 = (f32[12,64,128]{2,1,0:T(8,128)S(1)}, f32[12,64,128]{2,1,0:T(8,128)S(1)}, u32[]{:S(2)}, u32[]{:S(2)}) collective-permute-start(f32[12,64,128]{2,1,0:T(8,128)S(1)} %get-tuple-element.28.s), channel_id=1, source_target_pairs={{64,0},{128,64},{192,128},{256,192},{320,256},{384,320},{448,384},... | collective-permute-start | bytes 1179656 | tf_op jit(solution)/shard_map/ppermute | solution.py:545
  4.6 2.9 %collective-permute-start = (f32[6,64,128]{2,1,0:T(8,128)S(1)}, f32[6,64,128]{2,1,0:T(8,128)S(1)}, u32[]{:S(2)}, u32[]{:S(2)}) collective-permute-start(f32[6,64,128]{2,1,0:T(8,128)S(1)} %get-tuple-element.29), channel_id=1, source_target_pairs={{0,1},{1,2},{2,3},{3,4},{4,5},{5,6},{6,7},{7,8},{8,9},{9,10},{10,1... | collective-permute-start | bytes 589832 | tf_op jit(solution)/shard_map/ppermute | solution.py:539
  7.5 4.1 %collective-permute-start.1 = (f32[6,64,128]{2,1,0:T(8,128)S(1)}, f32[6,64,128]{2,1,0:T(8,128)S(1)}, u32[]{:S(2)}, u32[]{:S(2)}) collective-permute-start(f32[6,64,128]{2,1,0:T(8,128)S(1)} %get-tuple-element.30), channel_id=1, source_target_pairs={{1,0},{2,1},{3,2},{4,3},{5,4},{6,5},{7,6},{8,7},{9,8},{10,9},{11,1... | collective-permute-start | bytes 589832 | tf_op jit(solution)/shard_map/ppermute | solution.py:539
  11.6 0.0 collective-permute-start.4
  11.6 1.7 %collective-permute-done.up = f32[6,64,128]{2,1,0:T(8,128)S(1)} collective-permute-done((f32[6,64,128]{2,1,0:T(8,128)S(1)}, f32[6,64,128]{2,1,0:T(8,128)S(1)}, u32[]{:S(2)}, u32[]{:S(2)}) %collective-permute-start) | collective-permute-done | bytes 196640 | tf_op jit(solution)/shard_map/ppermute | solution.py:539
  13.3 1.7 %collective-permute-done.1.down = f32[6,64,128]{2,1,0:T(8,128)S(1)} collective-permute-done((f32[6,64,128]{2,1,0:T(8,128)S(1)}, f32[6,64,128]{2,1,0:T(8,128)S(1)}, u32[]{:S(2)}, u32[]{:S(2)}) %collective-permute-start.1) | collective-permute-done | bytes 196640 | tf_op jit(solution)/shard_map/ppermute | solution.py:539
  15.0 0.2 shard_map.29
  15.2 3.4 %collective-permute-start.2 = (f32[496,128]{1,0:T(8,128)S(1)}, f32[496,128]{1,0:T(8,128)S(1)}, u32[]{:S(2)}, u32[]{:S(2)}) collective-permute-start(f32[496,128]{1,0:T(8,128)S(1)} %get-tuple-element.32), channel_id=1, source_target_pairs={{0,16},{16,32},{32,48},{1,17},{17,33},{33,49},{2,18},{18,34},{34,5... | collective-permute-start | bytes 761864 | tf_op jit(solution)/shard_map/ppermute | solution.py:539
  18.6 1.3 %collective-permute-start.3 = (f32[496,128]{1,0:T(8,128)S(1)}, f32[496,128]{1,0:T(8,128)S(1)}, u32[]{:S(2)}, u32[]{:S(2)}) collective-permute-start(f32[496,128]{1,0:T(8,128)S(1)} %get-tuple-element.33), channel_id=1, source_target_pairs={{16,0},{32,16},{48,32},{17,1},{33,17},{49,33},{18,2},{34,18},{50,3... | collective-permute-start | bytes 761864 | tf_op jit(solution)/shard_map/ppermute | solution.py:539
  19.9 0.0 collective-permute-start.6
  20.0 0.0 collective-permute-done.5.rest_1_.s_right
  20.0 2.9 %collective-permute-start.7 = (f32[7,64,128]{2,1,0:T(8,128)S(1)}, f32[7,64,128]{2,1,0:T(8,128)S(1)}, u32[]{:S(2)}, u32[]{:S(2)}) collective-permute-start(f32[7,64,128]{2,1,0:T(8,128)S(1)} %get-tuple-element.35), channel_id=1, source_target_pairs={{64,0},{128,64},{192,128},{256,192},{320,256},{384,320},{448,384},... | collective-permute-start | bytes 688136 | tf_op jit(solution)/shard_map/ppermute | solution.py:545
  22.9 0.0 collective-permute-done.4.rest_0_.s_left
  22.9 3.7 %collective-permute-done.6.rest_2_.v_left = f32[7,64,128]{2,1,0:T(8,128)S(1)} collective-permute-done((f32[7,64,128]{2,1,0:T(8,128)S(1)}, f32[7,64,128]{2,1,0:T(8,128)S(1)}, u32[]{:S(2)}, u32[]{:S(2)}) %collective-permute-start.6) | collective-permute-done | bytes 229408 | tf_op jit(solution)/shard_map/ppermute | solution.py:545
  26.6 0.0 collective-permute-done.7.rest_3_.v_right
  26.6 0.0 collective-permute-done.2.before
  26.6 0.2 collective-permute-done.3.after
  26.8 0.2 shard_map.30
  27.0 0.0 collective-permute-start.8
  27.0 2.9 %collective-permute-start.9 = (f32[736,128]{1,0:T(8,128)S(1)}, f32[736,128]{1,0:T(8,128)S(1)}, u32[]{:S(2)}, u32[]{:S(2)}) collective-permute-start(f32[736,128]{1,0:T(8,128)S(1)} %get-tuple-element.37), channel_id=1, source_target_pairs={{64,0},{128,64},{192,128},{256,192},{320,256},{384,320},{448,384},... | collective-permute-start | bytes 1130504 | tf_op jit(solution)/shard_map/ppermute | solution.py:545
  30.0 5.3 %collective-permute-done.8.y_left = f32[736,128]{1,0:T(8,128)S(1)} collective-permute-done((f32[736,128]{1,0:T(8,128)S(1)}, f32[736,128]{1,0:T(8,128)S(1)}, u32[]{:S(2)}, u32[]{:S(2)}) %collective-permute-start.8) | collective-permute-done | bytes 376864 | tf_op jit(solution)/shard_map/ppermute | solution.py:545
  35.3 0.0 collective-permute-done.9.y_right
  35.3 4.2 %shard_map.31 = (f32[4,56,128]{2,1,0:T(8,128)S(1)}, f32[200,128]{1,0:T(8,128)S(1)}, f32[8,80,256]{2,1,0:T(8,128)S(1)}, f32[8,80,256]{2,1,0:T(8,128)S(1)}, f32[8,80,256]{2,1,0:T(8,128)S(1)}) custom-call(f32[12,64,128]{2,1,0:T(8,128)S(1)} %get-tuple-element.28.s, f32[12,64,128]{2,1,0:T(8,128)S(1)} %get-tuple-element.31.v, ...), custom_call_target="tpu_custom_call" | custom-call | tf_op jit(solution)/shard_map/pallas_call | solution.py:571
  39.5 12.1 %all_to_all.10 = f32[4,1,200,128]{3,2,1,0:T(8,128)S(1)} all-to-all(f32[4,1,200,128]{3,2,1,0:T(8,128)S(1)} %broadcast_in_dim.7), channel_id=1, replica_groups={{0,128,256,384},{64,192,320,448},{1,129,257,385},{65,193,321,449},{2,13..., dimensions={0} | all-to-all | bytes 819200 | tf_op jit(solution)/shard_map/all_to_all | solution.py:551
  51.7 2.1 %collective-permute-start.10 = (f32[4,1,200,128]{3,2,0,1:T(8,128)S(1)}, f32[4,1,200,128]{3,2,0,1:T(8,128)S(1)}, u32[]{:S(2)}, u32[]{:S(2)}) collective-permute-start(f32[4,1,200,128]{3,2,0,1:T(8,128)S(1)} %bitcast.3), channel_id=1, source_target_pairs={{0,64},{64,0},{128,192},{192,128},{256,320},{320,256},{384,448},{4... | collective-permute-start | bytes 1228808 | tf_op jit(solution)/shard_map/ppermute | solution.py:578
  53.7 1.6 %collective-permute-done.10 = f32[4,1,200,128]{3,2,0,1:T(8,128)S(1)} collective-permute-done((f32[4,1,200,128]{3,2,0,1:T(8,128)S(1)}, f32[4,1,200,128]{3,2,0,1:T(8,128)S(1)}, u32[]{:S(2)}, u32[]{:S(2)}) %collective-permute-start.10) | collective-permute-done | bytes 409632 | tf_op jit(solution)/shard_map/ppermute | solution.py:578
  55.3 1.5 %shard_map.32 = (f32[8,16,128]{2,1,0:T(8,128)S(1)}, f32[8,56,128]{2,1,0:T(8,128)S(1)}, f32[8,56,128]{2,1,0:T(8,128)S(1)}, f32[8,56,128]{2,1,0:T(8,128)S(1)}) custom-call(f32[4,56,128]{2,1,0:T(8,128)S(1)} %get-tuple-element.38.own, f32[4,200,128]{2,1,0:T(8,128)S(1)} %bitcast.4, f32[4,200,128]{2,1,0:T(8,128)S(1)} %bitcast.5), custom_call_target="tpu_custom_call" | custom-call | tf_op jit(solution)/shard_map/pallas_call | solution.py:583
  56.8 11.6 %all_to_all.11.b2 = f32[4,8,16,128]{3,2,1,0:T(8,128)S(1)} all-to-all(f32[4,8,16,128]{3,2,1,0:T(8,128)S(1)} %broadcast_in_dim.8), channel_id=1, replica_groups=mesh['gx'=8,'gy'=4,'gz'=16] {'gy'}, dimensions={0} | all-to-all | bytes 524288 | tf_op jit(solution)/shard_map/all_to_all | solution.py:551
  68.4 0.8 shard_map.33
  69.2 5.3 %collective-permute-start.12 = (f32[2,32,128]{2,1,0:T(8,128)S(1)}, f32[2,32,128]{2,1,0:T(8,128)S(1)}, u32[]{:S(2)}, u32[]{:S(2)}) collective-permute-start(f32[2,32,128]{2,1,0:T(8,128)S(1)} %get-tuple-element.41.b3), channel_id=1, source_target_pairs={{1,0},{2,1},{3,2},{4,3},{5,4},{6,5},{7,6},{8,7},{9,8},{10,9},{11,1... | collective-permute-start | bytes 98312 | tf_op jit(solution)/shard_map/ppermute | solution.py:539
  74.5 1.9 %collective-permute-start.11 = (f32[2,32,128]{2,1,0:T(8,128)S(1)}, f32[2,32,128]{2,1,0:T(8,128)S(1)}, u32[]{:S(2)}, u32[]{:S(2)}) collective-permute-start(f32[2,32,128]{2,1,0:T(8,128)S(1)} %get-tuple-element.41.b3), channel_id=1, source_target_pairs={{0,1},{1,2},{2,3},{3,4},{4,5},{5,6},{6,7},{7,8},{8,9},{9,10},{10,1... | collective-permute-start | bytes 98312 | tf_op jit(solution)/shard_map/ppermute | solution.py:539
  76.5 0.0 collective-permute-done.12.b3_right
  76.5 5.1 %collective-permute-done.11.b3_left = f32[2,32,128]{2,1,0:T(8,128)S(1)} collective-permute-done((f32[2,32,128]{2,1,0:T(8,128)S(1)}, f32[2,32,128]{2,1,0:T(8,128)S(1)}, u32[]{:S(2)}, u32[]{:S(2)}) %collective-permute-start.11) | collective-permute-done | bytes 32800 | tf_op jit(solution)/shard_map/ppermute | solution.py:539
  81.5 4.6 %shard_map.34 = f32[8,64,128]{2,1,0:T(8,128)} custom-call(f32[2,32,128]{2,1,0:T(8,128)S(1)} %get-tuple-element.41.b3, f32[2,32,128]{2,1,0:T(8,128)S(1)} %collective-permute-done.11.b3_left, f32[2,32,128]{2,1,0:T(8,128)S(1)} %collective-permute-done.12.b3_right, f32[4,64,128]{2,1,0:T(8,128)S(1)} %get-tuple-element.42.start2, ...), custom_call_target="tpu_custom_call" | custom-call | tf_op jit(solution)/shard_map/pallas_call | solution.py:598
  (2 shorter events, 0.0 us)
Async XLA Ops:
  0.0 0.9 %copy-start = (f32[8,64,128]{2,1,0:T(8,128)S(1)}, f32[8,64,128]{2,1,0:T(8,128)}, u32[]{:S(2)}) copy-start(f32[8,64,128]{2,1,0:T(8,128)} %start_hbm.1) | copy-start | bytes 786436
  1.0 0.9 %copy-start.1 = (f32[8,64,128]{2,1,0:T(8,128)S(1)}, f32[8,64,128]{2,1,0:T(8,128)}, u32[]{:S(2)}) copy-start(f32[8,64,128]{2,1,0:T(8,128)} %right_hbm.1) | copy-start | bytes 786436
  2.1 17.9 %collective-permute-start.5 = (f32[12,64,128]{2,1,0:T(8,128)S(1)}, f32[12,64,128]{2,1,0:T(8,128)S(1)}, u32[]{:S(2)}, u32[]{:S(2)}) collective-permute-start(f32[12,64,128]{2,1,0:T(8,128)S(1)} %get-tuple-element.28.s), channel_id=1, source_target_pairs={{64,0},{128,64},{192,128},{256,192},{320,256},{384,320},{448,384},... | collective-permute-start | bytes 1179656 | tf_op jit(solution)/shard_map/ppermute | solution.py:545
  4.6 8.8 %collective-permute-start = (f32[6,64,128]{2,1,0:T(8,128)S(1)}, f32[6,64,128]{2,1,0:T(8,128)S(1)}, u32[]{:S(2)}, u32[]{:S(2)}) collective-permute-start(f32[6,64,128]{2,1,0:T(8,128)S(1)} %get-tuple-element.29), channel_id=1, source_target_pairs={{0,1},{1,2},{2,3},{3,4},{4,5},{5,6},{6,7},{7,8},{8,9},{9,10},{10,1... | collective-permute-start | bytes 589832 | tf_op jit(solution)/shard_map/ppermute | solution.py:539
  7.5 7.6 %collective-permute-start.1 = (f32[6,64,128]{2,1,0:T(8,128)S(1)}, f32[6,64,128]{2,1,0:T(8,128)S(1)}, u32[]{:S(2)}, u32[]{:S(2)}) collective-permute-start(f32[6,64,128]{2,1,0:T(8,128)S(1)} %get-tuple-element.30), channel_id=1, source_target_pairs={{1,0},{2,1},{3,2},{4,3},{5,4},{6,5},{7,6},{8,7},{9,8},{10,9},{11,1... | collective-permute-start | bytes 589832 | tf_op jit(solution)/shard_map/ppermute | solution.py:539
  11.6 11.3 %collective-permute-start.4 = (f32[12,64,128]{2,1,0:T(8,128)S(1)}, f32[12,64,128]{2,1,0:T(8,128)S(1)}, u32[]{:S(2)}, u32[]{:S(2)}) collective-permute-start(f32[12,64,128]{2,1,0:T(8,128)S(1)} %get-tuple-element.28.s), channel_id=1, source_target_pairs={{0,64},{64,128},{128,192},{192,256},{256,320},{320,384},{384,448},... | collective-permute-start | bytes 1179656 | tf_op jit(solution)/shard_map/ppermute | solution.py:545
  15.2 11.4 %collective-permute-start.2 = (f32[496,128]{1,0:T(8,128)S(1)}, f32[496,128]{1,0:T(8,128)S(1)}, u32[]{:S(2)}, u32[]{:S(2)}) collective-permute-start(f32[496,128]{1,0:T(8,128)S(1)} %get-tuple-element.32), channel_id=1, source_target_pairs={{0,16},{16,32},{32,48},{1,17},{17,33},{33,49},{2,18},{18,34},{34,5... | collective-permute-start | bytes 761864 | tf_op jit(solution)/shard_map/ppermute | solution.py:539
  18.6 8.2 %collective-permute-start.3 = (f32[496,128]{1,0:T(8,128)S(1)}, f32[496,128]{1,0:T(8,128)S(1)}, u32[]{:S(2)}, u32[]{:S(2)}) collective-permute-start(f32[496,128]{1,0:T(8,128)S(1)} %get-tuple-element.33), channel_id=1, source_target_pairs={{16,0},{32,16},{48,32},{17,1},{33,17},{49,33},{18,2},{34,18},{50,3... | collective-permute-start | bytes 761864 | tf_op jit(solution)/shard_map/ppermute | solution.py:539
  19.9 6.7 %collective-permute-start.6 = (f32[7,64,128]{2,1,0:T(8,128)S(1)}, f32[7,64,128]{2,1,0:T(8,128)S(1)}, u32[]{:S(2)}, u32[]{:S(2)}) collective-permute-start(f32[7,64,128]{2,1,0:T(8,128)S(1)} %get-tuple-element.34), channel_id=1, source_target_pairs={{0,64},{64,128},{128,192},{192,256},{256,320},{320,384},{384,448},... | collective-permute-start | bytes 688136 | tf_op jit(solution)/shard_map/ppermute | solution.py:545
  20.0 6.6 %collective-permute-start.7 = (f32[7,64,128]{2,1,0:T(8,128)S(1)}, f32[7,64,128]{2,1,0:T(8,128)S(1)}, u32[]{:S(2)}, u32[]{:S(2)}) collective-permute-start(f32[7,64,128]{2,1,0:T(8,128)S(1)} %get-tuple-element.35), channel_id=1, source_target_pairs={{64,0},{128,64},{192,128},{256,192},{320,256},{384,320},{448,384},... | collective-permute-start | bytes 688136 | tf_op jit(solution)/shard_map/ppermute | solution.py:545
  27.0 8.2 %collective-permute-start.8 = (f32[736,128]{1,0:T(8,128)S(1)}, f32[736,128]{1,0:T(8,128)S(1)}, u32[]{:S(2)}, u32[]{:S(2)}) collective-permute-start(f32[736,128]{1,0:T(8,128)S(1)} %get-tuple-element.36), channel_id=1, source_target_pairs={{0,64},{64,128},{128,192},{192,256},{256,320},{320,384},{384,448},... | collective-permute-start | bytes 1130504 | tf_op jit(solution)/shard_map/ppermute | solution.py:545
  27.0 8.2 %collective-permute-start.9 = (f32[736,128]{1,0:T(8,128)S(1)}, f32[736,128]{1,0:T(8,128)S(1)}, u32[]{:S(2)}, u32[]{:S(2)}) collective-permute-start(f32[736,128]{1,0:T(8,128)S(1)} %get-tuple-element.37), channel_id=1, source_target_pairs={{64,0},{128,64},{192,128},{256,192},{320,256},{384,320},{448,384},... | collective-permute-start | bytes 1130504 | tf_op jit(solution)/shard_map/ppermute | solution.py:545
  51.7 3.6 %collective-permute-start.10 = (f32[4,1,200,128]{3,2,0,1:T(8,128)S(1)}, f32[4,1,200,128]{3,2,0,1:T(8,128)S(1)}, u32[]{:S(2)}, u32[]{:S(2)}) collective-permute-start(f32[4,1,200,128]{3,2,0,1:T(8,128)S(1)} %bitcast.3), channel_id=1, source_target_pairs={{0,64},{64,0},{128,192},{192,128},{256,320},{320,256},{384,448},{4... | collective-permute-start | bytes 1228808 | tf_op jit(solution)/shard_map/ppermute | solution.py:578
  69.2 7.3 %collective-permute-start.12 = (f32[2,32,128]{2,1,0:T(8,128)S(1)}, f32[2,32,128]{2,1,0:T(8,128)S(1)}, u32[]{:S(2)}, u32[]{:S(2)}) collective-permute-start(f32[2,32,128]{2,1,0:T(8,128)S(1)} %get-tuple-element.41.b3), channel_id=1, source_target_pairs={{1,0},{2,1},{3,2},{4,3},{5,4},{6,5},{7,6},{8,7},{9,8},{10,9},{11,1... | collective-permute-start | bytes 98312 | tf_op jit(solution)/shard_map/ppermute | solution.py:539
  74.5 7.0 %collective-permute-start.11 = (f32[2,32,128]{2,1,0:T(8,128)S(1)}, f32[2,32,128]{2,1,0:T(8,128)S(1)}, u32[]{:S(2)}, u32[]{:S(2)}) collective-permute-start(f32[2,32,128]{2,1,0:T(8,128)S(1)} %get-tuple-element.41.b3), channel_id=1, source_target_pairs={{0,1},{1,2},{2,3},{3,4},{4,5},{5,6},{6,7},{7,8},{8,9},{9,10},{10,1... | collective-permute-start | bytes 98312 | tf_op jit(solution)/shard_map/ppermute | solution.py:539
